TPU v7x, 128 devices: a whole 4x4x4 slice. The times are simulated.
128 devices in a mesh: grp: 8 (over y, core), sub: 16 (over x, z).
Axes of the slice: x: 4, y: 4, z: 4, core: 2. Of those that a mesh axis runs over, the one named last changes fastest.
Arguments:
- embeddings: bfloat16 [49152, 1024], P(('grp', 'sub')), may hold values from -6 to 6
- cluster_ids: int32 [49152], P(('grp', 'sub')), may hold values from 0 to 23, as said below
Outputs:
- best_similarity: float32 [49152], P(('grp', 'sub'))
Inputs may be any that keep to these rules, and one draw needn't show every extreme that they name: `cluster_ids`: cluster c belongs to group c // 3. Of the 384 embeddings of each device, exactly 96 lie in the clusters of one group, and the others are spread as evenly as possible over the other groups; which group is the one with 96 depends only on the device's index along sub.
All inputs are finite; a program needn't handle non-finite values.
Results may differ from a plain program's by a relative error of at most 0.0003.
Values may be sent and summed in bfloat16 or wider, within the bound.
No kernel may reach another device: no remote copies, remote signals or barrier semaphores. Data moves between devices by JAX's collectives and lax.ppermute only.
A program may use at most 128 MiB of HBM per device.

v0:
```python
import math

import jax
import jax.numpy as jnp
from jax import lax
from jax.sharding import PartitionSpec as P

KG = 3
CAP = 96


EPSILON = 1e-06


def inverse_norms(block):
    values = block.astype(jnp.float32)
    return lax.rsqrt(jnp.sum(values * values, axis=1) + EPSILON)


def tile_max(
    left_rows, left_ids, left_inverse, right_rows, right_ids, right_inverse, left_first, right_first
):
    scores = lax.dot_general(
        left_rows, right_rows, (((1,), (1,)), ((), ())), preferred_element_type=jnp.float32
    )
    scaled = scores * left_inverse[:, None] * right_inverse[None, :]
    left_index = left_first + jnp.arange(left_rows.shape[0], dtype=jnp.int32)
    right_index = right_first + jnp.arange(right_rows.shape[0], dtype=jnp.int32)
    same_cluster = (
        (left_ids[:, None] == right_ids[None, :])
        & (left_ids[:, None] >= 0)
        & (left_index[:, None] != right_index[None, :])
    )
    masked = jnp.where(same_cluster, scaled, jnp.float32(-1.0))
    return (jnp.max(masked, axis=1), jnp.max(masked, axis=0))


def local(embeddings, cluster_ids):
    groups_count = lax.axis_size("grp")
    feature_count = embeddings.shape[1]
    destination = cluster_ids // KG
    onehot = (destination[:, None] == jnp.arange(groups_count, dtype=jnp.int32)[None, :]).astype(
        jnp.int32
    )
    earlier = jnp.cumsum(onehot, axis=0) - onehot
    slot_index = jnp.sum(earlier * onehot, axis=1)
    position = destination * CAP + slot_index
    send_rows = (
        jnp.zeros((groups_count * CAP, feature_count), jnp.bfloat16).at[position].set(embeddings)
    )
    send_ids = (
        jnp.full((groups_count * CAP,), -1.0, jnp.bfloat16)
        .at[position]
        .set(cluster_ids.astype(jnp.bfloat16))
    )
    own_rows, own_ids = (
        lax.all_to_all(send_rows, "grp", split_axis=0, concat_axis=0, tiled=True),
        lax.all_to_all(send_ids, "grp", split_axis=0, concat_axis=0, tiled=True),
    )
    own_count = own_rows.shape[0]
    own_inverse = inverse_norms(own_rows)
    own_first = lax.axis_index("sub") * own_count
    piece_rows = lax.all_gather(own_rows, "sub", axis=0, tiled=True)
    piece_ids = lax.all_gather(own_ids, "sub", axis=0, tiled=True)
    piece_count = piece_rows.shape[0]
    block_rows = math.gcd(piece_count, own_count)
    block_count = piece_count // block_rows

    def one_block(index, current):
        right_rows = lax.dynamic_slice_in_dim(piece_rows, index * block_rows, block_rows, 0)
        right_ids = lax.dynamic_slice_in_dim(piece_ids, index * block_rows, block_rows, 0)
        row_max, column_max = tile_max(
            own_rows,
            own_ids,
            own_inverse,
            right_rows,
            right_ids,
            inverse_norms(right_rows),
            own_first,
            index * block_rows,
        )
        return jnp.maximum(current, row_max)

    best_seen = lax.fori_loop(0, block_count, one_block, jnp.full((own_count,), -1.0, jnp.float32))
    gathered_back = lax.all_to_all(best_seen, "grp", split_axis=0, concat_axis=0, tiled=True)
    return jnp.take(gathered_back, position, axis=0)


def solution(mesh):
    return jax.shard_map(
        local,
        mesh=mesh,
        in_specs=(P(("grp", "sub"), None), P(("grp", "sub"))),
        out_specs=P(("grp", "sub")),
        check_vma=False,
    )
```

profile of v0, /device:TPU:0, one launch (start us, length us, event | category | flops | bytes accessed | tf_op | source)
XLA Modules:
  0.0 295.1 jit_solution(15077629996468475146)
XLA Ops:
  6.5 0.8 fusion.11
  7.3 0.9 reduce-window.6
  8.2 0.2 slice_reduce_fusion
  8.4 0.1 fusion.6
  8.5 3.2 %scatter_custom_fusion.1 = bf16[768,1024]{1,0:T(8,128)(2,1)S(1)} fusion(s32[384]{0:T(512)S(1)} %compare_select_fusion, bf16[384,1024]{1,0:T(8,128)(2,1)} %param.4, bf16[]{:T(256)} %constant.102.clone.1), kind=kCustom, calls=%fused_computation.14 | custom fusion | bytes 1573376 | tf_op jit(solution)/shard_map/scatter | solution.py:49
  11.7 26.3 %all_to_all.37 = bf16[8,96,1024]{2,1,0:T(8,128)(2,1)} all-to-all(bf16[8,96,1024]{2,1,0:T(8,128)(2,1)S(1)} %bitcast.25), channel_id=1, replica_groups=mesh['grp'=8,'sub'=16] {'grp'}, dimensions={0} | all-to-all | bytes 3145728 | tf_op jit(solution)/shard_map/all_to_all | solution.py:57
  38.0 3.0 scatter_custom_fusion
  41.0 0.7 all_to_all.33
  41.6 3.3 %all-to-all-start = ((bf16[8,96,1]{1,2,0:T(2,128)(2,1)}), bf16[8,96,1]{1,2,0:T(2,128)(2,1)S(1)}, u32[]{:S(2)}, u32[]{:S(2)}) async-start(bf16[8,96,1]{1,2,0:T(2,128)(2,1)} %all_to_all.33), calls=%async_computation | async-start | bytes 8192 | tf_op jit(solution)/shard_map/all_to_all | solution.py:58
  44.9 5.2 %all-to-all-done = bf16[8,96,1]{1,2,0:T(2,128)(2,1)S(1)} async-done(((bf16[8,96,1]{1,2,0:T(2,128)(2,1)}), bf16[8,96,1]{1,2,0:T(2,128)(2,1)S(1)}, u32[]{:S(2)}, u32[]{:S(2)}) %all-to-all-start) | async-done | bytes 1568 | tf_op jit(solution)/shard_map/all_to_all | solution.py:58
  50.1 0.1 all_to_all.26
  50.3 25.0 %all-gather = bf16[16,1,768]{2,1,0:T(2,128)(2,1)S(1)} all-gather(bf16[1,1,768]{2,1,0:T(2,128)(2,1)S(1)} %reshape.82), channel_id=1, replica_groups=mesh['grp'=8,'sub'=16] {'sub'}, dimensions={0}, use_global_device_ids=true | all-gather | bytes 26112 | tf_op jit(solution)/shard_map/all_gather | solution.py:64
  75.3 0.1 reduce.4
  75.5 0.4 multiply_reduce_fusion.1
  76.0 117.1 %all-gather.3.cloned.1.call-done = bf16[12288,1024]{1,0:T(8,128)(2,1)} async-done(((bf16[768,1024]{1,0:T(8,128)(2,1)}), bf16[12288,1024]{1,0:T(8,128)(2,1)}) %all-gather.3.cloned.1.call-update) | async-done | bytes 25165840 | tf_op jit(solution)/shard_map/all_gather | solution.py:63
  193.1 81.2 %while.14 = (s32[]{:T(128)}, f32[768]{0:T(1024)S(1)}, bf16[768]{0:T(1024)(128)(2,1)S(1)}, bf16[12288]{0:T(1024)(128)(2,1)S(1)}, s32[]{:T(128)}, /*index=5*/bf16[...) while((s32[]{:T(128)}, f32[768]{0:T(1024)S(1)}, ...), condition=%wide.region_9.10_spmd.clone, body=%wide.region_6.9_spmd.clone.sunk | while | flops 1216220160 | bytes 4767945 | solution.py:84
  193.1 1.8 multiply_reduce_fusion.3
  194.9 0.1 dynamic_slice.24
  195.0 3.1 %fusion.18 = f32[768]{0:T(1024)S(1)} fusion(bf16[768,1024]{1,0:T(8,128)(2,1)S(1)} %get-tuple-element.275, bf16[12288,1024]{1,0:T(8,128)(2,1)} %get-tuple-element.274, s32[]{:T(128)S(6)} %select_n.45, f32[768]{0:T(1024)S(1)} %add_rsqrt_fusion.3, f32[768]{0:T(1024)S(1)} %get-tuple-element.276, s32[768]{0:T(1024)S(1)} %get-tuple-element.243, ...), kind=kOutput, calls=%fused_computation.5.clone.1 | convolution fusion | flops 1213857024 | bytes 3164932 | tf_op jit(solution)/shard_map/while/body/eval_jaxpr/dot_general | solution.py:23
  198.2 1.8 multiply_reduce_fusion.3
  200.0 0.1 dynamic_slice.24
  200.1 3.1 %fusion.18 = f32[768]{0:T(1024)S(1)} fusion(bf16[768,1024]{1,0:T(8,128)(2,1)S(1)} %get-tuple-element.275, bf16[12288,1024]{1,0:T(8,128)(2,1)} %get-tuple-element.274, s32[]{:T(128)S(6)} %select_n.45, f32[768]{0:T(1024)S(1)} %add_rsqrt_fusion.3, f32[768]{0:T(1024)S(1)} %get-tuple-element.276, s32[768]{0:T(1024)S(1)} %get-tuple-element.243, ...), kind=kOutput, calls=%fused_computation.5.clone.1 | convolution fusion | flops 1213857024 | bytes 3164932 | tf_op jit(solution)/shard_map/while/body/eval_jaxpr/dot_general | solution.py:23
  203.2 1.8 multiply_reduce_fusion.3
  205.1 0.1 dynamic_slice.24
  205.2 3.1 %fusion.18 = f32[768]{0:T(1024)S(1)} fusion(bf16[768,1024]{1,0:T(8,128)(2,1)S(1)} %get-tuple-element.275, bf16[12288,1024]{1,0:T(8,128)(2,1)} %get-tuple-element.274, s32[]{:T(128)S(6)} %select_n.45, f32[768]{0:T(1024)S(1)} %add_rsqrt_fusion.3, f32[768]{0:T(1024)S(1)} %get-tuple-element.276, s32[768]{0:T(1024)S(1)} %get-tuple-element.243, ...), kind=kOutput, calls=%fused_computation.5.clone.1 | convolution fusion | flops 1213857024 | bytes 3164932 | tf_op jit(solution)/shard_map/while/body/eval_jaxpr/dot_general | solution.py:23
  208.3 1.8 multiply_reduce_fusion.3
  210.1 0.1 dynamic_slice.24
  210.2 3.1 %fusion.18 = f32[768]{0:T(1024)S(1)} fusion(bf16[768,1024]{1,0:T(8,128)(2,1)S(1)} %get-tuple-element.275, bf16[12288,1024]{1,0:T(8,128)(2,1)} %get-tuple-element.274, s32[]{:T(128)S(6)} %select_n.45, f32[768]{0:T(1024)S(1)} %add_rsqrt_fusion.3, f32[768]{0:T(1024)S(1)} %get-tuple-element.276, s32[768]{0:T(1024)S(1)} %get-tuple-element.243, ...), kind=kOutput, calls=%fused_computation.5.clone.1 | convolution fusion | flops 1213857024 | bytes 3164932 | tf_op jit(solution)/shard_map/while/body/eval_jaxpr/dot_general | solution.py:23
  213.4 1.8 multiply_reduce_fusion.3
  215.3 3.1 %fusion.18 = f32[768]{0:T(1024)S(1)} fusion(bf16[768,1024]{1,0:T(8,128)(2,1)S(1)} %get-tuple-element.275, bf16[12288,1024]{1,0:T(8,128)(2,1)} %get-tuple-element.274, s32[]{:T(128)S(6)} %select_n.45, f32[768]{0:T(1024)S(1)} %add_rsqrt_fusion.3, f32[768]{0:T(1024)S(1)} %get-tuple-element.276, s32[768]{0:T(1024)S(1)} %get-tuple-element.243, ...), kind=kOutput, calls=%fused_computation.5.clone.1 | convolution fusion | flops 1213857024 | bytes 3164932 | tf_op jit(solution)/shard_map/while/body/eval_jaxpr/dot_general | solution.py:23
  218.5 1.8 multiply_reduce_fusion.3
  220.3 0.1 dynamic_slice.24
  220.4 3.1 %fusion.18 = f32[768]{0:T(1024)S(1)} fusion(bf16[768,1024]{1,0:T(8,128)(2,1)S(1)} %get-tuple-element.275, bf16[12288,1024]{1,0:T(8,128)(2,1)} %get-tuple-element.274, s32[]{:T(128)S(6)} %select_n.45, f32[768]{0:T(1024)S(1)} %add_rsqrt_fusion.3, f32[768]{0:T(1024)S(1)} %get-tuple-element.276, s32[768]{0:T(1024)S(1)} %get-tuple-element.243, ...), kind=kOutput, calls=%fused_computation.5.clone.1 | convolution fusion | flops 1213857024 | bytes 3164932 | tf_op jit(solution)/shard_map/while/body/eval_jaxpr/dot_general | solution.py:23
  223.6 1.8 multiply_reduce_fusion.3
  225.4 0.1 dynamic_slice.24
  225.5 3.1 %fusion.18 = f32[768]{0:T(1024)S(1)} fusion(bf16[768,1024]{1,0:T(8,128)(2,1)S(1)} %get-tuple-element.275, bf16[12288,1024]{1,0:T(8,128)(2,1)} %get-tuple-element.274, s32[]{:T(128)S(6)} %select_n.45, f32[768]{0:T(1024)S(1)} %add_rsqrt_fusion.3, f32[768]{0:T(1024)S(1)} %get-tuple-element.276, s32[768]{0:T(1024)S(1)} %get-tuple-element.243, ...), kind=kOutput, calls=%fused_computation.5.clone.1 | convolution fusion | flops 1213857024 | bytes 3164932 | tf_op jit(solution)/shard_map/while/body/eval_jaxpr/dot_general | solution.py:23
  228.6 1.8 multiply_reduce_fusion.3
  230.5 0.1 dynamic_slice.24
  230.5 3.1 %fusion.18 = f32[768]{0:T(1024)S(1)} fusion(bf16[768,1024]{1,0:T(8,128)(2,1)S(1)} %get-tuple-element.275, bf16[12288,1024]{1,0:T(8,128)(2,1)} %get-tuple-element.274, s32[]{:T(128)S(6)} %select_n.45, f32[768]{0:T(1024)S(1)} %add_rsqrt_fusion.3, f32[768]{0:T(1024)S(1)} %get-tuple-element.276, s32[768]{0:T(1024)S(1)} %get-tuple-element.243, ...), kind=kOutput, calls=%fused_computation.5.clone.1 | convolution fusion | flops 1213857024 | bytes 3164932 | tf_op jit(solution)/shard_map/while/body/eval_jaxpr/dot_general | solution.py:23
  233.7 1.8 multiply_reduce_fusion.3
  235.6 3.1 %fusion.18 = f32[768]{0:T(1024)S(1)} fusion(bf16[768,1024]{1,0:T(8,128)(2,1)S(1)} %get-tuple-element.275, bf16[12288,1024]{1,0:T(8,128)(2,1)} %get-tuple-element.274, s32[]{:T(128)S(6)} %select_n.45, f32[768]{0:T(1024)S(1)} %add_rsqrt_fusion.3, f32[768]{0:T(1024)S(1)} %get-tuple-element.276, s32[768]{0:T(1024)S(1)} %get-tuple-element.243, ...), kind=kOutput, calls=%fused_computation.5.clone.1 | convolution fusion | flops 1213857024 | bytes 3164932 | tf_op jit(solution)/shard_map/while/body/eval_jaxpr/dot_general | solution.py:23
  238.8 1.8 multiply_reduce_fusion.3
  240.6 0.1 dynamic_slice.24
  240.7 3.1 %fusion.18 = f32[768]{0:T(1024)S(1)} fusion(bf16[768,1024]{1,0:T(8,128)(2,1)S(1)} %get-tuple-element.275, bf16[12288,1024]{1,0:T(8,128)(2,1)} %get-tuple-element.274, s32[]{:T(128)S(6)} %select_n.45, f32[768]{0:T(1024)S(1)} %add_rsqrt_fusion.3, f32[768]{0:T(1024)S(1)} %get-tuple-element.276, s32[768]{0:T(1024)S(1)} %get-tuple-element.243, ...), kind=kOutput, calls=%fused_computation.5.clone.1 | convolution fusion | flops 1213857024 | bytes 3164932 | tf_op jit(solution)/shard_map/while/body/eval_jaxpr/dot_general | solution.py:23
  243.9 1.8 multiply_reduce_fusion.3
  245.7 0.1 dynamic_slice.24
  245.8 3.1 %fusion.18 = f32[768]{0:T(1024)S(1)} fusion(bf16[768,1024]{1,0:T(8,128)(2,1)S(1)} %get-tuple-element.275, bf16[12288,1024]{1,0:T(8,128)(2,1)} %get-tuple-element.274, s32[]{:T(128)S(6)} %select_n.45, f32[768]{0:T(1024)S(1)} %add_rsqrt_fusion.3, f32[768]{0:T(1024)S(1)} %get-tuple-element.276, s32[768]{0:T(1024)S(1)} %get-tuple-element.243, ...), kind=kOutput, calls=%fused_computation.5.clone.1 | convolution fusion | flops 1213857024 | bytes 3164932 | tf_op jit(solution)/shard_map/while/body/eval_jaxpr/dot_general | solution.py:23
  248.9 1.8 multiply_reduce_fusion.3
  250.9 3.1 %fusion.18 = f32[768]{0:T(1024)S(1)} fusion(bf16[768,1024]{1,0:T(8,128)(2,1)S(1)} %get-tuple-element.275, bf16[12288,1024]{1,0:T(8,128)(2,1)} %get-tuple-element.274, s32[]{:T(128)S(6)} %select_n.45, f32[768]{0:T(1024)S(1)} %add_rsqrt_fusion.3, f32[768]{0:T(1024)S(1)} %get-tuple-element.276, s32[768]{0:T(1024)S(1)} %get-tuple-element.243, ...), kind=kOutput, calls=%fused_computation.5.clone.1 | convolution fusion | flops 1213857024 | bytes 3164932 | tf_op jit(solution)/shard_map/while/body/eval_jaxpr/dot_general | solution.py:23
  254.0 1.8 multiply_reduce_fusion.3
  255.9 3.1 %fusion.18 = f32[768]{0:T(1024)S(1)} fusion(bf16[768,1024]{1,0:T(8,128)(2,1)S(1)} %get-tuple-element.275, bf16[12288,1024]{1,0:T(8,128)(2,1)} %get-tuple-element.274, s32[]{:T(128)S(6)} %select_n.45, f32[768]{0:T(1024)S(1)} %add_rsqrt_fusion.3, f32[768]{0:T(1024)S(1)} %get-tuple-element.276, s32[768]{0:T(1024)S(1)} %get-tuple-element.243, ...), kind=kOutput, calls=%fused_computation.5.clone.1 | convolution fusion | flops 1213857024 | bytes 3164932 | tf_op jit(solution)/shard_map/while/body/eval_jaxpr/dot_general | solution.py:23
  259.1 1.8 multiply_reduce_fusion.3
  261.0 3.1 %fusion.18 = f32[768]{0:T(1024)S(1)} fusion(bf16[768,1024]{1,0:T(8,128)(2,1)S(1)} %get-tuple-element.275, bf16[12288,1024]{1,0:T(8,128)(2,1)} %get-tuple-element.274, s32[]{:T(128)S(6)} %select_n.45, f32[768]{0:T(1024)S(1)} %add_rsqrt_fusion.3, f32[768]{0:T(1024)S(1)} %get-tuple-element.276, s32[768]{0:T(1024)S(1)} %get-tuple-element.243, ...), kind=kOutput, calls=%fused_computation.5.clone.1 | convolution fusion | flops 1213857024 | bytes 3164932 | tf_op jit(solution)/shard_map/while/body/eval_jaxpr/dot_general | solution.py:23
  264.2 1.8 multiply_reduce_fusion.3
  266.1 3.1 %fusion.18 = f32[768]{0:T(1024)S(1)} fusion(bf16[768,1024]{1,0:T(8,128)(2,1)S(1)} %get-tuple-element.275, bf16[12288,1024]{1,0:T(8,128)(2,1)} %get-tuple-element.274, s32[]{:T(128)S(6)} %select_n.45, f32[768]{0:T(1024)S(1)} %add_rsqrt_fusion.3, f32[768]{0:T(1024)S(1)} %get-tuple-element.276, s32[768]{0:T(1024)S(1)} %get-tuple-element.243, ...), kind=kOutput, calls=%fused_computation.5.clone.1 | convolution fusion | flops 1213857024 | bytes 3164932 | tf_op jit(solution)/shard_map/while/body/eval_jaxpr/dot_general | solution.py:23
  269.3 1.8 multiply_reduce_fusion.3
  271.2 3.1 %fusion.18 = f32[768]{0:T(1024)S(1)} fusion(bf16[768,1024]{1,0:T(8,128)(2,1)S(1)} %get-tuple-element.275, bf16[12288,1024]{1,0:T(8,128)(2,1)} %get-tuple-element.274, s32[]{:T(128)S(6)} %select_n.45, f32[768]{0:T(1024)S(1)} %add_rsqrt_fusion.3, f32[768]{0:T(1024)S(1)} %get-tuple-element.276, s32[768]{0:T(1024)S(1)} %get-tuple-element.243, ...), kind=kOutput, calls=%fused_computation.5.clone.1 | convolution fusion | flops 1213857024 | bytes 3164932 | tf_op jit(solution)/shard_map/while/body/eval_jaxpr/dot_general | solution.py:23
  274.3 0.7 all_to_all.30
  275.0 4.3 %all-to-all-start.2 = ((f32[8,96,1]{1,2,0:T(1,128)}), f32[8,96,1]{1,2,0:T(1,128)S(1)}, u32[]{:S(2)}, u32[]{:S(2)}) async-start(f32[8,96,1]{1,2,0:T(1,128)} %bitcast.5), calls=%async_computation.2 | async-start | bytes 8192 | tf_op jit(solution)/shard_map/all_to_all | solution.py:85
  279.3 5.3 %all-to-all-done.2 = f32[8,96,1]{1,2,0:T(1,128)S(1)} async-done(((f32[8,96,1]{1,2,0:T(1,128)}), f32[8,96,1]{1,2,0:T(1,128)S(1)}, u32[]{:S(2)}, u32[]{:S(2)}) %all-to-all-start.2) | async-done | bytes 3104 | tf_op jit(solution)/shard_map/all_to_all | solution.py:85
  284.5 0.5 broadcast.92
  285.1 0.7 reduce.9
  285.8 1.9 gather_fusion
  287.7 0.6 and_select_fusion
  (86 shorter events, 1.4 us)
Async XLA Ops:
  6.5 186.6 %all-gather.3.cloned.1.call-start = ((), (), s32[]{:S(2)}) async-start(), calls=%async_computation.3 | async-start | bytes 26738688 | tf_op jit(solution)/shard_map/all_gather | solution.py:63
  38.0 37.5 %copy-start = (bf16[8,96,1024]{2,1,0:T(8,128)(2,1)S(1)}, bf16[8,96,1024]{2,1,0:T(8,128)(2,1)}, u32[]{:S(2)}) copy-start(bf16[8,96,1024]{2,1,0:T(8,128)(2,1)} %all_to_all.37) | copy-start | bytes 4718596
  41.6 8.4 %all-to-all-start = ((bf16[8,96,1]{1,2,0:T(2,128)(2,1)}), bf16[8,96,1]{1,2,0:T(2,128)(2,1)S(1)}, u32[]{:S(2)}, u32[]{:S(2)}) async-start(bf16[8,96,1]{1,2,0:T(2,128)(2,1)} %all_to_all.33), calls=%async_computation | async-start | bytes 8192 | tf_op jit(solution)/shard_map/all_to_all | solution.py:58
  275.0 9.6 %all-to-all-start.2 = ((f32[8,96,1]{1,2,0:T(1,128)}), f32[8,96,1]{1,2,0:T(1,128)S(1)}, u32[]{:S(2)}, u32[]{:S(2)}) async-start(f32[8,96,1]{1,2,0:T(1,128)} %bitcast.5), calls=%async_computation.2 | async-start | bytes 8192 | tf_op jit(solution)/shard_map/all_to_all | solution.py:85
Sparse Core Ops, SparseCore 0:
  38.1 154.9 all-gather.2
where the time goes:
time: 297 us; the launch traced here: 295 us
  waiting for transfers between devices  128 us (43%)
  blocking collectives  51.3 us (17%)
  matrix products  49.9 us (17%)
  other arithmetic  32.6 us (11%)
  between operations  13.5 us (5%)
  local copies, waits for them, and re-layouts  11.8 us (4%)
  starting transfers between devices  7.55 us (3%)
    all_gather x1, waiting for transfers between devices, local(): piece_rows = lax.all_gather(own_rows, 'sub', axis=0, tiled=True)  117 us
    dot_general x16, matrix products, tile_max(): lax.dot_general(left_rows, right_rows, (((1,), (1,)), ((), ())), preferre...  49.9 us
    reduce_sum x17, other arithmetic, inverse_norms(): return lax.rsqrt(jnp.sum(values * values, axis=1) + EPSILON)  29 us
    all_to_all x1, blocking collectives, local(): lax.all_to_all(send_rows, 'grp', split_axis=0, concat_axis=0, tiled=True)  26.3 us
    all_gather x1, blocking collectives, local(): piece_ids = lax.all_gather(own_ids, 'sub', axis=0, tiled=True)  25 us
  transfers between devices with their start and end apart: 3, of which 3 were waited for; matrix products, arithmetic and copies ran while one was open for 1% of the time, Pallas kernels for 0%

commit v1 on v0

v1 whole, which is shorter than its diff:
```python
import functools
import math

import jax
import jax.numpy as jnp
from jax import lax
from jax.experimental import pallas as pl
from jax.experimental.pallas import tpu as pltpu
from jax.sharding import PartitionSpec as P

KG = 3
CAP = 96
EPSILON = 1e-06

ROWS = 384
CHUNK = 48
LIGHT = 42
EXTRA = 64
FIRST = 4 * CHUNK
SECOND = 4 * CHUNK + EXTRA
PARTS = (FIRST, SECOND)
LANES = 512
LOW = -1e30

STEPS = ((1, 1), (0, 1), (1, 3), (0, 3), (1, 2), (1, 0), (0, 2))

VMEM = pl.BlockSpec(memory_space=pltpu.VMEM)
PARAMS = pltpu.CompilerParams(vmem_limit_bytes=48 * 1024 * 1024)


def inverse_norms(block):
    values = block.astype(jnp.float32)
    return lax.rsqrt(jnp.sum(values * values, axis=1) + EPSILON)


def tile_max(left_rows, left_ids, left_inverse, right_rows, right_ids, right_inverse, left_first, right_first):
    scores = lax.dot_general(
        left_rows, right_rows, (((1,), (1,)), ((), ())), preferred_element_type=jnp.float32
    )
    scaled = scores * left_inverse[:, None] * right_inverse[None, :]
    left_index = left_first + jnp.arange(left_rows.shape[0], dtype=jnp.int32)
    right_index = right_first + jnp.arange(right_rows.shape[0], dtype=jnp.int32)
    same_cluster = (
        (left_ids[:, None] == right_ids[None, :])
        & (left_ids[:, None] >= 0)
        & (left_index[:, None] != right_index[None, :])
    )
    masked = jnp.where(same_cluster, scaled, jnp.float32(-1.0))
    return jnp.max(masked, axis=1)


def general(embeddings, cluster_ids):
    groups_count = lax.axis_size("grp")
    feature_count = embeddings.shape[1]
    destination = cluster_ids // KG
    onehot = (destination[:, None] == jnp.arange(groups_count, dtype=jnp.int32)[None, :]).astype(jnp.int32)
    earlier = jnp.cumsum(onehot, axis=0) - onehot
    slot_index = jnp.sum(earlier * onehot, axis=1)
    position = destination * CAP + slot_index
    send_rows = jnp.zeros((groups_count * CAP, feature_count), jnp.bfloat16).at[position].set(embeddings)
    send_ids = (
        jnp.full((groups_count * CAP,), -1.0, jnp.bfloat16).at[position].set(cluster_ids.astype(jnp.bfloat16))
    )
    own_rows = lax.all_to_all(send_rows, "grp", split_axis=0, concat_axis=0, tiled=True)
    own_ids = lax.all_to_all(send_ids, "grp", split_axis=0, concat_axis=0, tiled=True)
    own_count = own_rows.shape[0]
    own_inverse = inverse_norms(own_rows)
    sub_count = lax.axis_size("sub")
    own_sub = lax.axis_index("sub")
    ring = [(index, (index + 1) % sub_count) for index in range(sub_count)]

    def one_block(index, state):
        right_rows, right_ids, current = state
        row_max = tile_max(
            own_rows,
            own_ids,
            own_inverse,
            right_rows,
            right_ids,
            inverse_norms(right_rows),
            own_sub * own_count,
            ((own_sub - index) % sub_count) * own_count,
        )
        next_rows = lax.ppermute(right_rows, "sub", ring)
        next_ids = lax.ppermute(right_ids, "sub", ring)
        return next_rows, next_ids, jnp.maximum(current, row_max)

    start = (own_rows, own_ids, jnp.full((own_count,), -1.0, jnp.float32))
    best_seen = lax.fori_loop(0, sub_count, one_block, start)[2]
    gathered_back = lax.all_to_all(best_seen, "grp", split_axis=0, concat_axis=0, tiled=True)
    return jnp.take(gathered_back, position, axis=0)


def iota(shape, dim):
    return lax.broadcasted_iota(jnp.int32, shape, dim)


def dot_nt(left, right):
    return lax.dot_general(left, right, (((1,), (1,)), ((), ())), preferred_element_type=jnp.float32)


def dot_nn(left, right):
    return lax.dot_general(left, right, (((1,), (0,)), ((), ())), preferred_element_type=jnp.float32)


def three_parts(value):
    high = value.astype(jnp.bfloat16).astype(jnp.float32)
    rest = value - high
    middle = rest.astype(jnp.bfloat16).astype(jnp.float32)
    low = (rest - middle).astype(jnp.bfloat16).astype(jnp.float32)
    return high, middle, low


def as_bf16(mask):
    return jnp.where(mask, 1.0, 0.0).astype(jnp.bfloat16)


def owner_at(place_ref, step):
    dx, dz = (0, 0) if step < 0 else STEPS[step]
    return ((place_ref[0] + dx) % 2) * 4 + (place_ref[1] + dz) % 4


def lane_of_slot(slot):
    return slot * CHUNK if slot < 4 else 256 + (slot - 4) * CHUNK


def sort_kernel(at_ref, ids_ref, rows_ref, *out_refs):
    chunk_refs, extra_ref, lane_ref, home_ref = out_refs[:8], out_refs[8], out_refs[9], out_refs[10]
    ids = ids_ref[...].reshape(1, ROWS)
    group_of = iota((8, ROWS), 0)
    member = (ids >= group_of * KG) & (ids < group_of * KG + KG)
    member_f = jnp.where(member, 1.0, 0.0)
    before = as_bf16(iota((ROWS, ROWS), 0) < iota((ROWS, ROWS), 1))
    ranks = dot_nn(member_f.astype(jnp.bfloat16), before)
    rank = jnp.sum(member_f * ranks, axis=0, keepdims=True)
    group = jnp.sum(member_f * group_of.astype(jnp.float32), axis=0, keepdims=True)
    count = jnp.sum(member_f, axis=1, keepdims=True)
    most = jnp.where(count > 64.0, 1.0, 0.0)
    home = jnp.sum(most * iota((8, 1), 0).astype(jnp.float32), axis=0, keepdims=True)
    home_ref[...] = jnp.broadcast_to(home, home_ref.shape)
    values = rows_ref[...].astype(jnp.float32)
    inverse_column = lax.rsqrt(jnp.sum(values * values, axis=1, keepdims=True) + EPSILON)
    diagonal = iota((ROWS, ROWS), 0) == iota((ROWS, ROWS), 1)
    inverse = jnp.sum(jnp.where(diagonal, inverse_column, 0.0), axis=0, keepdims=True)
    high, middle, low = three_parts(inverse)
    line = iota((16, ROWS), 0)
    told = jnp.where(line == 10, ids.astype(jnp.float32) + 1.0, 0.0)
    told = jnp.where(line == 11, high, told)
    told = jnp.where(line == 12, middle, told)
    told = jnp.where(line == 13, low, told)
    lane = jnp.full((1, ROWS), -1.0, jnp.float32)
    tolds = []
    for slot in range(8):
        goes = (group == owner_at(at_ref, slot - 1).astype(jnp.float32)) & (rank < float(LIGHT))
        lane = jnp.where(goes, rank + float(lane_of_slot(slot)), lane)
        tolds.append(jnp.where(goes, told, 0.0))
    goes = (group == home) & (rank >= float(LIGHT))
    lane = jnp.where(goes, rank + float(lane_of_slot(8) - LIGHT), lane)
    tolds.append(jnp.where(goes, told, 0.0))
    lane_ref[...] = jnp.broadcast_to(lane, lane_ref.shape)
    pick = as_bf16(iota((LANES, ROWS), 0) == lane.astype(jnp.int32))
    data = dot_nn(pick, rows_ref[...])
    placed = dot_nt(jnp.concatenate(tolds, axis=0).astype(jnp.bfloat16), pick)
    for slot in range(9):
        ref = chunk_refs[slot] if slot < 8 else extra_ref
        first, count = lane_of_slot(slot), CHUNK if slot < 8 else EXTRA
        part = 0 if slot < 4 else 256
        ref[0 : count - 16, :] = data[first : first + count - 16].astype(jnp.bfloat16)
        tail = data[first + count - 16 : first + count]
        if slot == 8:
            tail = jnp.where(iota(tail.shape, 0) == 15, home + 1.0, tail)
        ref[count - 16 : count, :] = tail.astype(jnp.bfloat16)
        ref[count - 16 : count, 0:256] = (
            tail[:, 0:256] + placed[16 * slot : 16 * slot + 16, part : part + 256]
        ).astype(jnp.bfloat16)


def marked(ref):
    return ref[EXTRA - 16 : EXTRA, :].astype(jnp.float32)[15:16, 0:1]


def half_kernel(at_ref, own_ref, other_ref, out_ref):
    parity = at_ref[0] % 2
    own_fits = jnp.where(marked(own_ref) >= 5.0, 1, 0) == parity
    other_fits = jnp.where(marked(other_ref) >= 5.0, 1, 0) == parity
    taken = jnp.where(own_fits, own_ref[...], other_ref[...])
    out_ref[0 : EXTRA - 16, :] = taken[0 : EXTRA - 16]
    tail = taken[EXTRA - 16 : EXTRA].astype(jnp.float32)
    clash = (iota(tail.shape, 0) == 15) & (own_fits == other_fits)
    out_ref[EXTRA - 16 : EXTRA, :] = jnp.where(clash, 0.0, tail).astype(jnp.bfloat16)


def block_kernel(at_ref, *refs):
    chunks, extras, out_ref = refs[0:4], refs[4:8], refs[8]
    wanted = owner_at(at_ref, -1).astype(jnp.float32) + 1.0
    for index in range(4):
        out_ref[index * CHUNK : (index + 1) * CHUNK, :] = chunks[index][...]
    found = jnp.zeros((1, 1), jnp.float32)
    held = jnp.ones((1, 1), jnp.float32)
    taken = extras[0][...]
    for index in range(4):
        mark = marked(extras[index])
        found = found + jnp.where(mark == wanted, 1.0, 0.0)
        held = jnp.where(mark == 0.0, 0.0, held)
        if index > 0:
            taken = jnp.where(mark == wanted, extras[index][...], taken)
    good = jnp.where((found == 1.0) & (held == 1.0), 1.0, 0.0)
    out_ref[4 * CHUNK : SECOND - 16, :] = taken[0 : EXTRA - 16]
    tail = taken[EXTRA - 16 : EXTRA].astype(jnp.float32)
    out_ref[SECOND - 16 : SECOND, :] = jnp.where(iota(tail.shape, 0) == 14, good, tail).astype(jnp.bfloat16)


def told_of(ref, part):
    total = jnp.zeros((16, 256), jnp.float32)
    ends = [CHUNK, 2 * CHUNK, 3 * CHUNK, 4 * CHUNK] + ([SECOND] if part else [])
    for end in ends:
        total = total + ref[end - 16 : end, 0:256].astype(jnp.float32)
    rows = PARTS[part]
    return total[10:11, 0:rows], (total[11:12] + total[12:13] + total[13:14])[:, 0:rows], total[14:15, 0:1]


def column_of(row):
    count = row.shape[1]
    diagonal = iota((count, count), 0) == iota((count, count), 1)
    return jnp.sum(jnp.where(diagonal, row, 0.0), axis=1, keepdims=True)


def best_of(lefts, rights, own, out_refs):
    left_known = [[told_of(ref, part) for part, ref in enumerate(left)] for left in lefts]
    best = [[jnp.full((1, rows), LOW, jnp.float32) for rows in PARTS] for _ in lefts]
    for right_index, right in enumerate(rights):
        for right_part, right_ref in enumerate(right):
            ids, inverse, _ = told_of(right_ref, right_part)
            ids, inverse = column_of(ids), column_of(inverse)
            rows = right_ref[...]
            for left_index, left in enumerate(lefts):
                for left_part, left_ref in enumerate(left):
                    scores = dot_nt(rows, left_ref[...]) * inverse
                    alike = ids == left_known[left_index][left_part][0]
                    if own and left_index == 0 and right_index == 0 and left_part == right_part:
                        alike = alike & (iota(scores.shape, 0) != iota(scores.shape, 1))
                    top = jnp.max(jnp.where(alike, scores, LOW), axis=0, keepdims=True)
                    best[left_index][left_part] = jnp.maximum(best[left_index][left_part], top)
    for left_index, out_ref in enumerate(out_refs):
        out_ref[...] = jnp.full(out_ref.shape, -1.0, jnp.float32)
        for part, rows in enumerate(PARTS):
            inverse = left_known[left_index][part][1]
            out_ref[0:1, 256 * part : 256 * part + rows] = jnp.maximum(best[left_index][part] * inverse, -1.0)


def match_kernel(left_count, right_count, own, checked, *refs):
    pairs = [(refs[2 * index], refs[2 * index + 1]) for index in range(left_count + right_count)]
    out_refs = refs[2 * (left_count + right_count) :]
    best_of(pairs[:left_count], pairs[left_count:], own, out_refs)
    if checked:
        good = jnp.minimum(told_of(pairs[0][1], 1)[2], told_of(pairs[left_count][1], 1)[2])
        out_refs[0][1:2, :] = jnp.broadcast_to(good, (1, LANES))


def far_kernel(first_a, first_b, second_a, second_b, *refs):
    rights = [(refs[2 * index], refs[2 * index + 1]) for index in range(4)]
    out_ref, first, second = refs[8], refs[9], refs[10]
    first[0 : FIRST // 2, :] = first_a[...]
    first[FIRST // 2 : FIRST, :] = first_b[...]
    second[0 : SECOND // 2, :] = second_a[...]
    second[SECOND // 2 : SECOND, :] = second_b[...]
    best_of([(first, second)], rights, False, [out_ref])


def final_kernel(at_ref, own_ref, side_ref, z1_ref, z2_ref, z3_ref, lane_ref, home_ref, out_ref, ok_ref):
    lane = iota((1, LANES), 1)
    own = own_ref[0:1, :]
    good = own_ref[1:2, :]
    home = home_ref[0:1, 0:1]
    extra = jnp.where(home == owner_at(at_ref, -1).astype(jnp.float32), own, -1.0)
    total = own
    sources = {1: z1_ref, 2: z2_ref, 3: z3_ref}
    for step, (dx, dz) in enumerate(STEPS):
        ref, row = (side_ref, 0) if dz == 0 else (sources[dz], 8 * dx)
        vector = ref[row : row + 1, :]
        good = jnp.minimum(good, ref[row + 1 : row + 2, :])
        first = lane_of_slot(step + 1)
        total = jnp.where((lane >= first) & (lane < first + CHUNK), vector, total)
        extra = jnp.where(home == owner_at(at_ref, step).astype(jnp.float32), vector, extra)
    total = jnp.where(lane >= lane_of_slot(8), extra, total)
    high, middle, low = three_parts(total)
    line = iota((16, LANES), 0)
    parts = jnp.where(line == 0, high, jnp.where(line == 1, middle, jnp.where(line == 2, low, 0.0)))
    pick = as_bf16(iota((LANES, ROWS), 0) == lane_ref[0:1, :].astype(jnp.int32))
    picked = dot_nn(parts.astype(jnp.bfloat16), pick)
    out_ref[...] = jnp.sum(picked, axis=0, keepdims=True).reshape(ROWS)
    ok_ref[...] = jnp.where(good[:, 0:128] == 1.0, 1, 0)


SMEM = pl.BlockSpec(memory_space=pltpu.SMEM)


def call(kernel, outs, *args, scalars=0, scratch=(), flops=0):
    read = sum(math.prod(a.shape) * a.dtype.itemsize for a in args)
    return pl.pallas_call(
        kernel,
        out_shape=outs,
        in_specs=[SMEM] * scalars + [VMEM] * (len(args) - scalars),
        out_specs=[VMEM] * len(outs) if isinstance(outs, list) else VMEM,
        scratch_shapes=list(scratch),
        compiler_params=PARAMS,
        cost_estimate=pl.CostEstimate(flops=flops, bytes_accessed=read, transcendentals=0),
    )(*args)


def along_sub(value, to_x, to_z):
    perm = [(4 * x + z, 4 * to_x(x) + to_z(z)) for x in range(4) for z in range(4)]
    return lax.ppermute(value, "sub", perm)


def along_grp(value, to_y, to_core):
    perm = [(2 * y + c, 2 * to_y(y) + to_core(c)) for y in range(4) for c in range(2)]
    return lax.ppermute(value, "grp", perm)


def same(index):
    return index


def shift(amount):
    return lambda index: (index + amount) % 4


def flip(amount):
    return lambda index: index ^ amount


def local(embeddings, cluster_ids):
    f32, bf16 = jnp.float32, jnp.bfloat16
    width = embeddings.shape[1]
    shape = jax.ShapeDtypeStruct
    sub = lax.axis_index("sub")
    at = jnp.stack([sub // 4, sub % 4]).astype(jnp.int32)
    *chunks, extra, lane, home = call(
        sort_kernel,
        [shape((CHUNK, width), bf16)] * 8
        + [shape((EXTRA, width), bf16), shape((8, ROWS), f32), shape((8, 128), f32)],
        at,
        cluster_ids,
        embeddings,
        scalars=1,
        flops=500_000_000,
    )
    other_extra = along_sub(extra, flip(1), same)
    got = [chunks[0]] + [along_sub(chunk, flip(dx), shift(dz)) for chunk, (dx, dz) in zip(chunks[1:], STEPS)]
    extra = call(half_kernel, shape((EXTRA, width), bf16), at, extra, other_extra, scalars=1)
    extras = [extra] + [along_sub(extra, same, shift(dz)) for dz in (1, 2, 3)]
    first = jnp.concatenate(got[:4], axis=0)
    second = call(block_kernel, shape((SECOND, width), bf16), at, *got[4:], *extras, scalars=1)
    block = (first, second)
    below = tuple(along_grp(part, shift(1), same) for part in block)
    above = tuple(along_grp(part, shift(-1), same) for part in block)
    across = tuple(along_sub(part, shift(2), same) for part in block)
    sibling = tuple(along_grp(part, same, flip(1)) for part in block)
    across_sibling = tuple(along_grp(part, same, flip(1)) for part in across)
    far = [along_grp(part[: part.shape[0] // 2], shift(1), same) for part in below]
    far += [along_grp(part[part.shape[0] // 2 :], shift(-1), same) for part in above]
    flops = 2 * sum(PARTS) ** 2 * width
    vector = shape((8, LANES), f32)
    near = (*block, *sibling)
    others = (*across, *across_sibling)

    def match(lefts, rights, own=False, checked=False):
        kernel = functools.partial(match_kernel, len(lefts) // 2, len(rights) // 2, own, checked)
        work = flops * len(lefts) * len(rights) // 4
        out = call(kernel, [vector] * (len(lefts) // 2), *lefts, *rights, flops=work)
        return out

    (best_near,) = match(block, near, own=True)
    below_near, above_near = match((*below, *above), near)
    best, below_other, above_other = match((*block, *below, *above), others, checked=True)
    from_above = along_grp(jnp.maximum(below_near, below_other), shift(-1), same)
    from_below = along_grp(jnp.maximum(above_near, above_other), shift(1), same)
    best_far = call(
        far_kernel,
        vector,
        far[0],
        far[2],
        far[1],
        far[3],
        *near,
        *others,
        scratch=[pltpu.VMEM((rows, width), bf16) for rows in PARTS],
        flops=4 * flops,
    )
    from_far = along_grp(best_far, shift(2), same)
    best = jnp.maximum(jnp.maximum(best, best_near), jnp.maximum(from_above, from_below))
    best = jnp.maximum(best, from_far)
    side = along_sub(best, flip(1), same)
    both = jnp.concatenate([best, side], axis=0)
    pulled = [along_sub(both, same, shift(-dz)) for dz in (1, 2, 3)]
    out, ok = call(
        final_kernel,
        [shape((ROWS,), f32), shape((1, 128), jnp.int32)],
        at,
        best,
        side,
        *pulled,
        lane,
        home,
        scalars=1,
    )
    return lax.cond(ok[0, 0] == 1, lambda e, c, o: o, lambda e, c, o: general(e, c), embeddings, cluster_ids, out)


def solution(mesh):
    return jax.shard_map(
        local,
        mesh=mesh,
        in_specs=(P(("grp", "sub"), None), P(("grp", "sub"))),
        out_specs=P(("grp", "sub")),
        check_vma=False,
    )
```

time: 297 us -> 95.4 us (0.32)
  waiting for transfers between devices: 128 us -> 38.4 us
  blocking collectives: 51.3 us -> 0 us
  matrix products: 49.9 us -> 0 us
  starting transfers between devices: 7.55 us -> 42.4 us
  other arithmetic: 32.6 us -> 0.1 us
  Pallas kernels: 0 us -> 13.4 us
  between operations: 13.5 us -> 0.24 us
  local copies, waits for them, and re-layouts: 11.8 us -> 0.67 us
    all_gather x1 -> x0, waiting for transfers between devices: 117 us -> none  [local(): piece_rows = lax.all_gather(own_rows, 'sub', axis=0, tiled=True)]
    dot_general x16 -> x0, matrix products: 49.9 us -> none  [tile_max(): lax.dot_general(left_rows, right_rows, (((1,), (1,)), ((), ())), preferre...]
    ppermute x0 -> x32, starting transfers between devices: none -> 42.4 us  [the longest x17 24.5 us: along_sub(): return lax.ppermute(value, 'sub', perm)]
    ppermute x0 -> x32, waiting for transfers between devices: none -> 38.4 us  [the longest x17 21.7 us: along_sub(): return lax.ppermute(value, 'sub', perm)]
    reduce_sum x18 -> x0, other arithmetic: 29.1 us -> none  [the longest x17 29 us: inverse_norms(): return lax.rsqrt(jnp.sum(values * values, axis=1) + EPSILON)]
    all_to_all x1 -> x0, blocking collectives: 26.3 us -> none  [local(): lax.all_to_all(send_rows, 'grp', split_axis=0, concat_axis=0, tiled=True)]
    all_gather x1 -> x0, blocking collectives: 25 us -> none  [local(): piece_ids = lax.all_gather(own_ids, 'sub', axis=0, tiled=True)]
    pallas_call x0 -> x8, Pallas kernels: none -> 13.4 us  [call(): pl.pallas_call(kernel, out_shape=outs, in_specs=[SMEM] * scalars + [VMEM]...]
  transfers between devices with their start and end apart: 3 -> 32, of which waited for: 3 -> 11; matrix products, arithmetic and copies ran while one was open for 1% -> 0% of each run, Pallas kernels for 0% -> 11%
where the time goes in v1:
time: 95.4 us; the launch traced here: 95.2 us
  starting transfers between devices  42.4 us (44%)
  waiting for transfers between devices  38.4 us (40%)
  Pallas kernels  13.4 us (14%)
    ppermute x17, starting transfers between devices, along_sub(): return lax.ppermute(value, 'sub', perm)  24.5 us
    ppermute x17, waiting for transfers between devices, along_sub(): return lax.ppermute(value, 'sub', perm)  21.7 us
    ppermute x15, starting transfers between devices, along_grp(): return lax.ppermute(value, 'grp', perm)  17.9 us
    ppermute x15, waiting for transfers between devices, along_grp(): return lax.ppermute(value, 'grp', perm)  16.7 us
    pallas_call x8, Pallas kernels, call(): pl.pallas_call(kernel, out_shape=outs, in_specs=[SMEM] * scalars + [VMEM]...  13.4 us
  transfers between devices with their start and end apart: 32, of which 11 were waited for; matrix products, arithmetic and copies ran while one was open for 0% of the time, Pallas kernels for 11%

profile of v1, /device:TPU:0, one launch (start us, length us, event | category | flops | bytes accessed | tf_op | source)
XLA Modules:
  0.0 95.2 jit_solution(12303284398191001842)
XLA Ops:
  0.0 0.1 pad_add_fusion.at_ref
  0.1 2.1 %shard_map.30 = (bf16[48,1024]{1,0:T(8,128)(2,1)S(1)}, bf16[48,1024]{1,0:T(8,128)(2,1)S(1)}, bf16[48,1024]{1,0:T(8,128)(2,1)S(1)}, bf16[48,1024]{1,0:T(8,128)(2,...) custom-call(s32[2]{0:T(128)S(1)} %pad_add_fusion.at_ref, ...), custom_call_target="tpu_custom_call" | custom-call | flops 500000000 | bytes 787976 | tf_op jit(solution)/shard_map/pallas_call | solution.py:300
  2.2 1.7 %collective-permute-start.9 = (bf16[64,1024]{1,0:T(8,128)(2,1)S(1)}, bf16[64,1024]{1,0:T(8,128)(2,1)S(1)}, u32[]{:S(2)}, u32[]{:S(2)}) collective-permute-start(bf16[64,1024]{1,0:T(8,128)(2,1)S(1)} %get-tuple-element.246.own_ref), channel_id=1, source_target_pairs={{0,4},{1,5},{2,6},{3,7},{4,0},{5,1},{6,2},{7,3},{8,12},{9,13},{10,... | collective-permute-start | bytes 393224 | tf_op jit(solution)/shard_map/ppermute | solution.py:313
  3.8 4.0 %collective-permute-start.5 = (bf16[48,1024]{1,0:T(8,128)(2,1)S(1)}, bf16[48,1024]{1,0:T(8,128)(2,1)S(1)}, u32[]{:S(2)}, u32[]{:S(2)}) collective-permute-start(bf16[48,1024]{1,0:T(8,128)(2,1)S(1)} %get-tuple-element.242), channel_id=1, source_target_pairs={{0,3},{1,0},{2,1},{3,2},{4,7},{5,4},{6,5},{7,6},{8,11},{9,8},{10,9... | collective-permute-start | bytes 294920 | tf_op jit(solution)/shard_map/ppermute | solution.py:313
  7.9 0.0 collective-permute-start.6
  7.9 1.4 %collective-permute-start.7 = (bf16[48,1024]{1,0:T(8,128)(2,1)S(1)}, bf16[48,1024]{1,0:T(8,128)(2,1)S(1)}, u32[]{:S(2)}, u32[]{:S(2)}) collective-permute-start(bf16[48,1024]{1,0:T(8,128)(2,1)S(1)} %get-tuple-element.244), channel_id=1, source_target_pairs={{0,4},{1,5},{2,6},{3,7},{4,0},{5,1},{6,2},{7,3},{8,12},{9,13},{10,... | collective-permute-start | bytes 294920 | tf_op jit(solution)/shard_map/ppermute | solution.py:313
  9.3 1.3 %collective-permute-start.2 = (bf16[48,1024]{1,0:T(8,128)(2,1)S(1)}, bf16[48,1024]{1,0:T(8,128)(2,1)S(1)}, u32[]{:S(2)}, u32[]{:S(2)}) collective-permute-start(bf16[48,1024]{1,0:T(8,128)(2,1)S(1)} %get-tuple-element.239), channel_id=1, source_target_pairs={{0,5},{1,6},{2,7},{3,4},{4,1},{5,2},{6,3},{7,0},{8,13},{9,14},{10,... | collective-permute-start | bytes 294920 | tf_op jit(solution)/shard_map/ppermute | solution.py:313
  10.6 6.8 %collective-permute-done.2 = bf16[48,1024]{1,0:T(8,128)(2,1)S(1)} collective-permute-done((bf16[48,1024]{1,0:T(8,128)(2,1)S(1)}, bf16[48,1024]{1,0:T(8,128)(2,1)S(1)}, u32[]{:S(2)}, u32[]{:S(2)}) %collective-permute-start.2) | collective-permute-done | bytes 98336 | tf_op jit(solution)/shard_map/ppermute | solution.py:313
  17.4 0.0 collective-permute-start.3
  17.4 5.8 %collective-permute-done.3 = bf16[48,1024]{1,0:T(8,128)(2,1)S(1)} collective-permute-done((bf16[48,1024]{1,0:T(8,128)(2,1)S(1)}, bf16[48,1024]{1,0:T(8,128)(2,1)S(1)}, u32[]{:S(2)}, u32[]{:S(2)}) %collective-permute-start.3) | collective-permute-done | bytes 98336 | tf_op jit(solution)/shard_map/ppermute | solution.py:313
  23.2 0.6 collective-permute-start.4
  23.8 0.0 collective-permute-done.9.other_ref
  23.8 1.3 %collective-permute-start.8 = (bf16[48,1024]{1,0:T(8,128)(2,1)S(1)}, bf16[48,1024]{1,0:T(8,128)(2,1)S(1)}, u32[]{:S(2)}, u32[]{:S(2)}) collective-permute-start(bf16[48,1024]{1,0:T(8,128)(2,1)S(1)} %get-tuple-element.245), channel_id=1, source_target_pairs={{0,2},{1,3},{2,0},{3,1},{4,6},{5,7},{6,4},{7,5},{8,10},{9,11},{10,... | collective-permute-start | bytes 294920 | tf_op jit(solution)/shard_map/ppermute | solution.py:313
  25.1 0.6 shard_map.31.refs_4_
  25.7 0.0 collective-permute-done.5.refs_0_
  25.7 1.2 %collective-permute-start.10 = (bf16[64,1024]{1,0:T(8,128)(2,1)S(1)}, bf16[64,1024]{1,0:T(8,128)(2,1)S(1)}, u32[]{:S(2)}, u32[]{:S(2)}) collective-permute-start(bf16[64,1024]{1,0:T(8,128)(2,1)S(1)} %shard_map.31.refs_4_), channel_id=1, source_target_pairs={{0,1},{1,2},{2,3},{3,0},{4,5},{5,6},{6,7},{7,4},{8,9},{9,10},{10,1... | collective-permute-start | bytes 393224 | tf_op jit(solution)/shard_map/ppermute | solution.py:313
  26.9 0.0 collective-permute-done.6.refs_1_
  27.0 4.1 %collective-permute-start.11 = (bf16[64,1024]{1,0:T(8,128)(2,1)S(1)}, bf16[64,1024]{1,0:T(8,128)(2,1)S(1)}, u32[]{:S(2)}, u32[]{:S(2)}) collective-permute-start(bf16[64,1024]{1,0:T(8,128)(2,1)S(1)} %shard_map.31.refs_4_), channel_id=1, source_target_pairs={{0,2},{1,3},{2,0},{3,1},{4,6},{5,7},{6,4},{7,5},{8,10},{9,11},{10,... | collective-permute-start | bytes 393224 | tf_op jit(solution)/shard_map/ppermute | solution.py:313
  31.1 0.0 collective-permute-done.4
  31.1 0.0 collective-permute-start.12
  31.1 0.0 collective-permute-done.7.refs_2_
  31.1 2.8 %collective-permute-start.17 = (bf16[192,1024]{1,0:T(8,128)(2,1)S(1)}, bf16[192,1024]{1,0:T(8,128)(2,1)S(1)}, u32[]{:S(2)}, u32[]{:S(2)}) collective-permute-start(bf16[192,1024]{1,0:T(8,128)(2,1)S(1)} %constant_dynamic-update-slice_fusion.refs_0_.refs_2_.refs_4_), channel_id=1, source_target_pairs={{0,8},{1,9},{2,10},{3,11},{4,12},{5,13},{6,14},{7,15},{8,0},{9,1},... | collective-permute-start | bytes 1179656 | tf_op jit(solution)/shard_map/ppermute | solution.py:313
  33.9 0.0 collective-permute-done.8.refs_3_
  33.9 1.6 %collective-permute-start.13 = (bf16[192,1024]{1,0:T(8,128)(2,1)S(1)}, bf16[192,1024]{1,0:T(8,128)(2,1)S(1)}, u32[]{:S(2)}, u32[]{:S(2)}) collective-permute-start(bf16[192,1024]{1,0:T(8,128)(2,1)S(1)} %constant_dynamic-update-slice_fusion.refs_0_.refs_2_.refs_4_), channel_id=1, source_target_pairs={{0,32},{16,48},{32,64},{48,80},{64,96},{80,112},{96,0},{112,16},{1... | collective-permute-start | bytes 1179656 | tf_op jit(solution)/shard_map/ppermute | solution.py:318
  35.5 0.0 collective-permute-done.10.refs_5_
  35.5 0.0 collective-permute-done.11.refs_6_
  35.5 0.6 collective-permute-done.12.refs_7_
  36.0 0.6 shard_map.32.refs_1_.refs_3_.refs_5_
  36.7 2.8 %collective-permute-start.18 = (bf16[256,1024]{1,0:T(8,128)(2,1)S(1)}, bf16[256,1024]{1,0:T(8,128)(2,1)S(1)}, u32[]{:S(2)}, u32[]{:S(2)}) collective-permute-start(bf16[256,1024]{1,0:T(8,128)(2,1)S(1)} %shard_map.32.refs_1_.refs_3_.refs_5_), channel_id=1, source_target_pairs={{0,8},{1,9},{2,10},{3,11},{4,12},{5,13},{6,14},{7,15},{8,0},{9,1},... | collective-permute-start | bytes 1572872 | tf_op jit(solution)/shard_map/ppermute | solution.py:313
  39.5 3.0 %collective-permute-start.15 = (bf16[192,1024]{1,0:T(8,128)(2,1)S(1)}, bf16[192,1024]{1,0:T(8,128)(2,1)S(1)}, u32[]{:S(2)}, u32[]{:S(2)}) collective-permute-start(bf16[192,1024]{1,0:T(8,128)(2,1)S(1)} %constant_dynamic-update-slice_fusion.refs_0_.refs_2_.refs_4_), channel_id=1, source_target_pairs={{0,96},{16,112},{32,0},{48,16},{64,32},{80,48},{96,64},{112,80},{1... | collective-permute-start | bytes 1179656 | tf_op jit(solution)/shard_map/ppermute | solution.py:318
  42.5 0.0 collective-permute-start.14
  42.5 0.4 collective-permute-done.17.refs_6_.refs_4_
  42.9 3.0 %collective-permute-start.16 = (bf16[256,1024]{1,0:T(8,128)(2,1)S(1)}, bf16[256,1024]{1,0:T(8,128)(2,1)S(1)}, u32[]{:S(2)}, u32[]{:S(2)}) collective-permute-start(bf16[256,1024]{1,0:T(8,128)(2,1)S(1)} %shard_map.32.refs_1_.refs_3_.refs_5_), channel_id=1, source_target_pairs={{0,96},{16,112},{32,0},{48,16},{64,32},{80,48},{96,64},{112,80},{1... | collective-permute-start | bytes 1572872 | tf_op jit(solution)/shard_map/ppermute | solution.py:318
  45.9 0.0 collective-permute-done.13.refs_2_.refs_0_
  45.9 0.0 collective-permute-start.22
  45.9 6.2 %collective-permute-done.15.refs_4_.refs_2_ = bf16[192,1024]{1,0:T(8,128)(2,1)S(1)} collective-permute-done((bf16[192,1024]{1,0:T(8,128)(2,1)S(1)}, bf16[192,1024]{1,0:T(8,128)(2,1)S(1)}, u32[]{:S(2)}, u32[]{:S(2)}) %collective-permute-start.15) | collective-permute-done | bytes 393248 | tf_op jit(solution)/shard_map/ppermute | solution.py:318
  52.1 0.0 collective-permute-done.18.refs_7_.refs_5_
  52.1 0.5 collective-permute-start.20
  52.6 1.8 %collective-permute-done.14.refs_3_.refs_1_ = bf16[256,1024]{1,0:T(8,128)(2,1)S(1)} collective-permute-done((bf16[256,1024]{1,0:T(8,128)(2,1)S(1)}, bf16[256,1024]{1,0:T(8,128)(2,1)S(1)}, u32[]{:S(2)}, u32[]{:S(2)}) %collective-permute-start.14) | collective-permute-done | bytes 524320 | tf_op jit(solution)/shard_map/ppermute | solution.py:318
  54.5 4.9 %collective-permute-done.16.refs_5_.refs_3_ = bf16[256,1024]{1,0:T(8,128)(2,1)S(1)} collective-permute-done((bf16[256,1024]{1,0:T(8,128)(2,1)S(1)}, bf16[256,1024]{1,0:T(8,128)(2,1)S(1)}, u32[]{:S(2)}, u32[]{:S(2)}) %collective-permute-start.16) | collective-permute-done | bytes 524320 | tf_op jit(solution)/shard_map/ppermute | solution.py:318
  59.4 1.0 %collective-permute-start.25 = (bf16[96,1024]{1,0:T(8,128)(2,1)S(1)}, bf16[96,1024]{1,0:T(8,128)(2,1)S(1)}, u32[]{:S(2)}, u32[]{:S(2)}) collective-permute-start(bf16[96,1024]{1,0:T(8,128)(2,1)S(1)} %slice.29), channel_id=1, source_target_pairs={{0,32},{16,48},{32,64},{48,80},{64,96},{80,112},{96,0},{112,16},{1... | collective-permute-start | bytes 589832 | tf_op jit(solution)/shard_map/ppermute | solution.py:318
  60.5 0.0 collective-permute-done.21.refs_4_.refs_6_.refs_2_
  60.5 1.6 %collective-permute-start.27 = (bf16[128,1024]{1,0:T(8,128)(2,1)S(1)}, bf16[128,1024]{1,0:T(8,128)(2,1)S(1)}, u32[]{:S(2)}, u32[]{:S(2)}) collective-permute-start(bf16[128,1024]{1,0:T(8,128)(2,1)S(1)} %slice.31), channel_id=1, source_target_pairs={{0,32},{16,48},{32,64},{48,80},{64,96},{80,112},{96,0},{112,16},{1... | collective-permute-start | bytes 786440 | tf_op jit(solution)/shard_map/ppermute | solution.py:318
  62.1 1.7 %collective-permute-start.28 = (bf16[128,1024]{1,0:T(8,128)(2,1)S(1)}, bf16[128,1024]{1,0:T(8,128)(2,1)S(1)}, u32[]{:S(2)}, u32[]{:S(2)}) collective-permute-start(bf16[128,1024]{1,0:T(8,128)(2,1)S(1)} %slice.32), channel_id=1, source_target_pairs={{0,96},{16,112},{32,0},{48,16},{64,32},{80,48},{96,64},{112,80},{1... | collective-permute-start | bytes 786440 | tf_op jit(solution)/shard_map/ppermute | solution.py:318
  63.8 2.3 %shard_map.35 = (f32[8,512]{1,0:T(8,128)S(1)}, f32[8,512]{1,0:T(8,128)S(1)}) custom-call(bf16[192,1024]{1,0:T(8,128)(2,1)S(1)} %collective-permute-done.13.refs_2_.refs_0_, bf16[256,1024]{1,0:T(8,128)(2,1)S(1)} %collective-permute-done.14.refs_3_.refs_1_, bf16[192,1024]{1,0:T(8,128)(2,1)S(1)} %collective-permute-done.15.refs_4_.refs_2_, ...), custom_call_target="tpu_custom_call" | custom-call | flops 1644167168 | bytes 3670016 | tf_op jit(solution)/shard_map/pallas_call | solution.py:300
  66.1 1.8 %collective-permute-start.26 = (bf16[96,1024]{1,0:T(8,128)(2,1)S(1)}, bf16[96,1024]{1,0:T(8,128)(2,1)S(1)}, u32[]{:S(2)}, u32[]{:S(2)}) collective-permute-start(bf16[96,1024]{1,0:T(8,128)(2,1)S(1)} %slice.30), channel_id=1, source_target_pairs={{0,96},{16,112},{32,0},{48,16},{64,32},{80,48},{96,64},{112,80},{1... | collective-permute-start | bytes 589832 | tf_op jit(solution)/shard_map/ppermute | solution.py:318
  67.9 3.4 %shard_map.33 = (f32[8,512]{1,0:T(8,128)S(1)}, f32[8,512]{1,0:T(8,128)S(1)}, f32[8,512]{1,0:T(8,128)S(1)}) custom-call(bf16[192,1024]{1,0:T(8,128)(2,1)S(1)} %constant_dynamic-update-slice_fusion.refs_0_.refs_2_.refs_4_, bf16[256,1024]{1,0:T(8,128)(2,1)S(1)} %shard_map.32.refs_1_.refs_3_.refs_5_, ...), custom_call_target="tpu_custom_call" | custom-call | flops 2466250752 | bytes 4587520 | tf_op jit(solution)/shard_map/pallas_call | solution.py:300
  71.3 0.6 collective-permute-start.24
  71.9 0.0 collective-permute-done.25.first_a
  71.9 2.8 %collective-permute-start.23 = (f32[8,512]{1,0:T(8,128)S(1)}, f32[8,512]{1,0:T(8,128)S(1)}, u32[]{:S(2)}, u32[]{:S(2)}) collective-permute-start(f32[8,512]{1,0:T(8,128)S(1)} %max.29), channel_id=1, source_target_pairs={{0,96},{16,112},{32,0},{48,16},{64,32},{80,48},{96,64},{112,80},{1... | collective-permute-start | bytes 49160 | tf_op jit(solution)/shard_map/ppermute | solution.py:318
  74.7 2.3 %shard_map.36 = f32[8,512]{1,0:T(8,128)S(1)} custom-call(bf16[96,1024]{1,0:T(8,128)(2,1)S(1)} %collective-permute-done.25.first_a, bf16[96,1024]{1,0:T(8,128)(2,1)S(1)} %collective-permute-done.26.first_b, bf16[128,1024]{1,0:T(8,128)(2,1)S(1)} %collective-permute-done.27.second_a, bf16[128,1024]{1,0:T(8,128)(2,1)S(1)} %collective-permute-done.28.second_b, ...), custom_call_target="tpu_custom_call" | custom-call | flops 1644167168 | bytes 4587520 | tf_op jit(solution)/shard_map/pallas_call | solution.py:300
  77.0 0.0 copy-start
  77.0 0.3 collective-permute-start.29
  77.3 1.3 %shard_map.34 = f32[8,512]{1,0:T(8,128)S(1)} custom-call(bf16[192,1024]{1,0:T(8,128)(2,1)S(1)} %constant_dynamic-update-slice_fusion.refs_0_.refs_2_.refs_4_, bf16[256,1024]{1,0:T(8,128)(2,1)S(1)} %shard_map.32.refs_1_.refs_3_.refs_5_, bf16[192,1024]{1,0:T(8,128)(2,1)S(1)} %constant_dynamic-update-slice_fusion.refs_0_.refs_2_.refs_4_, ...), custom_call_target="tpu_custom_call" | custom-call | flops 822083584 | bytes 2752512 | tf_op jit(solution)/shard_map/pallas_call | solution.py:300
  78.6 3.7 %collective-permute-done.29 = f32[8,512]{1,0:T(8,128)S(1)} collective-permute-done((f32[8,512]{1,0:T(8,128)S(1)}, f32[8,512]{1,0:T(8,128)S(1)}, u32[]{:S(2)}, u32[]{:S(2)}) %collective-permute-start.29) | collective-permute-done | bytes 16416 | tf_op jit(solution)/shard_map/ppermute | solution.py:318
  82.4 0.3 collective-permute-start.30
  82.7 3.5 %collective-permute-done.30.side_ref = f32[8,512]{1,0:T(8,128)S(1)} collective-permute-done((f32[8,512]{1,0:T(8,128)S(1)}, f32[8,512]{1,0:T(8,128)S(1)}, u32[]{:S(2)}, u32[]{:S(2)}) %collective-permute-start.30) | collective-permute-done | bytes 16416 | tf_op jit(solution)/shard_map/ppermute | solution.py:313
  86.2 2.1 %collective-permute-start.31 = (f32[16,512]{1,0:T(8,128)S(1)}, f32[16,512]{1,0:T(8,128)S(1)}, u32[]{:S(2)}, u32[]{:S(2)}) collective-permute-start(f32[16,512]{1,0:T(8,128)S(1)} %pad_maximum_fusion), channel_id=1, source_target_pairs={{0,3},{1,0},{2,1},{3,2},{4,7},{5,4},{6,5},{7,6},{8,11},{9,8},{10,9... | collective-permute-start | bytes 98312 | tf_op jit(solution)/shard_map/ppermute | solution.py:313
  88.3 0.9 collective-permute-start.33
  89.2 0.9 collective-permute-done.31.z1_ref
  90.1 3.7 %collective-permute-done.32.z2_ref = f32[16,512]{1,0:T(8,128)S(1)} collective-permute-done((f32[16,512]{1,0:T(8,128)S(1)}, f32[16,512]{1,0:T(8,128)S(1)}, u32[]{:S(2)}, u32[]{:S(2)}) %collective-permute-start.32) | collective-permute-done | bytes 32800 | tf_op jit(solution)/shard_map/ppermute | solution.py:313
  93.8 0.8 shard_map.37
  94.7 0.0 copy-start.1
  94.7 0.6 copy-done.1
  (26 shorter events, 0.2 us)
Async XLA Ops:
  2.2 21.6 %collective-permute-start.9 = (bf16[64,1024]{1,0:T(8,128)(2,1)S(1)}, bf16[64,1024]{1,0:T(8,128)(2,1)S(1)}, u32[]{:S(2)}, u32[]{:S(2)}) collective-permute-start(bf16[64,1024]{1,0:T(8,128)(2,1)S(1)} %get-tuple-element.246.own_ref), channel_id=1, source_target_pairs={{0,4},{1,5},{2,6},{3,7},{4,0},{5,1},{6,2},{7,3},{8,12},{9,13},{10,... | collective-permute-start | bytes 393224 | tf_op jit(solution)/shard_map/ppermute | solution.py:313
  3.8 21.9 %collective-permute-start.5 = (bf16[48,1024]{1,0:T(8,128)(2,1)S(1)}, bf16[48,1024]{1,0:T(8,128)(2,1)S(1)}, u32[]{:S(2)}, u32[]{:S(2)}) collective-permute-start(bf16[48,1024]{1,0:T(8,128)(2,1)S(1)} %get-tuple-element.242), channel_id=1, source_target_pairs={{0,3},{1,0},{2,1},{3,2},{4,7},{5,4},{6,5},{7,6},{8,11},{9,8},{10,9... | collective-permute-start | bytes 294920 | tf_op jit(solution)/shard_map/ppermute | solution.py:313
  7.9 19.1 %collective-permute-start.6 = (bf16[48,1024]{1,0:T(8,128)(2,1)S(1)}, bf16[48,1024]{1,0:T(8,128)(2,1)S(1)}, u32[]{:S(2)}, u32[]{:S(2)}) collective-permute-start(bf16[48,1024]{1,0:T(8,128)(2,1)S(1)} %get-tuple-element.243), channel_id=1, source_target_pairs={{0,6},{1,7},{2,4},{3,5},{4,2},{5,3},{6,0},{7,1},{8,14},{9,15},{10,... | collective-permute-start | bytes 294920 | tf_op jit(solution)/shard_map/ppermute | solution.py:313
  7.9 23.2 %collective-permute-start.7 = (bf16[48,1024]{1,0:T(8,128)(2,1)S(1)}, bf16[48,1024]{1,0:T(8,128)(2,1)S(1)}, u32[]{:S(2)}, u32[]{:S(2)}) collective-permute-start(bf16[48,1024]{1,0:T(8,128)(2,1)S(1)} %get-tuple-element.244), channel_id=1, source_target_pairs={{0,4},{1,5},{2,6},{3,7},{4,0},{5,1},{6,2},{7,3},{8,12},{9,13},{10,... | collective-permute-start | bytes 294920 | tf_op jit(solution)/shard_map/ppermute | solution.py:313
  9.3 8.1 %collective-permute-start.2 = (bf16[48,1024]{1,0:T(8,128)(2,1)S(1)}, bf16[48,1024]{1,0:T(8,128)(2,1)S(1)}, u32[]{:S(2)}, u32[]{:S(2)}) collective-permute-start(bf16[48,1024]{1,0:T(8,128)(2,1)S(1)} %get-tuple-element.239), channel_id=1, source_target_pairs={{0,5},{1,6},{2,7},{3,4},{4,1},{5,2},{6,3},{7,0},{8,13},{9,14},{10,... | collective-permute-start | bytes 294920 | tf_op jit(solution)/shard_map/ppermute | solution.py:313
  17.4 5.8 %collective-permute-start.3 = (bf16[48,1024]{1,0:T(8,128)(2,1)S(1)}, bf16[48,1024]{1,0:T(8,128)(2,1)S(1)}, u32[]{:S(2)}, u32[]{:S(2)}) collective-permute-start(bf16[48,1024]{1,0:T(8,128)(2,1)S(1)} %get-tuple-element.240), channel_id=1, source_target_pairs={{0,1},{1,2},{2,3},{3,0},{4,5},{5,6},{6,7},{7,4},{8,9},{9,10},{10,1... | collective-permute-start | bytes 294920 | tf_op jit(solution)/shard_map/ppermute | solution.py:313
  23.2 7.9 %collective-permute-start.4 = (bf16[48,1024]{1,0:T(8,128)(2,1)S(1)}, bf16[48,1024]{1,0:T(8,128)(2,1)S(1)}, u32[]{:S(2)}, u32[]{:S(2)}) collective-permute-start(bf16[48,1024]{1,0:T(8,128)(2,1)S(1)} %get-tuple-element.241), channel_id=1, source_target_pairs={{0,7},{1,4},{2,5},{3,6},{4,3},{5,0},{6,1},{7,2},{8,15},{9,12},{10,... | collective-permute-start | bytes 294920 | tf_op jit(solution)/shard_map/ppermute | solution.py:313
  23.8 10.1 %collective-permute-start.8 = (bf16[48,1024]{1,0:T(8,128)(2,1)S(1)}, bf16[48,1024]{1,0:T(8,128)(2,1)S(1)}, u32[]{:S(2)}, u32[]{:S(2)}) collective-permute-start(bf16[48,1024]{1,0:T(8,128)(2,1)S(1)} %get-tuple-element.245), channel_id=1, source_target_pairs={{0,2},{1,3},{2,0},{3,1},{4,6},{5,7},{6,4},{7,5},{8,10},{9,11},{10,... | collective-permute-start | bytes 294920 | tf_op jit(solution)/shard_map/ppermute | solution.py:313
  25.7 9.8 %collective-permute-start.10 = (bf16[64,1024]{1,0:T(8,128)(2,1)S(1)}, bf16[64,1024]{1,0:T(8,128)(2,1)S(1)}, u32[]{:S(2)}, u32[]{:S(2)}) collective-permute-start(bf16[64,1024]{1,0:T(8,128)(2,1)S(1)} %shard_map.31.refs_4_), channel_id=1, source_target_pairs={{0,1},{1,2},{2,3},{3,0},{4,5},{5,6},{6,7},{7,4},{8,9},{9,10},{10,1... | collective-permute-start | bytes 393224 | tf_op jit(solution)/shard_map/ppermute | solution.py:313
  27.0 8.5 %collective-permute-start.11 = (bf16[64,1024]{1,0:T(8,128)(2,1)S(1)}, bf16[64,1024]{1,0:T(8,128)(2,1)S(1)}, u32[]{:S(2)}, u32[]{:S(2)}) collective-permute-start(bf16[64,1024]{1,0:T(8,128)(2,1)S(1)} %shard_map.31.refs_4_), channel_id=1, source_target_pairs={{0,2},{1,3},{2,0},{3,1},{4,6},{5,7},{6,4},{7,5},{8,10},{9,11},{10,... | collective-permute-start | bytes 393224 | tf_op jit(solution)/shard_map/ppermute | solution.py:313
  31.1 5.0 %collective-permute-start.12 = (bf16[64,1024]{1,0:T(8,128)(2,1)S(1)}, bf16[64,1024]{1,0:T(8,128)(2,1)S(1)}, u32[]{:S(2)}, u32[]{:S(2)}) collective-permute-start(bf16[64,1024]{1,0:T(8,128)(2,1)S(1)} %shard_map.31.refs_4_), channel_id=1, source_target_pairs={{0,3},{1,0},{2,1},{3,2},{4,7},{5,4},{6,5},{7,6},{8,11},{9,8},{10,9... | collective-permute-start | bytes 393224 | tf_op jit(solution)/shard_map/ppermute | solution.py:313
  31.1 11.8 %collective-permute-start.17 = (bf16[192,1024]{1,0:T(8,128)(2,1)S(1)}, bf16[192,1024]{1,0:T(8,128)(2,1)S(1)}, u32[]{:S(2)}, u32[]{:S(2)}) collective-permute-start(bf16[192,1024]{1,0:T(8,128)(2,1)S(1)} %constant_dynamic-update-slice_fusion.refs_0_.refs_2_.refs_4_), channel_id=1, source_target_pairs={{0,8},{1,9},{2,10},{3,11},{4,12},{5,13},{6,14},{7,15},{8,0},{9,1},... | collective-permute-start | bytes 1179656 | tf_op jit(solution)/shard_map/ppermute | solution.py:313
  33.9 12.0 %collective-permute-start.13 = (bf16[192,1024]{1,0:T(8,128)(2,1)S(1)}, bf16[192,1024]{1,0:T(8,128)(2,1)S(1)}, u32[]{:S(2)}, u32[]{:S(2)}) collective-permute-start(bf16[192,1024]{1,0:T(8,128)(2,1)S(1)} %constant_dynamic-update-slice_fusion.refs_0_.refs_2_.refs_4_), channel_id=1, source_target_pairs={{0,32},{16,48},{32,64},{48,80},{64,96},{80,112},{96,0},{112,16},{1... | collective-permute-start | bytes 1179656 | tf_op jit(solution)/shard_map/ppermute | solution.py:318
  36.7 15.4 %collective-permute-start.18 = (bf16[256,1024]{1,0:T(8,128)(2,1)S(1)}, bf16[256,1024]{1,0:T(8,128)(2,1)S(1)}, u32[]{:S(2)}, u32[]{:S(2)}) collective-permute-start(bf16[256,1024]{1,0:T(8,128)(2,1)S(1)} %shard_map.32.refs_1_.refs_3_.refs_5_), channel_id=1, source_target_pairs={{0,8},{1,9},{2,10},{3,11},{4,12},{5,13},{6,14},{7,15},{8,0},{9,1},... | collective-permute-start | bytes 1572872 | tf_op jit(solution)/shard_map/ppermute | solution.py:313
  39.5 12.6 %collective-permute-start.15 = (bf16[192,1024]{1,0:T(8,128)(2,1)S(1)}, bf16[192,1024]{1,0:T(8,128)(2,1)S(1)}, u32[]{:S(2)}, u32[]{:S(2)}) collective-permute-start(bf16[192,1024]{1,0:T(8,128)(2,1)S(1)} %constant_dynamic-update-slice_fusion.refs_0_.refs_2_.refs_4_), channel_id=1, source_target_pairs={{0,96},{16,112},{32,0},{48,16},{64,32},{80,48},{96,64},{112,80},{1... | collective-permute-start | bytes 1179656 | tf_op jit(solution)/shard_map/ppermute | solution.py:318
  42.5 11.9 %collective-permute-start.14 = (bf16[256,1024]{1,0:T(8,128)(2,1)S(1)}, bf16[256,1024]{1,0:T(8,128)(2,1)S(1)}, u32[]{:S(2)}, u32[]{:S(2)}) collective-permute-start(bf16[256,1024]{1,0:T(8,128)(2,1)S(1)} %shard_map.32.refs_1_.refs_3_.refs_5_), channel_id=1, source_target_pairs={{0,32},{16,48},{32,64},{48,80},{64,96},{80,112},{96,0},{112,16},{1... | collective-permute-start | bytes 1572872 | tf_op jit(solution)/shard_map/ppermute | solution.py:318
  42.9 16.5 %collective-permute-start.16 = (bf16[256,1024]{1,0:T(8,128)(2,1)S(1)}, bf16[256,1024]{1,0:T(8,128)(2,1)S(1)}, u32[]{:S(2)}, u32[]{:S(2)}) collective-permute-start(bf16[256,1024]{1,0:T(8,128)(2,1)S(1)} %shard_map.32.refs_1_.refs_3_.refs_5_), channel_id=1, source_target_pairs={{0,96},{16,112},{32,0},{48,16},{64,32},{80,48},{96,64},{112,80},{1... | collective-permute-start | bytes 1572872 | tf_op jit(solution)/shard_map/ppermute | solution.py:318
  45.9 16.3 %collective-permute-start.22 = (bf16[256,1024]{1,0:T(8,128)(2,1)S(1)}, bf16[256,1024]{1,0:T(8,128)(2,1)S(1)}, u32[]{:S(2)}, u32[]{:S(2)}) collective-permute-start(bf16[256,1024]{1,0:T(8,128)(2,1)S(1)} %shard_map.32.refs_1_.refs_3_.refs_5_), channel_id=1, source_target_pairs={{0,16},{16,0},{32,48},{48,32},{64,80},{80,64},{96,112},{112,96},{1... | collective-permute-start | bytes 1572872 | tf_op jit(solution)/shard_map/ppermute | solution.py:318
  52.1 8.4 %collective-permute-start.21 = (bf16[192,1024]{1,0:T(8,128)(2,1)S(1)}, bf16[192,1024]{1,0:T(8,128)(2,1)S(1)}, u32[]{:S(2)}, u32[]{:S(2)}) collective-permute-start(bf16[192,1024]{1,0:T(8,128)(2,1)S(1)} %constant_dynamic-update-slice_fusion.refs_0_.refs_2_.refs_4_), channel_id=1, source_target_pairs={{0,16},{16,0},{32,48},{48,32},{64,80},{80,64},{96,112},{112,96},{1... | collective-permute-start | bytes 1179656 | tf_op jit(solution)/shard_map/ppermute | solution.py:318
  52.1 15.8 %collective-permute-start.20 = (bf16[256,1024]{1,0:T(8,128)(2,1)S(1)}, bf16[256,1024]{1,0:T(8,128)(2,1)S(1)}, u32[]{:S(2)}, u32[]{:S(2)}) collective-permute-start(bf16[256,1024]{1,0:T(8,128)(2,1)S(1)} %collective-permute-done.18.refs_7_.refs_5_), channel_id=1, source_target_pairs={{0,16},{16,0},{32,48},{48,32},{64,80},{80,64},{96,112},{112,96},{1... | collective-permute-start | bytes 1572872 | tf_op jit(solution)/shard_map/ppermute | solution.py:318
  54.4 11.7 %collective-permute-start.19 = (bf16[192,1024]{1,0:T(8,128)(2,1)S(1)}, bf16[192,1024]{1,0:T(8,128)(2,1)S(1)}, u32[]{:S(2)}, u32[]{:S(2)}) collective-permute-start(bf16[192,1024]{1,0:T(8,128)(2,1)S(1)} %collective-permute-done.17.refs_6_.refs_4_), channel_id=1, source_target_pairs={{0,16},{16,0},{32,48},{48,32},{64,80},{80,64},{96,112},{112,96},{1... | collective-permute-start | bytes 1179656 | tf_op jit(solution)/shard_map/ppermute | solution.py:318
  59.4 12.5 %collective-permute-start.25 = (bf16[96,1024]{1,0:T(8,128)(2,1)S(1)}, bf16[96,1024]{1,0:T(8,128)(2,1)S(1)}, u32[]{:S(2)}, u32[]{:S(2)}) collective-permute-start(bf16[96,1024]{1,0:T(8,128)(2,1)S(1)} %slice.29), channel_id=1, source_target_pairs={{0,32},{16,48},{32,64},{48,80},{64,96},{80,112},{96,0},{112,16},{1... | collective-permute-start | bytes 589832 | tf_op jit(solution)/shard_map/ppermute | solution.py:318
  60.5 14.2 %collective-permute-start.27 = (bf16[128,1024]{1,0:T(8,128)(2,1)S(1)}, bf16[128,1024]{1,0:T(8,128)(2,1)S(1)}, u32[]{:S(2)}, u32[]{:S(2)}) collective-permute-start(bf16[128,1024]{1,0:T(8,128)(2,1)S(1)} %slice.31), channel_id=1, source_target_pairs={{0,32},{16,48},{32,64},{48,80},{64,96},{80,112},{96,0},{112,16},{1... | collective-permute-start | bytes 786440 | tf_op jit(solution)/shard_map/ppermute | solution.py:318
  62.1 12.6 %collective-permute-start.28 = (bf16[128,1024]{1,0:T(8,128)(2,1)S(1)}, bf16[128,1024]{1,0:T(8,128)(2,1)S(1)}, u32[]{:S(2)}, u32[]{:S(2)}) collective-permute-start(bf16[128,1024]{1,0:T(8,128)(2,1)S(1)} %slice.32), channel_id=1, source_target_pairs={{0,96},{16,112},{32,0},{48,16},{64,32},{80,48},{96,64},{112,80},{1... | collective-permute-start | bytes 786440 | tf_op jit(solution)/shard_map/ppermute | solution.py:318
  66.1 8.6 %collective-permute-start.26 = (bf16[96,1024]{1,0:T(8,128)(2,1)S(1)}, bf16[96,1024]{1,0:T(8,128)(2,1)S(1)}, u32[]{:S(2)}, u32[]{:S(2)}) collective-permute-start(bf16[96,1024]{1,0:T(8,128)(2,1)S(1)} %slice.30), channel_id=1, source_target_pairs={{0,96},{16,112},{32,0},{48,16},{64,32},{80,48},{96,64},{112,80},{1... | collective-permute-start | bytes 589832 | tf_op jit(solution)/shard_map/ppermute | solution.py:318
  71.3 7.3 %collective-permute-start.24 = (f32[8,512]{1,0:T(8,128)S(1)}, f32[8,512]{1,0:T(8,128)S(1)}, u32[]{:S(2)}, u32[]{:S(2)}) collective-permute-start(f32[8,512]{1,0:T(8,128)S(1)} %max.30), channel_id=1, source_target_pairs={{0,32},{16,48},{32,64},{48,80},{64,96},{80,112},{96,0},{112,16},{1... | collective-permute-start | bytes 49160 | tf_op jit(solution)/shard_map/ppermute | solution.py:318
  71.9 6.8 %collective-permute-start.23 = (f32[8,512]{1,0:T(8,128)S(1)}, f32[8,512]{1,0:T(8,128)S(1)}, u32[]{:S(2)}, u32[]{:S(2)}) collective-permute-start(f32[8,512]{1,0:T(8,128)S(1)} %max.29), channel_id=1, source_target_pairs={{0,96},{16,112},{32,0},{48,16},{64,32},{80,48},{96,64},{112,80},{1... | collective-permute-start | bytes 49160 | tf_op jit(solution)/shard_map/ppermute | solution.py:318
  77.0 17.6 %copy-start = (s32[384]{0:T(512)S(1)}, s32[384]{0:T(512)}, u32[]{:S(2)}) copy-start(s32[384]{0:T(512)} %ids_ref.1) | copy-start | bytes 4612
  77.0 5.3 %collective-permute-start.29 = (f32[8,512]{1,0:T(8,128)S(1)}, f32[8,512]{1,0:T(8,128)S(1)}, u32[]{:S(2)}, u32[]{:S(2)}) collective-permute-start(f32[8,512]{1,0:T(8,128)S(1)} %shard_map.36), channel_id=1, source_target_pairs={{0,64},{16,80},{32,96},{48,112},{64,0},{80,16},{96,32},{112,48},{1... | collective-permute-start | bytes 49160 | tf_op jit(solution)/shard_map/ppermute | solution.py:318
  82.4 3.8 %collective-permute-start.30 = (f32[8,512]{1,0:T(8,128)S(1)}, f32[8,512]{1,0:T(8,128)S(1)}, u32[]{:S(2)}, u32[]{:S(2)}) collective-permute-start(f32[8,512]{1,0:T(8,128)S(1)} %maximum_maximum_fusion.own_ref), channel_id=1, source_target_pairs={{0,4},{1,5},{2,6},{3,7},{4,0},{5,1},{6,2},{7,3},{8,12},{9,13},{10,... | collective-permute-start | bytes 49160 | tf_op jit(solution)/shard_map/ppermute | solution.py:313
  86.2 3.9 %collective-permute-start.31 = (f32[16,512]{1,0:T(8,128)S(1)}, f32[16,512]{1,0:T(8,128)S(1)}, u32[]{:S(2)}, u32[]{:S(2)}) collective-permute-start(f32[16,512]{1,0:T(8,128)S(1)} %pad_maximum_fusion), channel_id=1, source_target_pairs={{0,3},{1,0},{2,1},{3,2},{4,7},{5,4},{6,5},{7,6},{8,11},{9,8},{10,9... | collective-permute-start | bytes 98312 | tf_op jit(solution)/shard_map/ppermute | solution.py:313
  88.3 5.5 %collective-permute-start.32 = (f32[16,512]{1,0:T(8,128)S(1)}, f32[16,512]{1,0:T(8,128)S(1)}, u32[]{:S(2)}, u32[]{:S(2)}) collective-permute-start(f32[16,512]{1,0:T(8,128)S(1)} %pad_maximum_fusion), channel_id=1, source_target_pairs={{0,2},{1,3},{2,0},{3,1},{4,6},{5,7},{6,4},{7,5},{8,10},{9,11},{10,... | collective-permute-start | bytes 98312 | tf_op jit(solution)/shard_map/ppermute | solution.py:313
  88.3 5.5 %collective-permute-start.33 = (f32[16,512]{1,0:T(8,128)S(1)}, f32[16,512]{1,0:T(8,128)S(1)}, u32[]{:S(2)}, u32[]{:S(2)}) collective-permute-start(f32[16,512]{1,0:T(8,128)S(1)} %pad_maximum_fusion), channel_id=1, source_target_pairs={{0,1},{1,2},{2,3},{3,0},{4,5},{5,6},{6,7},{7,4},{8,9},{9,10},{10,1... | collective-permute-start | bytes 98312 | tf_op jit(solution)/shard_map/ppermute | solution.py:313
  94.7 0.6 copy-start.1

commit v2 on v1

v2 whole, which is shorter than its diff:
```python
import functools
import math

import jax
import jax.numpy as jnp
from jax import lax
from jax.experimental import pallas as pl
from jax.experimental.pallas import tpu as pltpu
from jax.sharding import PartitionSpec as P

KG = 3
CAP = 96
EPSILON = 1e-06

ROWS = 384
OWNERS = 8
CHUNK = 48
LIGHT = 42
MAIN = OWNERS * CHUNK
EXTRA = 64
BLOCK = MAIN + EXTRA
LANES = 512
LOW = -1e30

STEPS = ((1, 0), (0, 1), (0, 3), (1, 1), (1, 3), (1, 2), (0, 2))

VMEM = pl.BlockSpec(memory_space=pltpu.VMEM)
PARAMS = pltpu.CompilerParams(vmem_limit_bytes=48 * 1024 * 1024)


def inverse_norms(block):
    values = block.astype(jnp.float32)
    return lax.rsqrt(jnp.sum(values * values, axis=1) + EPSILON)


def tile_max(left_rows, left_ids, left_inverse, right_rows, right_ids, right_inverse, left_first, right_first):
    scores = lax.dot_general(
        left_rows, right_rows, (((1,), (1,)), ((), ())), preferred_element_type=jnp.float32
    )
    scaled = scores * left_inverse[:, None] * right_inverse[None, :]
    left_index = left_first + jnp.arange(left_rows.shape[0], dtype=jnp.int32)
    right_index = right_first + jnp.arange(right_rows.shape[0], dtype=jnp.int32)
    same_cluster = (
        (left_ids[:, None] == right_ids[None, :])
        & (left_ids[:, None] >= 0)
        & (left_index[:, None] != right_index[None, :])
    )
    masked = jnp.where(same_cluster, scaled, jnp.float32(-1.0))
    return jnp.max(masked, axis=1)


def general(embeddings, cluster_ids):
    groups_count = lax.axis_size("grp")
    feature_count = embeddings.shape[1]
    destination = cluster_ids // KG
    onehot = (destination[:, None] == jnp.arange(groups_count, dtype=jnp.int32)[None, :]).astype(jnp.int32)
    earlier = jnp.cumsum(onehot, axis=0) - onehot
    slot_index = jnp.sum(earlier * onehot, axis=1)
    position = destination * CAP + slot_index
    send_rows = jnp.zeros((groups_count * CAP, feature_count), jnp.bfloat16).at[position].set(embeddings)
    send_ids = (
        jnp.full((groups_count * CAP,), -1.0, jnp.bfloat16).at[position].set(cluster_ids.astype(jnp.bfloat16))
    )
    own_rows = lax.all_to_all(send_rows, "grp", split_axis=0, concat_axis=0, tiled=True)
    own_ids = lax.all_to_all(send_ids, "grp", split_axis=0, concat_axis=0, tiled=True)
    own_count = own_rows.shape[0]
    own_inverse = inverse_norms(own_rows)
    sub_count = lax.axis_size("sub")
    own_sub = lax.axis_index("sub")
    ring = [(index, (index + 1) % sub_count) for index in range(sub_count)]

    def one_block(index, state):
        right_rows, right_ids, current = state
        row_max = tile_max(
            own_rows,
            own_ids,
            own_inverse,
            right_rows,
            right_ids,
            inverse_norms(right_rows),
            own_sub * own_count,
            ((own_sub - index) % sub_count) * own_count,
        )
        next_rows = lax.ppermute(right_rows, "sub", ring)
        next_ids = lax.ppermute(right_ids, "sub", ring)
        return next_rows, next_ids, jnp.maximum(current, row_max)

    start = (own_rows, own_ids, jnp.full((own_count,), -1.0, jnp.float32))
    best_seen = lax.fori_loop(0, sub_count, one_block, start)[2]
    gathered_back = lax.all_to_all(best_seen, "grp", split_axis=0, concat_axis=0, tiled=True)
    return jnp.take(gathered_back, position, axis=0)


def iota(shape, dim):
    return lax.broadcasted_iota(jnp.int32, shape, dim)


def dot_nt(left, right):
    return lax.dot_general(left, right, (((1,), (1,)), ((), ())), preferred_element_type=jnp.float32)


def dot_nn(left, right):
    return lax.dot_general(left, right, (((1,), (0,)), ((), ())), preferred_element_type=jnp.float32)


def three_parts(value):
    high = value.astype(jnp.bfloat16).astype(jnp.float32)
    rest = value - high
    middle = rest.astype(jnp.bfloat16).astype(jnp.float32)
    low = (rest - middle).astype(jnp.bfloat16).astype(jnp.float32)
    return high, middle, low


def as_bf16(mask):
    return jnp.where(mask, 1.0, 0.0).astype(jnp.bfloat16)


def owner_at(place_ref, dx, dz):
    return ((place_ref[0] + dx) % 2) * 4 + (place_ref[1] + dz) % 4


def sort_kernel(at_ref, ids_ref, rows_ref, *out_refs):
    chunk_refs, extra_ref, known_ref = out_refs[:OWNERS], out_refs[OWNERS], out_refs[OWNERS + 1]
    ids = ids_ref[...].reshape(1, ROWS)
    group_of = iota((OWNERS, ROWS), 0)
    member = (ids >= group_of * KG) & (ids < group_of * KG + KG)
    member_f = jnp.where(member, 1.0, 0.0)
    before = as_bf16(iota((ROWS, ROWS), 0) < iota((ROWS, ROWS), 1))
    ranks = dot_nn(member_f.astype(jnp.bfloat16), before)
    rank = jnp.sum(member_f * ranks, axis=0, keepdims=True)
    group = jnp.sum(member_f * group_of.astype(jnp.float32), axis=0, keepdims=True)
    count = jnp.sum(member_f, axis=1, keepdims=True)
    most = jnp.where(count > 64.0, 1.0, 0.0)
    home = jnp.sum(most * iota((OWNERS, 1), 0).astype(jnp.float32), axis=0, keepdims=True)
    values = rows_ref[...].astype(jnp.float32)
    inverse_column = lax.rsqrt(jnp.sum(values * values, axis=1, keepdims=True) + EPSILON)
    diagonal = iota((ROWS, ROWS), 0) == iota((ROWS, ROWS), 1)
    inverse = jnp.sum(jnp.where(diagonal, inverse_column, 0.0), axis=0, keepdims=True)
    high, middle, low = three_parts(inverse)
    line = iota((16, ROWS), 0)
    told = jnp.where(line == 10, ids.astype(jnp.float32) + 1.0, 0.0)
    told = jnp.where(line == 11, high, told)
    told = jnp.where(line == 12, middle, told)
    told = jnp.where(line == 13, low, told)
    rest = (group == home) & (rank >= float(LIGHT))
    lane = jnp.where(rest, rank + float(MAIN - LIGHT), -1.0)
    tolds = []
    for slot, (dx, dz) in enumerate(((0, 0), *STEPS)):
        goes = (group == owner_at(at_ref, dx, dz).astype(jnp.float32)) & (rank < float(LIGHT))
        lane = jnp.where(goes, rank + float(slot * CHUNK), lane)
        tolds.append(jnp.where(goes, told, 0.0))
    tolds.append(jnp.where(rest, told, 0.0))
    known_ref[...] = jnp.where(line == 0, lane, group)[0:8]
    pick = as_bf16(iota((LANES, ROWS), 0) == lane.astype(jnp.int32))
    data = dot_nn(pick, rows_ref[...])
    placed = dot_nt(jnp.concatenate(tolds, axis=0).astype(jnp.bfloat16), pick)
    for slot, ref in enumerate(chunk_refs):
        first = slot * CHUNK
        ref[0:32, :] = data[first : first + 32].astype(jnp.bfloat16)
        tail = data[first + 32 : first + CHUNK]
        ref[32:CHUNK, :] = tail.astype(jnp.bfloat16)
        ref[32:CHUNK, 0:MAIN] = (tail[:, 0:MAIN] + placed[16 * slot : 16 * slot + 16, 0:MAIN]).astype(jnp.bfloat16)
    extra_ref[0:48, :] = data[MAIN : MAIN + 48].astype(jnp.bfloat16)
    tail = data[MAIN + 48 : BLOCK]
    tail = jnp.where(iota(tail.shape, 0) == 15, home + 1.0, tail)
    extra_ref[48:EXTRA, :] = tail.astype(jnp.bfloat16)
    extra_ref[48:EXTRA, 0:128] = (
        tail[:, 0:128] + placed[16 * OWNERS : 16 * OWNERS + 16, MAIN:LANES]
    ).astype(jnp.bfloat16)


def marked(ref):
    return ref[EXTRA - 16 : EXTRA, :].astype(jnp.float32)[15:16, 0:1]


def half_kernel(at_ref, own_ref, other_ref, out_ref):
    parity = at_ref[0] % 2
    own_fits = jnp.where(marked(own_ref) >= 5.0, 1, 0) == parity
    other_fits = jnp.where(marked(other_ref) >= 5.0, 1, 0) == parity
    taken = jnp.where(own_fits, own_ref[...], other_ref[...])
    out_ref[0 : EXTRA - 16, :] = taken[0 : EXTRA - 16]
    tail = taken[EXTRA - 16 : EXTRA].astype(jnp.float32)
    clash = (iota(tail.shape, 0) == 15) & (own_fits == other_fits)
    out_ref[EXTRA - 16 : EXTRA, :] = jnp.where(clash, 0.0, tail).astype(jnp.bfloat16)


def block_kernel(at_ref, *refs):
    chunks, extras, out_ref = refs[0:8], refs[8:12], refs[12]
    for slot, chunk_ref in enumerate(chunks):
        out_ref[slot * CHUNK : (slot + 1) * CHUNK, :] = chunk_ref[...]
    wanted = owner_at(at_ref, 0, 0).astype(jnp.float32) + 1.0
    found = jnp.zeros((1, 1), jnp.float32)
    held = jnp.ones((1, 1), jnp.float32)
    taken = extras[0][...]
    for index in range(4):
        mark = marked(extras[index])
        found = found + jnp.where(mark == wanted, 1.0, 0.0)
        held = jnp.where(mark == 0.0, 0.0, held)
        if index > 0:
            taken = jnp.where(mark == wanted, extras[index][...], taken)
    good = jnp.where((found == 1.0) & (held == 1.0), 1.0, 0.0)
    out_ref[MAIN : BLOCK - 16, :] = taken[0 : EXTRA - 16]
    tail = taken[EXTRA - 16 : EXTRA].astype(jnp.float32)
    out_ref[BLOCK - 16 : BLOCK, :] = jnp.where(iota(tail.shape, 0) == 14, good, tail).astype(jnp.bfloat16)


def told_of(ref):
    total = jnp.zeros((16, MAIN), jnp.float32)
    for index in range(1, OWNERS + 1):
        total = total + ref[index * CHUNK - 16 : index * CHUNK, 0:MAIN].astype(jnp.float32)
    end = ref[BLOCK - 16 : BLOCK, 0:128].astype(jnp.float32)
    total = jnp.concatenate([total, end], axis=1)[:, 0:BLOCK]
    return total[10:11], total[11:12] + total[12:13] + total[13:14], end[14:15, 0:1]


def column_of(row):
    count = row.shape[1]
    diagonal = iota((count, count), 0) == iota((count, count), 1)
    return jnp.sum(jnp.where(diagonal, row, 0.0), axis=1, keepdims=True)


def match_kernel(left_count, right_count, own, checked, *refs):
    blocks, out_refs = refs[: left_count + right_count], refs[left_count + right_count :]
    told = [told_of(ref) for ref in blocks]
    best = [jnp.full((1, BLOCK), LOW, jnp.float32)] * left_count
    for right in range(left_count, left_count + right_count):
        ids, inverse = column_of(told[right][0]), column_of(told[right][1])
        rows = blocks[right][...]
        for left in range(left_count):
            scores = dot_nt(rows, blocks[left][...]) * inverse
            alike = ids == told[left][0]
            if own and left == 0 and right == left_count:
                alike = alike & (iota(scores.shape, 0) != iota(scores.shape, 1))
            best[left] = jnp.maximum(best[left], jnp.max(jnp.where(alike, scores, LOW), axis=0, keepdims=True))
    for left in range(left_count):
        out_refs[left][...] = jnp.full(out_refs[left].shape, -1.0, jnp.float32)
        out_refs[left][0:1, 0:BLOCK] = jnp.maximum(best[left] * told[left][1], -1.0)
    if checked:
        good = jnp.minimum(told[0][2], told[left_count][2])
        out_refs[0][1:2, :] = jnp.broadcast_to(good, (1, LANES))


def far_kernel(upper_ref, lower_ref, *refs):
    rights, out_ref, left = refs[0:4], refs[4], refs[5]
    left[0 : BLOCK // 2, :] = upper_ref[...]
    left[BLOCK // 2 : BLOCK, :] = lower_ref[...]
    match_kernel(1, 4, False, False, left, *rights, out_ref)


def final_kernel(at_ref, own_ref, side_ref, z1_ref, z2_ref, z3_ref, known_ref, out_ref, ok_ref):
    sources = {1: z1_ref, 2: z2_ref, 3: z3_ref}
    vectors, groups, good = [], [], jnp.ones((1, LANES), jnp.float32)
    for dx, dz in ((0, 0), *STEPS):
        ref, row = (side_ref if dx else own_ref, 0) if dz == 0 else (sources[dz], 8 * dx)
        vectors.append(ref[row : row + 1, :])
        groups.append(owner_at(at_ref, dx, dz).astype(jnp.float32))
        good = jnp.minimum(good, ref[row + 1 : row + 2, :])
    parts = three_parts(jnp.concatenate(vectors, axis=0))
    pick = as_bf16(iota((LANES, ROWS), 0) == known_ref[0:1, :].astype(jnp.int32))
    picked = dot_nn(jnp.concatenate(parts, axis=0).astype(jnp.bfloat16), pick)
    picked = picked[0:8] + picked[8:16] + picked[16:24]
    total = jnp.zeros((1, ROWS), jnp.float32)
    for index, group in enumerate(groups):
        total = jnp.where(known_ref[1:2, :] == group, picked[index : index + 1], total)
    out_ref[...] = total.reshape(ROWS)
    ok_ref[...] = jnp.where(good[:, 0:128] == 1.0, 1, 0)


SMEM = pl.BlockSpec(memory_space=pltpu.SMEM)


def call(kernel, outs, *args, scalars=0, scratch=(), flops=0):
    read = sum(math.prod(a.shape) * a.dtype.itemsize for a in args)
    return pl.pallas_call(
        kernel,
        out_shape=outs,
        in_specs=[SMEM] * scalars + [VMEM] * (len(args) - scalars),
        out_specs=[VMEM] * len(outs) if isinstance(outs, list) else VMEM,
        scratch_shapes=list(scratch),
        compiler_params=PARAMS,
        cost_estimate=pl.CostEstimate(flops=flops, bytes_accessed=read, transcendentals=0),
    )(*args)


def along_sub(value, to_x, to_z):
    perm = [(4 * x + z, 4 * to_x(x) + to_z(z)) for x in range(4) for z in range(4)]
    return lax.ppermute(value, "sub", perm)


def along_grp(value, to_y, to_core):
    perm = [(2 * y + c, 2 * to_y(y) + to_core(c)) for y in range(4) for c in range(2)]
    return lax.ppermute(value, "grp", perm)


def after(value, other):
    return lax.optimization_barrier((value, other))[0]


def same(index):
    return index


def shift(amount):
    return lambda index: (index + amount) % 4


def flip(amount):
    return lambda index: index ^ amount


def local(embeddings, cluster_ids):
    f32, bf16 = jnp.float32, jnp.bfloat16
    width = embeddings.shape[1]
    shape = jax.ShapeDtypeStruct
    sub = lax.axis_index("sub")
    at = jnp.stack([sub // 4, sub % 4]).astype(jnp.int32)
    *chunks, extra, known = call(
        sort_kernel,
        [shape((CHUNK, width), bf16)] * OWNERS + [shape((EXTRA, width), bf16), shape((8, ROWS), f32)],
        at,
        cluster_ids,
        embeddings,
        scalars=1,
        flops=500_000_000,
    )
    other_extra = along_sub(extra, flip(1), same)
    got = [chunks[0]]
    for slot, (dx, dz) in enumerate(STEPS, 1):
        chunk = chunks[slot]
        if slot > 3:
            chunk = after(chunk, other_extra if slot == 4 else got[slot - 4])
        got.append(along_sub(chunk, flip(dx), shift(dz)))
    extra = call(half_kernel, shape((EXTRA, width), bf16), at, extra, other_extra, scalars=1)
    extras = [extra] + [along_sub(extra, same, shift(dz)) for dz in (1, 2, 3)]
    block = call(block_kernel, shape((BLOCK, width), bf16), at, *got, *extras, scalars=1)
    half = BLOCK // 2
    below = along_grp(block, shift(1), same)
    above = along_grp(block, shift(-1), same)
    across = along_sub(block, shift(2), same)
    sibling = along_grp(block, same, flip(1))
    far = (along_grp(below[:half], shift(1), same), along_grp(above[half:], shift(-1), same))
    across_sibling = along_grp(across, same, flip(1))

    flops = 2 * BLOCK * BLOCK * width
    vector = shape((8, LANES), f32)

    def match(lefts, rights, own=False, checked=False):
        counts = len(lefts), len(rights)
        kernel = functools.partial(match_kernel, *counts, own, checked)
        return call(kernel, [vector] * counts[0], *lefts, *rights, flops=flops * counts[0] * counts[1])

    near, others = (block, sibling), (across, across_sibling)
    best_near, below_near, above_near = match((block, below, above), near, own=True)
    best, below_other, above_other = match((block, below, above), others, checked=True)
    from_above = along_grp(jnp.maximum(below_near, below_other), shift(-1), same)
    from_below = along_grp(jnp.maximum(above_near, above_other), shift(1), same)
    best_far = call(
        far_kernel,
        vector,
        *far,
        *near,
        *others,
        scratch=[pltpu.VMEM((BLOCK, width), bf16)],
        flops=4 * flops,
    )
    from_far = along_grp(best_far, shift(2), same)
    best = jnp.maximum(jnp.maximum(best, best_near), jnp.maximum(from_above, from_below))
    best = jnp.maximum(best, from_far)
    side = along_sub(best, flip(1), same)
    both = jnp.concatenate([best, side], axis=0)
    pulled = [along_sub(both, same, shift(-dz)) for dz in (1, 2, 3)]
    out, ok = call(
        final_kernel,
        [shape((ROWS,), f32), shape((1, 128), jnp.int32)],
        at,
        best,
        side,
        *pulled,
        known,
        scalars=1,
    )
    return lax.cond(ok[0, 0] == 1, lambda e, c, o: o, lambda e, c, o: general(e, c), embeddings, cluster_ids, out)


def solution(mesh):
    return jax.shard_map(
        local,
        mesh=mesh,
        in_specs=(P(("grp", "sub"), None), P(("grp", "sub"))),
        out_specs=P(("grp", "sub")),
        check_vma=False,
    )
```

time: 95.4 us -> 84.6 us (0.89)
  waiting for transfers between devices: 38.4 us -> 31.2 us
  starting transfers between devices: 42.4 us -> 39.8 us
    ppermute x15 -> x9, waiting for transfers between devices: 16.7 us -> 3.93 us  [along_grp(): return lax.ppermute(value, 'grp', perm)]
    ppermute x17 -> x16, waiting for transfers between devices: 21.7 us -> 27.3 us  [along_sub(): return lax.ppermute(value, 'sub', perm)]
    ppermute x15 -> x9, starting transfers between devices: 17.9 us -> 13 us  [along_grp(): return lax.ppermute(value, 'grp', perm)]
    ppermute x17 -> x16, starting transfers between devices: 24.5 us -> 26.8 us  [along_sub(): return lax.ppermute(value, 'sub', perm)]
    pallas_call x8 -> x7, Pallas kernels: 13.4 us -> 12.5 us  [call(): pl.pallas_call(kernel, out_shape=outs, in_specs=[SMEM] * scalars + [VMEM]...]
  transfers between devices with their start and end apart: 32 -> 25, of which waited for: 11 -> 11; matrix products, arithmetic and copies ran while one was open for 0% -> 0% of each run, Pallas kernels for 11% -> 11%
where the time goes in v2:
time: 84.6 us; the launch traced here: 84.5 us
  starting transfers between devices  39.8 us (47%)
  waiting for transfers between devices  31.2 us (37%)
  Pallas kernels  12.5 us (15%)
    ppermute x16, waiting for transfers between devices, along_sub(): return lax.ppermute(value, 'sub', perm)  27.3 us
    ppermute x16, starting transfers between devices, along_sub(): return lax.ppermute(value, 'sub', perm)  26.8 us
    ppermute x9, starting transfers between devices, along_grp(): return lax.ppermute(value, 'grp', perm)  13 us
    pallas_call x7, Pallas kernels, call(): pl.pallas_call(kernel, out_shape=outs, in_specs=[SMEM] * scalars + [VMEM]...  12.5 us
    ppermute x9, waiting for transfers between devices, along_grp(): return lax.ppermute(value, 'grp', perm)  3.93 us
  transfers between devices with their start and end apart: 25, of which 11 were waited for; matrix products, arithmetic and copies ran while one was open for 0% of the time, Pallas kernels for 11%

profile of v2, /device:TPU:0, one launch (start us, length us, event | category | flops | bytes accessed | tf_op | source)
XLA Modules:
  0.0 84.5 jit_solution(15147278060806302402)
XLA Ops:
  0.0 0.1 pad_add_fusion.at_ref
  0.1 2.1 %shard_map.30 = (bf16[48,1024]{1,0:T(8,128)(2,1)S(1)}, bf16[48,1024]{1,0:T(8,128)(2,1)S(1)}, bf16[48,1024]{1,0:T(8,128)(2,1)S(1)}, bf16[48,1024]{1,0:T(8,128)(2,...) custom-call(s32[2]{0:T(128)S(1)} %pad_add_fusion.at_ref, ...), custom_call_target="tpu_custom_call" | custom-call | flops 500000000 | bytes 787976 | tf_op jit(solution)/shard_map/pallas_call | solution.py:274
  2.2 4.2 %collective-permute-start.4 = (bf16[48,1024]{1,0:T(8,128)(2,1)S(1)}, bf16[48,1024]{1,0:T(8,128)(2,1)S(1)}, u32[]{:S(2)}, u32[]{:S(2)}) collective-permute-start(bf16[48,1024]{1,0:T(8,128)(2,1)S(1)} %get-tuple-element.245), channel_id=1, source_target_pairs={{0,3},{1,0},{2,1},{3,2},{4,7},{5,4},{6,5},{7,6},{8,11},{9,8},{10,9... | collective-permute-start | bytes 294920 | tf_op jit(solution)/shard_map/ppermute | solution.py:287
  6.4 0.0 collective-permute-start.3
  6.4 1.5 %collective-permute-start.5 = (bf16[64,1024]{1,0:T(8,128)(2,1)S(1)}, bf16[64,1024]{1,0:T(8,128)(2,1)S(1)}, u32[]{:S(2)}, u32[]{:S(2)}) collective-permute-start(bf16[64,1024]{1,0:T(8,128)(2,1)S(1)} %get-tuple-element.247.own_ref), channel_id=1, source_target_pairs={{0,4},{1,5},{2,6},{3,7},{4,0},{5,1},{6,2},{7,3},{8,12},{9,13},{10,... | collective-permute-start | bytes 393224 | tf_op jit(solution)/shard_map/ppermute | solution.py:287
  7.9 0.5 collective-permute-start.2
  8.4 0.2 collective-permute-done.4.refs_3_
  8.6 2.2 %collective-permute-start.9 = (bf16[48,1024]{1,0:T(8,128)(2,1)S(1)}, bf16[48,1024]{1,0:T(8,128)(2,1)S(1)}, u32[]{:S(2)}, u32[]{:S(2)}) collective-permute-start(bf16[48,1024]{1,0:T(8,128)(2,1)S(1)} %get-tuple-element.254), channel_id=1, source_target_pairs={{0,2},{1,3},{2,0},{3,1},{4,6},{5,7},{6,4},{7,5},{8,10},{9,11},{10,... | collective-permute-start | bytes 294920 | tf_op jit(solution)/shard_map/ppermute | solution.py:287
  10.8 2.4 %collective-permute-done.3.refs_2_ = bf16[48,1024]{1,0:T(8,128)(2,1)S(1)} collective-permute-done((bf16[48,1024]{1,0:T(8,128)(2,1)S(1)}, bf16[48,1024]{1,0:T(8,128)(2,1)S(1)}, u32[]{:S(2)}, u32[]{:S(2)}) %collective-permute-start.3) | collective-permute-done | bytes 98336 | tf_op jit(solution)/shard_map/ppermute | solution.py:287
  13.3 0.0 collective-permute-start.8
  13.3 0.0 collective-permute-done.5.other_ref
  13.3 0.6 shard_map.31.refs_8_
  13.9 1.4 %collective-permute-start.10 = (bf16[64,1024]{1,0:T(8,128)(2,1)S(1)}, bf16[64,1024]{1,0:T(8,128)(2,1)S(1)}, u32[]{:S(2)}, u32[]{:S(2)}) collective-permute-start(bf16[64,1024]{1,0:T(8,128)(2,1)S(1)} %shard_map.31.refs_8_), channel_id=1, source_target_pairs={{0,1},{1,2},{2,3},{3,0},{4,5},{5,6},{6,7},{7,4},{8,9},{9,10},{10,1... | collective-permute-start | bytes 393224 | tf_op jit(solution)/shard_map/ppermute | solution.py:287
  15.3 3.5 %collective-permute-start.11 = (bf16[64,1024]{1,0:T(8,128)(2,1)S(1)}, bf16[64,1024]{1,0:T(8,128)(2,1)S(1)}, u32[]{:S(2)}, u32[]{:S(2)}) collective-permute-start(bf16[64,1024]{1,0:T(8,128)(2,1)S(1)} %shard_map.31.refs_8_), channel_id=1, source_target_pairs={{0,2},{1,3},{2,0},{3,1},{4,6},{5,7},{6,4},{7,5},{8,10},{9,11},{10,... | collective-permute-start | bytes 393224 | tf_op jit(solution)/shard_map/ppermute | solution.py:287
  18.8 0.0 collective-permute-done.2.refs_1_
  18.8 2.2 %collective-permute-start.12 = (bf16[64,1024]{1,0:T(8,128)(2,1)S(1)}, bf16[64,1024]{1,0:T(8,128)(2,1)S(1)}, u32[]{:S(2)}, u32[]{:S(2)}) collective-permute-start(bf16[64,1024]{1,0:T(8,128)(2,1)S(1)} %shard_map.31.refs_8_), channel_id=1, source_target_pairs={{0,3},{1,0},{2,1},{3,2},{4,7},{5,4},{6,5},{7,6},{8,11},{9,8},{10,9... | collective-permute-start | bytes 393224 | tf_op jit(solution)/shard_map/ppermute | solution.py:287
  21.0 0.0 collective-permute-done.9.refs_7_
  21.0 0.1 collective-permute-start.7
  21.1 0.0 collective-permute-done.8.refs_6_
  21.1 2.9 %collective-permute-start.6 = (bf16[48,1024]{1,0:T(8,128)(2,1)S(1)}, bf16[48,1024]{1,0:T(8,128)(2,1)S(1)}, u32[]{:S(2)}, u32[]{:S(2)}) collective-permute-start(bf16[48,1024]{1,0:T(8,128)(2,1)S(1)} %get-tuple-element.248), channel_id=1, source_target_pairs={{0,5},{1,6},{2,7},{3,4},{4,1},{5,2},{6,3},{7,0},{8,13},{9,14},{10,... | collective-permute-start | bytes 294920 | tf_op jit(solution)/shard_map/ppermute | solution.py:287
  24.0 2.6 %collective-permute-done.7.refs_5_ = bf16[48,1024]{1,0:T(8,128)(2,1)S(1)} collective-permute-done((bf16[48,1024]{1,0:T(8,128)(2,1)S(1)}, bf16[48,1024]{1,0:T(8,128)(2,1)S(1)}, u32[]{:S(2)}, u32[]{:S(2)}) %collective-permute-start.7) | collective-permute-done | bytes 98336 | tf_op jit(solution)/shard_map/ppermute | solution.py:287
  26.5 1.3 %collective-permute-done.6.refs_4_ = bf16[48,1024]{1,0:T(8,128)(2,1)S(1)} collective-permute-done((bf16[48,1024]{1,0:T(8,128)(2,1)S(1)}, bf16[48,1024]{1,0:T(8,128)(2,1)S(1)}, u32[]{:S(2)}, u32[]{:S(2)}) %collective-permute-start.6) | collective-permute-done | bytes 98336 | tf_op jit(solution)/shard_map/ppermute | solution.py:287
  27.8 0.0 collective-permute-done.10.refs_9_
  27.8 0.0 collective-permute-done.11.refs_10_
  27.8 0.0 collective-permute-done.12.refs_11_
  27.8 0.7 shard_map.32.refs_0_.refs_3_
  28.5 3.6 %collective-permute-start.15 = (bf16[448,1024]{1,0:T(8,128)(2,1)S(1)}, bf16[448,1024]{1,0:T(8,128)(2,1)S(1)}, u32[]{:S(2)}, u32[]{:S(2)}) collective-permute-start(bf16[448,1024]{1,0:T(8,128)(2,1)S(1)} %shard_map.32.refs_0_.refs_3_), channel_id=1, source_target_pairs={{0,8},{1,9},{2,10},{3,11},{4,12},{5,13},{6,14},{7,15},{8,0},{9,1},... | collective-permute-start | bytes 2752520 | tf_op jit(solution)/shard_map/ppermute | solution.py:287
  32.1 1.6 %collective-permute-start.13 = (bf16[448,1024]{1,0:T(8,128)(2,1)S(1)}, bf16[448,1024]{1,0:T(8,128)(2,1)S(1)}, u32[]{:S(2)}, u32[]{:S(2)}) collective-permute-start(bf16[448,1024]{1,0:T(8,128)(2,1)S(1)} %shard_map.32.refs_0_.refs_3_), channel_id=1, source_target_pairs={{0,32},{16,48},{32,64},{48,80},{64,96},{80,112},{96,0},{112,16},{1... | collective-permute-start | bytes 2752520 | tf_op jit(solution)/shard_map/ppermute | solution.py:292
  33.7 1.6 %collective-permute-start.14 = (bf16[448,1024]{1,0:T(8,128)(2,1)S(1)}, bf16[448,1024]{1,0:T(8,128)(2,1)S(1)}, u32[]{:S(2)}, u32[]{:S(2)}) collective-permute-start(bf16[448,1024]{1,0:T(8,128)(2,1)S(1)} %shard_map.32.refs_0_.refs_3_), channel_id=1, source_target_pairs={{0,96},{16,112},{32,0},{48,16},{64,32},{80,48},{96,64},{112,80},{1... | collective-permute-start | bytes 2752520 | tf_op jit(solution)/shard_map/ppermute | solution.py:292
  35.3 0.0 collective-permute-start.17
  35.3 13.6 %collective-permute-done.15.refs_3_.refs_2_ = bf16[448,1024]{1,0:T(8,128)(2,1)S(1)} collective-permute-done((bf16[448,1024]{1,0:T(8,128)(2,1)S(1)}, bf16[448,1024]{1,0:T(8,128)(2,1)S(1)}, u32[]{:S(2)}, u32[]{:S(2)}) %collective-permute-start.15) | collective-permute-done | bytes 917536 | tf_op jit(solution)/shard_map/ppermute | solution.py:287
  48.9 0.0 collective-permute-start.16
  48.9 1.3 %collective-permute-done.13.refs_1_ = bf16[448,1024]{1,0:T(8,128)(2,1)S(1)} collective-permute-done((bf16[448,1024]{1,0:T(8,128)(2,1)S(1)}, bf16[448,1024]{1,0:T(8,128)(2,1)S(1)}, u32[]{:S(2)}, u32[]{:S(2)}) %collective-permute-start.13) | collective-permute-done | bytes 917536 | tf_op jit(solution)/shard_map/ppermute | solution.py:292
  50.2 0.4 collective-permute-start.20
  50.6 0.0 collective-permute-done.14.refs_2_
  50.7 3.2 %collective-permute-start.21 = (bf16[224,1024]{1,0:T(8,128)(2,1)S(1)}, bf16[224,1024]{1,0:T(8,128)(2,1)S(1)}, u32[]{:S(2)}, u32[]{:S(2)}) collective-permute-start(bf16[224,1024]{1,0:T(8,128)(2,1)S(1)} %slice.22), channel_id=1, source_target_pairs={{0,96},{16,112},{32,0},{48,16},{64,32},{80,48},{96,64},{112,80},{1... | collective-permute-start | bytes 1376264 | tf_op jit(solution)/shard_map/ppermute | solution.py:292
  53.8 0.0 collective-permute-done.17.refs_4_.refs_1_
  53.8 3.1 %shard_map.34 = (f32[8,512]{1,0:T(8,128)S(1)}, f32[8,512]{1,0:T(8,128)S(1)}, f32[8,512]{1,0:T(8,128)S(1)}) custom-call(bf16[448,1024]{1,0:T(8,128)(2,1)S(1)} %shard_map.32.refs_0_.refs_3_, bf16[448,1024]{1,0:T(8,128)(2,1)S(1)} %collective-permute-done.13.refs_1_, bf16[448,1024]{1,0:T(8,128)(2,1)S(1)} %collective-permute-done.14.refs_2_, ...), custom_call_target="tpu_custom_call" | custom-call | flops 2466250752 | bytes 4587520 | tf_op jit(solution)/shard_map/pallas_call | solution.py:274
  57.0 0.0 collective-permute-done.16.refs_4_.refs_3_
  57.0 3.1 %shard_map.33 = (f32[8,512]{1,0:T(8,128)S(1)}, f32[8,512]{1,0:T(8,128)S(1)}, f32[8,512]{1,0:T(8,128)S(1)}) custom-call(bf16[448,1024]{1,0:T(8,128)(2,1)S(1)} %shard_map.32.refs_0_.refs_3_, bf16[448,1024]{1,0:T(8,128)(2,1)S(1)} %collective-permute-done.13.refs_1_, bf16[448,1024]{1,0:T(8,128)(2,1)S(1)} %collective-permute-done.14.refs_2_, ...), custom_call_target="tpu_custom_call" | custom-call | flops 2466250752 | bytes 4587520 | tf_op jit(solution)/shard_map/pallas_call | solution.py:274
  60.1 0.1 collective-permute-start.19
  60.2 0.0 copy-start
  60.2 3.2 %collective-permute-start.18 = (f32[8,512]{1,0:T(8,128)S(1)}, f32[8,512]{1,0:T(8,128)S(1)}, u32[]{:S(2)}, u32[]{:S(2)}) collective-permute-start(f32[8,512]{1,0:T(8,128)S(1)} %max.29), channel_id=1, source_target_pairs={{0,96},{16,112},{32,0},{48,16},{64,32},{80,48},{96,64},{112,80},{1... | collective-permute-start | bytes 49160 | tf_op jit(solution)/shard_map/ppermute | solution.py:292
  63.4 0.0 collective-permute-done.20.upper_ref
  63.4 0.3 collective-permute-done.21.lower_ref
  63.7 2.2 %shard_map.35 = f32[8,512]{1,0:T(8,128)S(1)} custom-call(bf16[224,1024]{1,0:T(8,128)(2,1)S(1)} %collective-permute-done.20.upper_ref, bf16[224,1024]{1,0:T(8,128)(2,1)S(1)} %collective-permute-done.21.lower_ref, bf16[448,1024]{1,0:T(8,128)(2,1)S(1)} %shard_map.32.refs_0_.refs_3_, bf16[448,1024]{1,0:T(8,128)(2,1)S(1)} %collective-permute-done.17.refs_4_.refs_1_, ...), custom_call_target="tpu_custom_call" | custom-call | flops 1644167168 | bytes 4587520 | tf_op jit(solution)/shard_map/pallas_call | solution.py:274
  65.9 3.0 %collective-permute-start.22 = (f32[8,512]{1,0:T(8,128)S(1)}, f32[8,512]{1,0:T(8,128)S(1)}, u32[]{:S(2)}, u32[]{:S(2)}) collective-permute-start(f32[8,512]{1,0:T(8,128)S(1)} %shard_map.35), channel_id=1, source_target_pairs={{0,64},{16,80},{32,96},{48,112},{64,0},{80,16},{96,32},{112,48},{1... | collective-permute-start | bytes 49160 | tf_op jit(solution)/shard_map/ppermute | solution.py:292
  68.9 0.0 collective-permute-done.19
  68.9 0.0 collective-permute-done.18
  68.9 2.3 %collective-permute-done.22 = f32[8,512]{1,0:T(8,128)S(1)} collective-permute-done((f32[8,512]{1,0:T(8,128)S(1)}, f32[8,512]{1,0:T(8,128)S(1)}, u32[]{:S(2)}, u32[]{:S(2)}) %collective-permute-start.22) | collective-permute-done | bytes 16416 | tf_op jit(solution)/shard_map/ppermute | solution.py:292
  71.2 0.4 collective-permute-start.23
  71.6 3.5 %collective-permute-done.23.side_ref = f32[8,512]{1,0:T(8,128)S(1)} collective-permute-done((f32[8,512]{1,0:T(8,128)S(1)}, f32[8,512]{1,0:T(8,128)S(1)}, u32[]{:S(2)}, u32[]{:S(2)}) %collective-permute-start.23) | collective-permute-done | bytes 16416 | tf_op jit(solution)/shard_map/ppermute | solution.py:287
  75.1 1.2 %collective-permute-start.24 = (f32[16,512]{1,0:T(8,128)S(1)}, f32[16,512]{1,0:T(8,128)S(1)}, u32[]{:S(2)}, u32[]{:S(2)}) collective-permute-start(f32[16,512]{1,0:T(8,128)S(1)} %pad_maximum_fusion), channel_id=1, source_target_pairs={{0,3},{1,0},{2,1},{3,2},{4,7},{5,4},{6,5},{7,6},{8,11},{9,8},{10,9... | collective-permute-start | bytes 98312 | tf_op jit(solution)/shard_map/ppermute | solution.py:287
  76.2 1.7 %collective-permute-start.25 = (f32[16,512]{1,0:T(8,128)S(1)}, f32[16,512]{1,0:T(8,128)S(1)}, u32[]{:S(2)}, u32[]{:S(2)}) collective-permute-start(f32[16,512]{1,0:T(8,128)S(1)} %pad_maximum_fusion), channel_id=1, source_target_pairs={{0,2},{1,3},{2,0},{3,1},{4,6},{5,7},{6,4},{7,5},{8,10},{9,11},{10,... | collective-permute-start | bytes 98312 | tf_op jit(solution)/shard_map/ppermute | solution.py:287
  78.0 1.4 %collective-permute-start.26 = (f32[16,512]{1,0:T(8,128)S(1)}, f32[16,512]{1,0:T(8,128)S(1)}, u32[]{:S(2)}, u32[]{:S(2)}) collective-permute-start(f32[16,512]{1,0:T(8,128)S(1)} %pad_maximum_fusion), channel_id=1, source_target_pairs={{0,1},{1,2},{2,3},{3,0},{4,5},{5,6},{6,7},{7,4},{8,9},{9,10},{10,1... | collective-permute-start | bytes 98312 | tf_op jit(solution)/shard_map/ppermute | solution.py:287
  79.4 0.0 collective-permute-done.24.z1_ref
  79.4 2.3 %collective-permute-done.25.z2_ref = f32[16,512]{1,0:T(8,128)S(1)} collective-permute-done((f32[16,512]{1,0:T(8,128)S(1)}, f32[16,512]{1,0:T(8,128)S(1)}, u32[]{:S(2)}, u32[]{:S(2)}) %collective-permute-start.25) | collective-permute-done | bytes 32800 | tf_op jit(solution)/shard_map/ppermute | solution.py:287
  81.6 1.4 %collective-permute-done.26.z3_ref = f32[16,512]{1,0:T(8,128)S(1)} collective-permute-done((f32[16,512]{1,0:T(8,128)S(1)}, f32[16,512]{1,0:T(8,128)S(1)}, u32[]{:S(2)}, u32[]{:S(2)}) %collective-permute-start.26) | collective-permute-done | bytes 32800 | tf_op jit(solution)/shard_map/ppermute | solution.py:287
  83.1 0.7 shard_map.36
  83.9 0.0 copy-done
  83.9 0.0 copy-start.1
  83.9 0.6 copy-done.1
  (7 shorter events, 0.1 us)
Async XLA Ops:
  2.2 6.4 %collective-permute-start.4 = (bf16[48,1024]{1,0:T(8,128)(2,1)S(1)}, bf16[48,1024]{1,0:T(8,128)(2,1)S(1)}, u32[]{:S(2)}, u32[]{:S(2)}) collective-permute-start(bf16[48,1024]{1,0:T(8,128)(2,1)S(1)} %get-tuple-element.245), channel_id=1, source_target_pairs={{0,3},{1,0},{2,1},{3,2},{4,7},{5,4},{6,5},{7,6},{8,11},{9,8},{10,9... | collective-permute-start | bytes 294920 | tf_op jit(solution)/shard_map/ppermute | solution.py:287
  6.4 6.9 %collective-permute-start.3 = (bf16[48,1024]{1,0:T(8,128)(2,1)S(1)}, bf16[48,1024]{1,0:T(8,128)(2,1)S(1)}, u32[]{:S(2)}, u32[]{:S(2)}) collective-permute-start(bf16[48,1024]{1,0:T(8,128)(2,1)S(1)} %get-tuple-element.244), channel_id=1, source_target_pairs={{0,1},{1,2},{2,3},{3,0},{4,5},{5,6},{6,7},{7,4},{8,9},{9,10},{10,1... | collective-permute-start | bytes 294920 | tf_op jit(solution)/shard_map/ppermute | solution.py:287
  6.4 6.9 %collective-permute-start.5 = (bf16[64,1024]{1,0:T(8,128)(2,1)S(1)}, bf16[64,1024]{1,0:T(8,128)(2,1)S(1)}, u32[]{:S(2)}, u32[]{:S(2)}) collective-permute-start(bf16[64,1024]{1,0:T(8,128)(2,1)S(1)} %get-tuple-element.247.own_ref), channel_id=1, source_target_pairs={{0,4},{1,5},{2,6},{3,7},{4,0},{5,1},{6,2},{7,3},{8,12},{9,13},{10,... | collective-permute-start | bytes 393224 | tf_op jit(solution)/shard_map/ppermute | solution.py:287
  7.9 10.9 %collective-permute-start.2 = (bf16[48,1024]{1,0:T(8,128)(2,1)S(1)}, bf16[48,1024]{1,0:T(8,128)(2,1)S(1)}, u32[]{:S(2)}, u32[]{:S(2)}) collective-permute-start(bf16[48,1024]{1,0:T(8,128)(2,1)S(1)} %get-tuple-element.243), channel_id=1, source_target_pairs={{0,4},{1,5},{2,6},{3,7},{4,0},{5,1},{6,2},{7,3},{8,12},{9,13},{10,... | collective-permute-start | bytes 294920 | tf_op jit(solution)/shard_map/ppermute | solution.py:287
  8.6 12.4 %collective-permute-start.9 = (bf16[48,1024]{1,0:T(8,128)(2,1)S(1)}, bf16[48,1024]{1,0:T(8,128)(2,1)S(1)}, u32[]{:S(2)}, u32[]{:S(2)}) collective-permute-start(bf16[48,1024]{1,0:T(8,128)(2,1)S(1)} %get-tuple-element.254), channel_id=1, source_target_pairs={{0,2},{1,3},{2,0},{3,1},{4,6},{5,7},{6,4},{7,5},{8,10},{9,11},{10,... | collective-permute-start | bytes 294920 | tf_op jit(solution)/shard_map/ppermute | solution.py:287
  13.3 7.8 %collective-permute-start.8 = (bf16[48,1024]{1,0:T(8,128)(2,1)S(1)}, bf16[48,1024]{1,0:T(8,128)(2,1)S(1)}, u32[]{:S(2)}, u32[]{:S(2)}) collective-permute-start(bf16[48,1024]{1,0:T(8,128)(2,1)S(1)} %get-tuple-element.252), channel_id=1, source_target_pairs={{0,6},{1,7},{2,4},{3,5},{4,2},{5,3},{6,0},{7,1},{8,14},{9,15},{10,... | collective-permute-start | bytes 294920 | tf_op jit(solution)/shard_map/ppermute | solution.py:287
  13.9 14.0 %collective-permute-start.10 = (bf16[64,1024]{1,0:T(8,128)(2,1)S(1)}, bf16[64,1024]{1,0:T(8,128)(2,1)S(1)}, u32[]{:S(2)}, u32[]{:S(2)}) collective-permute-start(bf16[64,1024]{1,0:T(8,128)(2,1)S(1)} %shard_map.31.refs_8_), channel_id=1, source_target_pairs={{0,1},{1,2},{2,3},{3,0},{4,5},{5,6},{6,7},{7,4},{8,9},{9,10},{10,1... | collective-permute-start | bytes 393224 | tf_op jit(solution)/shard_map/ppermute | solution.py:287
  15.3 12.5 %collective-permute-start.11 = (bf16[64,1024]{1,0:T(8,128)(2,1)S(1)}, bf16[64,1024]{1,0:T(8,128)(2,1)S(1)}, u32[]{:S(2)}, u32[]{:S(2)}) collective-permute-start(bf16[64,1024]{1,0:T(8,128)(2,1)S(1)} %shard_map.31.refs_8_), channel_id=1, source_target_pairs={{0,2},{1,3},{2,0},{3,1},{4,6},{5,7},{6,4},{7,5},{8,10},{9,11},{10,... | collective-permute-start | bytes 393224 | tf_op jit(solution)/shard_map/ppermute | solution.py:287
  18.8 9.0 %collective-permute-start.12 = (bf16[64,1024]{1,0:T(8,128)(2,1)S(1)}, bf16[64,1024]{1,0:T(8,128)(2,1)S(1)}, u32[]{:S(2)}, u32[]{:S(2)}) collective-permute-start(bf16[64,1024]{1,0:T(8,128)(2,1)S(1)} %shard_map.31.refs_8_), channel_id=1, source_target_pairs={{0,3},{1,0},{2,1},{3,2},{4,7},{5,4},{6,5},{7,6},{8,11},{9,8},{10,9... | collective-permute-start | bytes 393224 | tf_op jit(solution)/shard_map/ppermute | solution.py:287
  21.0 5.5 %collective-permute-start.7 = (bf16[48,1024]{1,0:T(8,128)(2,1)S(1)}, bf16[48,1024]{1,0:T(8,128)(2,1)S(1)}, u32[]{:S(2)}, u32[]{:S(2)}) collective-permute-start(bf16[48,1024]{1,0:T(8,128)(2,1)S(1)} %get-tuple-element.250), channel_id=1, source_target_pairs={{0,7},{1,4},{2,5},{3,6},{4,3},{5,0},{6,1},{7,2},{8,15},{9,12},{10,... | collective-permute-start | bytes 294920 | tf_op jit(solution)/shard_map/ppermute | solution.py:287
  21.1 6.8 %collective-permute-start.6 = (bf16[48,1024]{1,0:T(8,128)(2,1)S(1)}, bf16[48,1024]{1,0:T(8,128)(2,1)S(1)}, u32[]{:S(2)}, u32[]{:S(2)}) collective-permute-start(bf16[48,1024]{1,0:T(8,128)(2,1)S(1)} %get-tuple-element.248), channel_id=1, source_target_pairs={{0,5},{1,6},{2,7},{3,4},{4,1},{5,2},{6,3},{7,0},{8,13},{9,14},{10,... | collective-permute-start | bytes 294920 | tf_op jit(solution)/shard_map/ppermute | solution.py:287
  28.5 20.4 %collective-permute-start.15 = (bf16[448,1024]{1,0:T(8,128)(2,1)S(1)}, bf16[448,1024]{1,0:T(8,128)(2,1)S(1)}, u32[]{:S(2)}, u32[]{:S(2)}) collective-permute-start(bf16[448,1024]{1,0:T(8,128)(2,1)S(1)} %shard_map.32.refs_0_.refs_3_), channel_id=1, source_target_pairs={{0,8},{1,9},{2,10},{3,11},{4,12},{5,13},{6,14},{7,15},{8,0},{9,1},... | collective-permute-start | bytes 2752520 | tf_op jit(solution)/shard_map/ppermute | solution.py:287
  32.1 18.1 %collective-permute-start.13 = (bf16[448,1024]{1,0:T(8,128)(2,1)S(1)}, bf16[448,1024]{1,0:T(8,128)(2,1)S(1)}, u32[]{:S(2)}, u32[]{:S(2)}) collective-permute-start(bf16[448,1024]{1,0:T(8,128)(2,1)S(1)} %shard_map.32.refs_0_.refs_3_), channel_id=1, source_target_pairs={{0,32},{16,48},{32,64},{48,80},{64,96},{80,112},{96,0},{112,16},{1... | collective-permute-start | bytes 2752520 | tf_op jit(solution)/shard_map/ppermute | solution.py:292
  33.7 16.9 %collective-permute-start.14 = (bf16[448,1024]{1,0:T(8,128)(2,1)S(1)}, bf16[448,1024]{1,0:T(8,128)(2,1)S(1)}, u32[]{:S(2)}, u32[]{:S(2)}) collective-permute-start(bf16[448,1024]{1,0:T(8,128)(2,1)S(1)} %shard_map.32.refs_0_.refs_3_), channel_id=1, source_target_pairs={{0,96},{16,112},{32,0},{48,16},{64,32},{80,48},{96,64},{112,80},{1... | collective-permute-start | bytes 2752520 | tf_op jit(solution)/shard_map/ppermute | solution.py:292
  35.3 18.5 %collective-permute-start.17 = (bf16[448,1024]{1,0:T(8,128)(2,1)S(1)}, bf16[448,1024]{1,0:T(8,128)(2,1)S(1)}, u32[]{:S(2)}, u32[]{:S(2)}) collective-permute-start(bf16[448,1024]{1,0:T(8,128)(2,1)S(1)} %shard_map.32.refs_0_.refs_3_), channel_id=1, source_target_pairs={{0,16},{16,0},{32,48},{48,32},{64,80},{80,64},{96,112},{112,96},{1... | collective-permute-start | bytes 2752520 | tf_op jit(solution)/shard_map/ppermute | solution.py:292
  48.9 8.0 %collective-permute-start.16 = (bf16[448,1024]{1,0:T(8,128)(2,1)S(1)}, bf16[448,1024]{1,0:T(8,128)(2,1)S(1)}, u32[]{:S(2)}, u32[]{:S(2)}) collective-permute-start(bf16[448,1024]{1,0:T(8,128)(2,1)S(1)} %collective-permute-done.15.refs_3_.refs_2_), channel_id=1, source_target_pairs={{0,16},{16,0},{32,48},{48,32},{64,80},{80,64},{96,112},{112,96},{1... | collective-permute-start | bytes 2752520 | tf_op jit(solution)/shard_map/ppermute | solution.py:292
  50.2 13.2 %collective-permute-start.20 = (bf16[224,1024]{1,0:T(8,128)(2,1)S(1)}, bf16[224,1024]{1,0:T(8,128)(2,1)S(1)}, u32[]{:S(2)}, u32[]{:S(2)}) collective-permute-start(bf16[224,1024]{1,0:T(8,128)(2,1)S(1)} %slice.21), channel_id=1, source_target_pairs={{0,32},{16,48},{32,64},{48,80},{64,96},{80,112},{96,0},{112,16},{1... | collective-permute-start | bytes 1376264 | tf_op jit(solution)/shard_map/ppermute | solution.py:292
  50.7 13.1 %collective-permute-start.21 = (bf16[224,1024]{1,0:T(8,128)(2,1)S(1)}, bf16[224,1024]{1,0:T(8,128)(2,1)S(1)}, u32[]{:S(2)}, u32[]{:S(2)}) collective-permute-start(bf16[224,1024]{1,0:T(8,128)(2,1)S(1)} %slice.22), channel_id=1, source_target_pairs={{0,96},{16,112},{32,0},{48,16},{64,32},{80,48},{96,64},{112,80},{1... | collective-permute-start | bytes 1376264 | tf_op jit(solution)/shard_map/ppermute | solution.py:292
  60.1 8.8 %collective-permute-start.19 = (f32[8,512]{1,0:T(8,128)S(1)}, f32[8,512]{1,0:T(8,128)S(1)}, u32[]{:S(2)}, u32[]{:S(2)}) collective-permute-start(f32[8,512]{1,0:T(8,128)S(1)} %max.30), channel_id=1, source_target_pairs={{0,32},{16,48},{32,64},{48,80},{64,96},{80,112},{96,0},{112,16},{1... | collective-permute-start | bytes 49160 | tf_op jit(solution)/shard_map/ppermute | solution.py:292
  60.2 23.7 %copy-start = (s32[384]{0:T(512)S(1)}, s32[384]{0:T(512)}, u32[]{:S(2)}) copy-start(s32[384]{0:T(512)} %ids_ref.1) | copy-start | bytes 4612
  60.2 8.7 %collective-permute-start.18 = (f32[8,512]{1,0:T(8,128)S(1)}, f32[8,512]{1,0:T(8,128)S(1)}, u32[]{:S(2)}, u32[]{:S(2)}) collective-permute-start(f32[8,512]{1,0:T(8,128)S(1)} %max.29), channel_id=1, source_target_pairs={{0,96},{16,112},{32,0},{48,16},{64,32},{80,48},{96,64},{112,80},{1... | collective-permute-start | bytes 49160 | tf_op jit(solution)/shard_map/ppermute | solution.py:292
  65.9 5.3 %collective-permute-start.22 = (f32[8,512]{1,0:T(8,128)S(1)}, f32[8,512]{1,0:T(8,128)S(1)}, u32[]{:S(2)}, u32[]{:S(2)}) collective-permute-start(f32[8,512]{1,0:T(8,128)S(1)} %shard_map.35), channel_id=1, source_target_pairs={{0,64},{16,80},{32,96},{48,112},{64,0},{80,16},{96,32},{112,48},{1... | collective-permute-start | bytes 49160 | tf_op jit(solution)/shard_map/ppermute | solution.py:292
  71.2 3.8 %collective-permute-start.23 = (f32[8,512]{1,0:T(8,128)S(1)}, f32[8,512]{1,0:T(8,128)S(1)}, u32[]{:S(2)}, u32[]{:S(2)}) collective-permute-start(f32[8,512]{1,0:T(8,128)S(1)} %maximum_maximum_fusion.own_ref), channel_id=1, source_target_pairs={{0,4},{1,5},{2,6},{3,7},{4,0},{5,1},{6,2},{7,3},{8,12},{9,13},{10,... | collective-permute-start | bytes 49160 | tf_op jit(solution)/shard_map/ppermute | solution.py:287
  75.1 4.3 %collective-permute-start.24 = (f32[16,512]{1,0:T(8,128)S(1)}, f32[16,512]{1,0:T(8,128)S(1)}, u32[]{:S(2)}, u32[]{:S(2)}) collective-permute-start(f32[16,512]{1,0:T(8,128)S(1)} %pad_maximum_fusion), channel_id=1, source_target_pairs={{0,3},{1,0},{2,1},{3,2},{4,7},{5,4},{6,5},{7,6},{8,11},{9,8},{10,9... | collective-permute-start | bytes 98312 | tf_op jit(solution)/shard_map/ppermute | solution.py:287
  76.2 5.4 %collective-permute-start.25 = (f32[16,512]{1,0:T(8,128)S(1)}, f32[16,512]{1,0:T(8,128)S(1)}, u32[]{:S(2)}, u32[]{:S(2)}) collective-permute-start(f32[16,512]{1,0:T(8,128)S(1)} %pad_maximum_fusion), channel_id=1, source_target_pairs={{0,2},{1,3},{2,0},{3,1},{4,6},{5,7},{6,4},{7,5},{8,10},{9,11},{10,... | collective-permute-start | bytes 98312 | tf_op jit(solution)/shard_map/ppermute | solution.py:287
  78.0 5.1 %collective-permute-start.26 = (f32[16,512]{1,0:T(8,128)S(1)}, f32[16,512]{1,0:T(8,128)S(1)}, u32[]{:S(2)}, u32[]{:S(2)}) collective-permute-start(f32[16,512]{1,0:T(8,128)S(1)} %pad_maximum_fusion), channel_id=1, source_target_pairs={{0,1},{1,2},{2,3},{3,0},{4,5},{5,6},{6,7},{7,4},{8,9},{9,10},{10,1... | collective-permute-start | bytes 98312 | tf_op jit(solution)/shard_map/ppermute | solution.py:287
  83.9 0.6 copy-start.1

commit v3 on v2

--- a/solution.py
+++ b/solution.py
@@ -18,11 +18,13 @@
 LIGHT = 42
 MAIN = OWNERS * CHUNK
 EXTRA = 64
-BLOCK = MAIN + EXTRA
 LANES = 512
+BLOCK = 352
+UPPER = BLOCK // 2
+EXTRA_LANE = 384
 LOW = -1e30
 
-STEPS = ((1, 0), (0, 1), (0, 3), (1, 1), (1, 3), (1, 2), (0, 2))
+STEPS = ((0, 0), (1, 1), (1, 3), (1, 2), (0, 2), (0, 1), (0, 3), (1, 0))
 
 VMEM = pl.BlockSpec(memory_space=pltpu.VMEM)
 PARAMS = pltpu.CompilerParams(vmem_limit_bytes=48 * 1024 * 1024)
@@ -143,15 +145,17 @@
     told = jnp.where(line == 12, middle, told)
     told = jnp.where(line == 13, low, told)
     rest = (group == home) & (rank >= float(LIGHT))
-    lane = jnp.where(rest, rank + float(MAIN - LIGHT), -1.0)
+    place = jnp.where(rest, rank + float(MAIN - LIGHT), -1.0)
+    lane = jnp.where(rest, rank + float(EXTRA_LANE - LIGHT), -1.0)
     tolds = []
-    for slot, (dx, dz) in enumerate(((0, 0), *STEPS)):
+    for slot, (dx, dz) in enumerate(STEPS):
         goes = (group == owner_at(at_ref, dx, dz).astype(jnp.float32)) & (rank < float(LIGHT))
-        lane = jnp.where(goes, rank + float(slot * CHUNK), lane)
+        place = jnp.where(goes, rank + float(slot * CHUNK), place)
+        lane = jnp.where(goes, rank + float(slot * LIGHT), lane)
         tolds.append(jnp.where(goes, told, 0.0))
     tolds.append(jnp.where(rest, told, 0.0))
     known_ref[...] = jnp.where(line == 0, lane, group)[0:8]
-    pick = as_bf16(iota((LANES, ROWS), 0) == lane.astype(jnp.int32))
+    pick = as_bf16(iota((LANES, ROWS), 0) == place.astype(jnp.int32))
     data = dot_nn(pick, rows_ref[...])
     placed = dot_nt(jnp.concatenate(tolds, axis=0).astype(jnp.bfloat16), pick)
     for slot, ref in enumerate(chunk_refs):
@@ -159,9 +163,9 @@
         ref[0:32, :] = data[first : first + 32].astype(jnp.bfloat16)
         tail = data[first + 32 : first + CHUNK]
         ref[32:CHUNK, :] = tail.astype(jnp.bfloat16)
-        ref[32:CHUNK, 0:MAIN] = (tail[:, 0:MAIN] + placed[16 * slot : 16 * slot + 16, 0:MAIN]).astype(jnp.bfloat16)
+        ref[32:CHUNK, 0:LANES] = (tail[:, 0:LANES] + placed[16 * slot : 16 * slot + 16]).astype(jnp.bfloat16)
     extra_ref[0:48, :] = data[MAIN : MAIN + 48].astype(jnp.bfloat16)
-    tail = data[MAIN + 48 : BLOCK]
+    tail = data[MAIN + 48 : MAIN + EXTRA]
     tail = jnp.where(iota(tail.shape, 0) == 15, home + 1.0, tail)
     extra_ref[48:EXTRA, :] = tail.astype(jnp.bfloat16)
     extra_ref[48:EXTRA, 0:128] = (
@@ -184,10 +188,8 @@
     out_ref[EXTRA - 16 : EXTRA, :] = jnp.where(clash, 0.0, tail).astype(jnp.bfloat16)
 
 
-def block_kernel(at_ref, *refs):
-    chunks, extras, out_ref = refs[0:8], refs[8:12], refs[12]
-    for slot, chunk_ref in enumerate(chunks):
-        out_ref[slot * CHUNK : (slot + 1) * CHUNK, :] = chunk_ref[...]
+def extra_kernel(at_ref, *refs):
+    extras, out_ref = refs[0:4], refs[4]
     wanted = owner_at(at_ref, 0, 0).astype(jnp.float32) + 1.0
     found = jnp.zeros((1, 1), jnp.float32)
     held = jnp.ones((1, 1), jnp.float32)
@@ -199,18 +201,36 @@
         if index > 0:
             taken = jnp.where(mark == wanted, extras[index][...], taken)
     good = jnp.where((found == 1.0) & (held == 1.0), 1.0, 0.0)
-    out_ref[MAIN : BLOCK - 16, :] = taken[0 : EXTRA - 16]
+    out_ref[0 : EXTRA - 16, :] = taken[0 : EXTRA - 16]
     tail = taken[EXTRA - 16 : EXTRA].astype(jnp.float32)
-    out_ref[BLOCK - 16 : BLOCK, :] = jnp.where(iota(tail.shape, 0) == 14, good, tail).astype(jnp.bfloat16)
+    out_ref[EXTRA - 16 : EXTRA, :] = jnp.where(iota(tail.shape, 0) == 14, good, tail).astype(jnp.bfloat16)
+
+
+def block_kernel(*refs):
+    chunk_refs, out_ref, whole = refs[0:8], refs[8], refs[9]
+    total = jnp.zeros((16, MAIN), jnp.float32)
+    for slot, chunk_ref in enumerate(chunk_refs):
+        whole[slot * CHUNK : (slot + 1) * CHUNK, :] = chunk_ref[...]
+        total = total + chunk_ref[CHUNK - 16 : CHUNK, 0:MAIN].astype(jnp.float32)
+    row = iota((BLOCK, MAIN), 0)
+    source = row
+    for slot in range(1, OWNERS):
+        source = source + jnp.where(row >= slot * LIGHT, CHUNK - LIGHT, 0)
+    source = jnp.where(row < OWNERS * LIGHT, source, -1)
+    pick = as_bf16(iota((BLOCK, MAIN), 1) == source)
+    data = dot_nn(pick, whole[...])
+    told = dot_nt(total.astype(jnp.bfloat16), pick)
+    line = iota((16, BLOCK), 0)
+    told = jnp.where((line >= 10) & (line <= 13), told, 0.0)
+    out_ref[0 : BLOCK - 16, :] = data[0 : BLOCK - 16].astype(jnp.bfloat16)
+    out_ref[BLOCK - 16 : BLOCK, :] = jnp.zeros((16, out_ref.shape[1]), jnp.bfloat16)
+    out_ref[BLOCK - 16 : BLOCK, 0:BLOCK] = told.astype(jnp.bfloat16)
 
 
 def told_of(ref):
-    total = jnp.zeros((16, MAIN), jnp.float32)
-    for index in range(1, OWNERS + 1):
-        total = total + ref[index * CHUNK - 16 : index * CHUNK, 0:MAIN].astype(jnp.float32)
-    end = ref[BLOCK - 16 : BLOCK, 0:128].astype(jnp.float32)
-    total = jnp.concatenate([total, end], axis=1)[:, 0:BLOCK]
-    return total[10:11], total[11:12] + total[12:13] + total[13:14], end[14:15, 0:1]
+    count = ref.shape[0]
+    end = ref[count - 16 : count, 0:BLOCK].astype(jnp.float32)[:, 0:count]
+    return end[10:11], end[11:12] + end[12:13] + end[13:14]
 
 
 def column_of(row):
@@ -219,42 +239,90 @@
     return jnp.sum(jnp.where(diagonal, row, 0.0), axis=1, keepdims=True)
 
 
-def match_kernel(left_count, right_count, own, checked, *refs):
-    blocks, out_refs = refs[: left_count + right_count], refs[left_count + right_count :]
-    told = [told_of(ref) for ref in blocks]
-    best = [jnp.full((1, BLOCK), LOW, jnp.float32)] * left_count
-    for right in range(left_count, left_count + right_count):
-        ids, inverse = column_of(told[right][0]), column_of(told[right][1])
-        rows = blocks[right][...]
-        for left in range(left_count):
-            scores = dot_nt(rows, blocks[left][...]) * inverse
-            alike = ids == told[left][0]
-            if own and left == 0 and right == left_count:
-                alike = alike & (iota(scores.shape, 0) != iota(scores.shape, 1))
-            best[left] = jnp.maximum(best[left], jnp.max(jnp.where(alike, scores, LOW), axis=0, keepdims=True))
-    for left in range(left_count):
-        out_refs[left][...] = jnp.full(out_refs[left].shape, -1.0, jnp.float32)
-        out_refs[left][0:1, 0:BLOCK] = jnp.maximum(best[left] * told[left][1], -1.0)
-    if checked:
-        good = jnp.minimum(told[0][2], told[left_count][2])
-        out_refs[0][1:2, :] = jnp.broadcast_to(good, (1, LANES))
+def best_over(lefts, rights, shared):
+    best = [jnp.full((1, left.shape[0]), LOW, jnp.float32) for left, _ in lefts]
+    for right_index, (right, (right_ids, right_inverse)) in enumerate(rights):
+        ids, inverse = column_of(right_ids), column_of(right_inverse)
+        rows = right[...]
+        for left_index, (left, (left_ids, _)) in enumerate(lefts):
+            scores = dot_nt(rows, left[...]) * inverse
+            alike = ids == left_ids
+            if shared and left_index == 0 and right_index == 0:
+                row, column = iota(scores.shape, 0), iota(scores.shape, 1)
+                alike = alike & ((row != column) | (row >= shared))
+            top = jnp.max(jnp.where(alike, scores, LOW), axis=0, keepdims=True)
+            best[left_index] = jnp.maximum(best[left_index], top)
+    return best
+
+
+def scaled(best, inverse):
+    return jnp.maximum(best * inverse, -1.0)
+
+
+def main_kernel(left_count, own, *refs):
+    out_refs = refs[len(refs) - left_count :]
+    blocks = [(ref, told_of(ref)) for ref in refs[: len(refs) - left_count]]
+    lefts = blocks[:left_count]
+    best = best_over(lefts, blocks[left_count:], BLOCK if own else 0)
+    for out_ref, (_, (_, inverse)), top in zip(out_refs, lefts, best):
+        out_ref[...] = jnp.full(out_ref.shape, -1.0, jnp.float32)
+        out_ref[0:1, 0:BLOCK] = scaled(top, inverse)
+
+
+def stack(refs, whole):
+    told = [told_of(ref) for ref in refs]
+    for index, ref in enumerate(refs):
+        whole[index * EXTRA : (index + 1) * EXTRA, :] = ref[...]
+    return whole, tuple(jnp.concatenate([part[index] for part in told], axis=1) for index in range(2))
+
+
+def extras_kernel(count, *refs):
+    blocks, extras, rights, right_extras = (
+        refs[:count],
+        refs[count : 2 * count],
+        refs[2 * count : 2 * count + 4],
+        refs[2 * count + 4 : 2 * count + 8],
+    )
+    out_refs, left_whole, right_whole = refs[2 * count + 8 : -2], refs[-2], refs[-1]
+    lefts = [(ref, told_of(ref)) for ref in blocks]
+    left_stack, right_stack = stack(extras, left_whole), stack(right_extras, right_whole)
+    best = best_over(lefts, [right_stack], 0)
+    (extra_best,) = best_over(
+        [left_stack], [right_stack, *[(ref, told_of(ref)) for ref in rights]], EXTRA if count > 1 else 0
+    )
+    extra_best = scaled(extra_best, left_stack[1][1])
+    bad = jnp.zeros((1, 1), jnp.float32)
+    for ref in right_extras:
+        bad = jnp.maximum(bad, 1.0 - ref[EXTRA - 16 : EXTRA, :].astype(jnp.float32)[14:15, 0:1])
+    for index, out_ref in enumerate(out_refs):
+        out_ref[...] = jnp.full(out_ref.shape, -1.0, jnp.float32)
+        out_ref[0:1, 0:BLOCK] = scaled(best[index], lefts[index][1][1])
+        out_ref[0:1, EXTRA_LANE : EXTRA_LANE + EXTRA] = extra_best[:, index * EXTRA : (index + 1) * EXTRA]
+        out_ref[1:2, :] = jnp.broadcast_to(bad if count > 1 else jnp.zeros_like(bad), (1, LANES))
 
 
 def far_kernel(upper_ref, lower_ref, *refs):
-    rights, out_ref, left = refs[0:4], refs[4], refs[5]
-    left[0 : BLOCK // 2, :] = upper_ref[...]
-    left[BLOCK // 2 : BLOCK, :] = lower_ref[...]
-    match_kernel(1, 4, False, False, left, *rights, out_ref)
+    rights, out_ref, left = refs[:4], refs[4], refs[5]
+    left[0:UPPER, :] = upper_ref[...]
+    left[UPPER:BLOCK, :] = lower_ref[...]
+    main_kernel(1, False, left, *rights, out_ref)
+
+
+def far_extras_kernel(upper_ref, lower_ref, *refs):
+    left = refs[-3]
+    left[0:UPPER, :] = upper_ref[...]
+    left[UPPER:BLOCK, :] = lower_ref[...]
+    extras_kernel(1, left, *refs[:-3], *refs[-2:])
 
 
 def final_kernel(at_ref, own_ref, side_ref, z1_ref, z2_ref, z3_ref, known_ref, out_ref, ok_ref):
     sources = {1: z1_ref, 2: z2_ref, 3: z3_ref}
-    vectors, groups, good = [], [], jnp.ones((1, LANES), jnp.float32)
-    for dx, dz in ((0, 0), *STEPS):
+    vectors, groups, bad = [], [], jnp.zeros((1, LANES), jnp.float32)
+    for dx, dz in STEPS:
         ref, row = (side_ref if dx else own_ref, 0) if dz == 0 else (sources[dz], 8 * dx)
         vectors.append(ref[row : row + 1, :])
         groups.append(owner_at(at_ref, dx, dz).astype(jnp.float32))
-        good = jnp.minimum(good, ref[row + 1 : row + 2, :])
+        bad = jnp.maximum(bad, ref[row + 1 : row + 2, :])
     parts = three_parts(jnp.concatenate(vectors, axis=0))
     pick = as_bf16(iota((LANES, ROWS), 0) == known_ref[0:1, :].astype(jnp.int32))
     picked = dot_nn(jnp.concatenate(parts, axis=0).astype(jnp.bfloat16), pick)
@@ -263,7 +331,7 @@
     for index, group in enumerate(groups):
         total = jnp.where(known_ref[1:2, :] == group, picked[index : index + 1], total)
     out_ref[...] = total.reshape(ROWS)
-    ok_ref[...] = jnp.where(good[:, 0:128] == 1.0, 1, 0)
+    ok_ref[...] = jnp.where(bad[:, 0:128] == 0.0, 1, 0)
 
 
 SMEM = pl.BlockSpec(memory_space=pltpu.SMEM)
@@ -282,30 +350,40 @@
     )(*args)
 
 
-def along_sub(value, to_x, to_z):
-    perm = [(4 * x + z, 4 * to_x(x) + to_z(z)) for x in range(4) for z in range(4)]
-    return lax.ppermute(value, "sub", perm)
-
-
-def along_grp(value, to_y, to_core):
-    perm = [(2 * y + c, 2 * to_y(y) + to_core(c)) for y in range(4) for c in range(2)]
-    return lax.ppermute(value, "grp", perm)
-
-
-def after(value, other):
-    return lax.optimization_barrier((value, other))[0]
-
-
-def same(index):
-    return index
-
-
-def shift(amount):
-    return lambda index: (index + amount) % 4
-
-
-def flip(amount):
-    return lambda index: index ^ amount
+def along(value, move):
+    def index(y, core, x, z):
+        return ((2 * (y % 4) + core) * 4 + x % 4) * 4 + z % 4
+
+    places = [(y, core, x, z) for y in range(4) for core in range(2) for x in range(4) for z in range(4)]
+    return lax.ppermute(value, ("grp", "sub"), [(index(*place), index(*move(*place))) for place in places])
+
+
+def partner(core, x):
+    return x ^ (3 if core else 1)
+
+
+def to_owner(dx, dz):
+    return lambda y, core, x, z: (y, core, partner(core, x) if dx else x, z + dz)
+
+
+def to_y(amount):
+    return lambda y, core, x, z: (y + amount, core, x, z)
+
+
+def to_sibling(y, core, x, z):
+    return y, 1 - core, x, z
+
+
+def to_across(y, core, x, z):
+    return y, core, x + 2, z
+
+
+def join(value, other):
+    return jnp.concatenate([value, other], axis=0)
+
+
+def after(value, *others):
+    return lax.optimization_barrier((value, *others))[0]
 
 
 def local(embeddings, cluster_ids):
@@ -323,52 +401,72 @@
         scalars=1,
         flops=500_000_000,
     )
-    other_extra = along_sub(extra, flip(1), same)
-    got = [chunks[0]]
-    for slot, (dx, dz) in enumerate(STEPS, 1):
-        chunk = chunks[slot]
-        if slot > 3:
-            chunk = after(chunk, other_extra if slot == 4 else got[slot - 4])
-        got.append(along_sub(chunk, flip(dx), shift(dz)))
+    other_extra = along(extra, to_owner(1, 0))
+    got = [after(chunks[0], other_extra)]
+    got += [along(chunks[slot], to_owner(*STEPS[slot])) for slot in range(1, OWNERS)]
+    block = call(
+        block_kernel,
+        shape((BLOCK, width), bf16),
+        *got,
+        scratch=[pltpu.VMEM((MAIN, width), bf16)],
+    )
     extra = call(half_kernel, shape((EXTRA, width), bf16), at, extra, other_extra, scalars=1)
-    extras = [extra] + [along_sub(extra, same, shift(dz)) for dz in (1, 2, 3)]
-    block = call(block_kernel, shape((BLOCK, width), bf16), at, *got, *extras, scalars=1)
-    half = BLOCK // 2
-    below = along_grp(block, shift(1), same)
-    above = along_grp(block, shift(-1), same)
-    across = along_sub(block, shift(2), same)
-    sibling = along_grp(block, same, flip(1))
-    far = (along_grp(below[:half], shift(1), same), along_grp(above[half:], shift(-1), same))
-    across_sibling = along_grp(across, same, flip(1))
-
+    extras = [extra] + [along(extra, to_owner(0, dz)) for dz in (1, 3)]
+    extras.append(along(after(extra, extras[1]), to_owner(0, 2)))
+    extra = call(extra_kernel, shape((EXTRA, width), bf16), at, *extras, scalars=1)
+    below = along(block, to_y(1))
+    above = along(block, to_y(-1))
+    across = along(block, to_across)
+    sibling = along(block, to_sibling)
+    from_lower = along(join(below[:UPPER], extra), to_y(1))
+    from_upper = along(join(above[UPPER:], extra), to_y(-1))
+    across_extra = along(after(extra, below, above), to_across)
+    from_sibling = along(join(across, extra), to_sibling)
+    below_extra, above_extra, sibling_extra = from_lower[UPPER:], from_upper[UPPER:], from_sibling[BLOCK:]
+    across_sibling = from_sibling[:BLOCK]
+    far, far_extra = (from_lower[:UPPER], from_upper[:UPPER]), along(below_extra, to_y(1))
+    vector = shape((8, LANES), f32)
     flops = 2 * BLOCK * BLOCK * width
-    vector = shape((8, LANES), f32)
-
-    def match(lefts, rights, own=False, checked=False):
-        counts = len(lefts), len(rights)
-        kernel = functools.partial(match_kernel, *counts, own, checked)
-        return call(kernel, [vector] * counts[0], *lefts, *rights, flops=flops * counts[0] * counts[1])
-
-    near, others = (block, sibling), (across, across_sibling)
-    best_near, below_near, above_near = match((block, below, above), near, own=True)
-    best, below_other, above_other = match((block, below, above), others, checked=True)
-    from_above = along_grp(jnp.maximum(below_near, below_other), shift(-1), same)
-    from_below = along_grp(jnp.maximum(above_near, above_other), shift(1), same)
-    best_far = call(
-        far_kernel,
+    blocks, rights = (block, below, above), (block, sibling, across, across_sibling)
+    extras = (extra, below_extra, above_extra)
+    wholes = [pltpu.VMEM((count * EXTRA, width), bf16) for count in (3, 4)]
+    near = call(functools.partial(main_kernel, 3, True), [vector] * 3, *blocks, *rights[:2], flops=6 * flops)
+    others = call(functools.partial(main_kernel, 3, False), [vector] * 3, *blocks, *rights[2:], flops=6 * flops)
+    across_sibling_extra = along(after(across_extra, near[0], others[0]), to_sibling)
+    right_extras = (extra, sibling_extra, across_extra, across_sibling_extra)
+    added = call(
+        functools.partial(extras_kernel, 3),
+        [vector] * 3,
+        *blocks,
+        *extras,
+        *rights,
+        *right_extras,
+        scratch=wholes,
+        flops=5 * flops,
+    )
+    best, best_below, best_above = [
+        jnp.maximum(jnp.maximum(first, second), third) for first, second, third in zip(near, others, added)
+    ]
+    from_above = along(best_below, to_y(-1))
+    from_below = along(best_above, to_y(1))
+    left = pltpu.VMEM((BLOCK, width), bf16)
+    best_far = call(far_kernel, vector, *far, *rights, scratch=[left], flops=4 * flops)
+    added_far = call(
+        far_extras_kernel,
         vector,
         *far,
-        *near,
-        *others,
-        scratch=[pltpu.VMEM((BLOCK, width), bf16)],
-        flops=4 * flops,
-    )
-    from_far = along_grp(best_far, shift(2), same)
-    best = jnp.maximum(jnp.maximum(best, best_near), jnp.maximum(from_above, from_below))
+        far_extra,
+        *rights,
+        *right_extras,
+        scratch=[left, pltpu.VMEM((EXTRA, width), bf16), wholes[1]],
+        flops=2 * flops,
+    )
+    from_far = along(jnp.maximum(best_far, added_far), to_y(2))
+    best = jnp.maximum(best, jnp.maximum(from_above, from_below))
     best = jnp.maximum(best, from_far)
-    side = along_sub(best, flip(1), same)
+    side = along(best, to_owner(1, 0))
     both = jnp.concatenate([best, side], axis=0)
-    pulled = [along_sub(both, same, shift(-dz)) for dz in (1, 2, 3)]
+    pulled = [along(both, to_owner(0, -dz)) for dz in (1, 2, 3)]
     out, ok = call(
         final_kernel,
         [shape((ROWS,), f32), shape((1, 128), jnp.int32)],

time: 84.6 us -> 84.2 us (level)
  waiting for transfers between devices: 31.2 us -> 28.7 us
  Pallas kernels: 12.5 us -> 14.5 us
    ppermute x25 -> x28, waiting for transfers between devices: 31.2 us -> 28.7 us  [along(): lax.ppermute(value, ('grp', 'sub'), [(index(*place), index(*move(*place))...]
    pallas_call x7 -> x10, Pallas kernels: 12.5 us -> 14.5 us  [call(): pl.pallas_call(kernel, out_shape=outs, in_specs=[SMEM] * scalars + [VMEM]...]
    ppermute x25 -> x28, starting transfers between devices: 39.8 us -> 39.4 us  [along(): lax.ppermute(value, ('grp', 'sub'), [(index(*place), index(*move(*place))...]
  transfers between devices with their start and end apart: 25 -> 28, of which waited for: 11 -> 13; matrix products, arithmetic and copies ran while one was open for 0% -> 0% of each run, Pallas kernels for 11% -> 13%
where the time goes in v3:
time: 84.2 us; the launch traced here: 83.8 us
  starting transfers between devices  39.4 us (47%)
  waiting for transfers between devices  28.7 us (34%)
  Pallas kernels  14.5 us (17%)
    ppermute x28, starting transfers between devices, along(): lax.ppermute(value, ('grp', 'sub'), [(index(*place), index(*move(*place))...  39.4 us
    ppermute x28, waiting for transfers between devices, along(): lax.ppermute(value, ('grp', 'sub'), [(index(*place), index(*move(*place))...  28.7 us
    pallas_call x10, Pallas kernels, call(): pl.pallas_call(kernel, out_shape=outs, in_specs=[SMEM] * scalars + [VMEM]...  14.5 us
  transfers between devices with their start and end apart: 28, of which 13 were waited for; matrix products, arithmetic and copies ran while one was open for 0% of the time, Pallas kernels for 13%

profile of v3, /device:TPU:0, one launch (start us, length us, event | category | flops | bytes accessed | tf_op | source)
XLA Modules:
  0.0 83.8 jit_solution(10105540152576830269)
XLA Ops:
  0.0 0.1 pad_add_fusion.at_ref
  0.1 2.1 %shard_map.30 = (bf16[48,1024]{1,0:T(8,128)(2,1)S(1)}, bf16[48,1024]{1,0:T(8,128)(2,1)S(1)}, bf16[48,1024]{1,0:T(8,128)(2,1)S(1)}, bf16[48,1024]{1,0:T(8,128)(2,...) custom-call(s32[2]{0:T(128)S(1)} %pad_add_fusion.at_ref, ...), custom_call_target="tpu_custom_call" | custom-call | flops 500000000 | bytes 787976 | tf_op jit(solution)/shard_map/pallas_call | solution.py:342
  2.2 1.7 %collective-permute-start.2 = (bf16[64,1024]{1,0:T(8,128)(2,1)S(1)}, bf16[64,1024]{1,0:T(8,128)(2,1)S(1)}, u32[]{:S(2)}, u32[]{:S(2)}) collective-permute-start(bf16[64,1024]{1,0:T(8,128)(2,1)S(1)} %get-tuple-element.246.own_ref), channel_id=1, source_target_pairs={{0,4},{1,5},{2,6},{3,7},{4,0},{5,1},{6,2},{7,3},{8,12},{9,13},{10,... | collective-permute-start | bytes 393224 | tf_op jit(solution)/shard_map/ppermute | solution.py:358
  3.8 1.9 %collective-permute-start.3 = (bf16[48,1024]{1,0:T(8,128)(2,1)S(1)}, bf16[48,1024]{1,0:T(8,128)(2,1)S(1)}, u32[]{:S(2)}, u32[]{:S(2)}) collective-permute-start(bf16[48,1024]{1,0:T(8,128)(2,1)S(1)} %get-tuple-element.248), channel_id=1, source_target_pairs={{0,5},{1,6},{2,7},{3,4},{4,1},{5,2},{6,3},{7,0},{8,13},{9,14},{10,... | collective-permute-start | bytes 294920 | tf_op jit(solution)/shard_map/ppermute | solution.py:358
  5.7 2.3 %collective-permute-start.4 = (bf16[48,1024]{1,0:T(8,128)(2,1)S(1)}, bf16[48,1024]{1,0:T(8,128)(2,1)S(1)}, u32[]{:S(2)}, u32[]{:S(2)}) collective-permute-start(bf16[48,1024]{1,0:T(8,128)(2,1)S(1)} %get-tuple-element.249), channel_id=1, source_target_pairs={{0,7},{1,4},{2,5},{3,6},{4,3},{5,0},{6,1},{7,2},{8,15},{9,12},{10,... | collective-permute-start | bytes 294920 | tf_op jit(solution)/shard_map/ppermute | solution.py:358
  8.0 2.6 %collective-permute-start.5 = (bf16[48,1024]{1,0:T(8,128)(2,1)S(1)}, bf16[48,1024]{1,0:T(8,128)(2,1)S(1)}, u32[]{:S(2)}, u32[]{:S(2)}) collective-permute-start(bf16[48,1024]{1,0:T(8,128)(2,1)S(1)} %get-tuple-element.250), channel_id=1, source_target_pairs={{0,6},{1,7},{2,4},{3,5},{4,2},{5,3},{6,0},{7,1},{8,14},{9,15},{10,... | collective-permute-start | bytes 294920 | tf_op jit(solution)/shard_map/ppermute | solution.py:358
  10.6 1.7 %collective-permute-start.6 = (bf16[48,1024]{1,0:T(8,128)(2,1)S(1)}, bf16[48,1024]{1,0:T(8,128)(2,1)S(1)}, u32[]{:S(2)}, u32[]{:S(2)}) collective-permute-start(bf16[48,1024]{1,0:T(8,128)(2,1)S(1)} %get-tuple-element.251), channel_id=1, source_target_pairs={{0,2},{1,3},{2,0},{3,1},{4,6},{5,7},{6,4},{7,5},{8,10},{9,11},{10,... | collective-permute-start | bytes 294920 | tf_op jit(solution)/shard_map/ppermute | solution.py:358
  12.3 0.5 collective-permute-done.3.refs_1_
  12.8 0.0 collective-permute-start.7
  12.8 0.0 collective-permute-done.4.refs_2_
  12.8 3.3 %collective-permute-start.8 = (bf16[48,1024]{1,0:T(8,128)(2,1)S(1)}, bf16[48,1024]{1,0:T(8,128)(2,1)S(1)}, u32[]{:S(2)}, u32[]{:S(2)}) collective-permute-start(bf16[48,1024]{1,0:T(8,128)(2,1)S(1)} %get-tuple-element.253), channel_id=1, source_target_pairs={{0,3},{1,0},{2,1},{3,2},{4,7},{5,4},{6,5},{7,6},{8,11},{9,8},{10,9... | collective-permute-start | bytes 294920 | tf_op jit(solution)/shard_map/ppermute | solution.py:358
  16.1 0.5 collective-permute-start.9
  16.6 0.0 collective-permute-done.5.refs_3_
  16.6 2.3 %collective-permute-done.6.refs_4_ = bf16[48,1024]{1,0:T(8,128)(2,1)S(1)} collective-permute-done((bf16[48,1024]{1,0:T(8,128)(2,1)S(1)}, bf16[48,1024]{1,0:T(8,128)(2,1)S(1)}, u32[]{:S(2)}, u32[]{:S(2)}) %collective-permute-start.6) | collective-permute-done | bytes 98336 | tf_op jit(solution)/shard_map/ppermute | solution.py:358
  18.9 2.0 %collective-permute-done.7.refs_5_ = bf16[48,1024]{1,0:T(8,128)(2,1)S(1)} collective-permute-done((bf16[48,1024]{1,0:T(8,128)(2,1)S(1)}, bf16[48,1024]{1,0:T(8,128)(2,1)S(1)}, u32[]{:S(2)}, u32[]{:S(2)}) %collective-permute-start.7) | collective-permute-done | bytes 98336 | tf_op jit(solution)/shard_map/ppermute | solution.py:358
  20.9 0.0 collective-permute-done.8.refs_6_
  20.9 0.0 collective-permute-done.9.refs_7_
  20.9 0.6 shard_map.31.refs_0_.refs_3_.refs_6_.refs_1_
  21.5 2.1 %collective-permute-start.13 = (bf16[352,1024]{1,0:T(8,128)(2,1)S(1)}, bf16[352,1024]{1,0:T(8,128)(2,1)S(1)}, u32[]{:S(2)}, u32[]{:S(2)}) collective-permute-start(bf16[352,1024]{1,0:T(8,128)(2,1)S(1)} %shard_map.31.refs_0_.refs_3_.refs_6_.refs_1_), channel_id=1, source_target_pairs={{0,8},{1,9},{2,10},{3,11},{4,12},{5,13},{6,14},{7,15},{8,0},{9,1},... | collective-permute-start | bytes 2162696 | tf_op jit(solution)/shard_map/ppermute | solution.py:358
  23.5 0.6 shard_map.33.refs_0_
  24.1 0.2 collective-permute-start.14
  24.3 1.6 %collective-permute-start.10 = (bf16[352,1024]{1,0:T(8,128)(2,1)S(1)}, bf16[352,1024]{1,0:T(8,128)(2,1)S(1)}, u32[]{:S(2)}, u32[]{:S(2)}) collective-permute-start(bf16[352,1024]{1,0:T(8,128)(2,1)S(1)} %shard_map.31.refs_0_.refs_3_.refs_6_.refs_1_), channel_id=1, source_target_pairs={{0,32},{1,33},{2,34},{3,35},{4,36},{5,37},{6,38},{7,39},{8,40},{9,... | collective-permute-start | bytes 2162696 | tf_op jit(solution)/shard_map/ppermute | solution.py:358
  25.9 1.7 %collective-permute-start.11 = (bf16[352,1024]{1,0:T(8,128)(2,1)S(1)}, bf16[352,1024]{1,0:T(8,128)(2,1)S(1)}, u32[]{:S(2)}, u32[]{:S(2)}) collective-permute-start(bf16[352,1024]{1,0:T(8,128)(2,1)S(1)} %shard_map.31.refs_0_.refs_3_.refs_6_.refs_1_), channel_id=1, source_target_pairs={{0,96},{1,97},{2,98},{3,99},{4,100},{5,101},{6,102},{7,103},{8,104... | collective-permute-start | bytes 2162696 | tf_op jit(solution)/shard_map/ppermute | solution.py:358
  27.6 3.1 %collective-permute-start.15 = (bf16[64,1024]{1,0:T(8,128)(2,1)S(1)}, bf16[64,1024]{1,0:T(8,128)(2,1)S(1)}, u32[]{:S(2)}, u32[]{:S(2)}) collective-permute-start(bf16[64,1024]{1,0:T(8,128)(2,1)S(1)} %shard_map.33.refs_0_), channel_id=1, source_target_pairs={{0,3},{1,0},{2,1},{3,2},{4,7},{5,4},{6,5},{7,6},{8,11},{9,8},{10,9... | collective-permute-start | bytes 393224 | tf_op jit(solution)/shard_map/ppermute | solution.py:358
  30.7 0.0 collective-permute-start.16
  30.7 3.9 %collective-permute-done.15.refs_2_ = bf16[64,1024]{1,0:T(8,128)(2,1)S(1)} collective-permute-done((bf16[64,1024]{1,0:T(8,128)(2,1)S(1)}, bf16[64,1024]{1,0:T(8,128)(2,1)S(1)}, u32[]{:S(2)}, u32[]{:S(2)}) %collective-permute-start.15) | collective-permute-done | bytes 131104 | tf_op jit(solution)/shard_map/ppermute | solution.py:358
  34.6 0.0 collective-permute-start.12
  34.6 2.5 %collective-permute-done.16.refs_3_ = bf16[64,1024]{1,0:T(8,128)(2,1)S(1)} collective-permute-done((bf16[64,1024]{1,0:T(8,128)(2,1)S(1)}, bf16[64,1024]{1,0:T(8,128)(2,1)S(1)}, u32[]{:S(2)}, u32[]{:S(2)}) %collective-permute-start.16) | collective-permute-done | bytes 131104 | tf_op jit(solution)/shard_map/ppermute | solution.py:358
  37.2 0.6 shard_map.34.refs_3_.refs_10_.refs_5_
  37.8 3.4 %collective-permute-done.13.refs_3_.refs_8_.refs_2_ = bf16[352,1024]{1,0:T(8,128)(2,1)S(1)} collective-permute-done((bf16[352,1024]{1,0:T(8,128)(2,1)S(1)}, bf16[352,1024]{1,0:T(8,128)(2,1)S(1)}, u32[]{:S(2)}, u32[]{:S(2)}) %collective-permute-start.13) | collective-permute-done | bytes 720928 | tf_op jit(solution)/shard_map/ppermute | solution.py:358
  41.2 0.1 pad_maximum_fusion
  41.3 0.1 collective-permute-start.17
  41.4 1.3 %collective-permute-done.10.refs_1_ = bf16[352,1024]{1,0:T(8,128)(2,1)S(1)} collective-permute-done((bf16[352,1024]{1,0:T(8,128)(2,1)S(1)}, bf16[352,1024]{1,0:T(8,128)(2,1)S(1)}, u32[]{:S(2)}, u32[]{:S(2)}) %collective-permute-start.10) | collective-permute-done | bytes 720928 | tf_op jit(solution)/shard_map/ppermute | solution.py:358
  42.7 0.1 pad_maximum_fusion.1
  42.8 1.6 %collective-permute-start.18 = (bf16[240,1024]{1,0:T(8,128)(2,1)S(1)}, bf16[240,1024]{1,0:T(8,128)(2,1)S(1)}, u32[]{:S(2)}, u32[]{:S(2)}) collective-permute-start(bf16[240,1024]{1,0:T(8,128)(2,1)S(1)} %get-tuple-element.322), channel_id=1, source_target_pairs={{0,32},{1,33},{2,34},{3,35},{4,36},{5,37},{6,38},{7,39},{8,40},{9,... | collective-permute-start | bytes 1474568 | tf_op jit(solution)/shard_map/ppermute | solution.py:358
  44.4 1.7 %collective-permute-start.19 = (bf16[240,1024]{1,0:T(8,128)(2,1)S(1)}, bf16[240,1024]{1,0:T(8,128)(2,1)S(1)}, u32[]{:S(2)}, u32[]{:S(2)}) collective-permute-start(bf16[240,1024]{1,0:T(8,128)(2,1)S(1)} %get-tuple-element.321), channel_id=1, source_target_pairs={{0,96},{1,97},{2,98},{3,99},{4,100},{5,101},{6,102},{7,103},{8,104... | collective-permute-start | bytes 1474568 | tf_op jit(solution)/shard_map/ppermute | solution.py:358
  46.1 2.7 %collective-permute-start.20 = (bf16[64,1024]{1,0:T(8,128)(2,1)S(1)}, bf16[64,1024]{1,0:T(8,128)(2,1)S(1)}, u32[]{:S(2)}, u32[]{:S(2)}) collective-permute-start(bf16[64,1024]{1,0:T(8,128)(2,1)S(1)} %shard_map.34.refs_3_.refs_10_.refs_5_), channel_id=1, source_target_pairs={{0,8},{1,9},{2,10},{3,11},{4,12},{5,13},{6,14},{7,15},{8,0},{9,1},... | collective-permute-start | bytes 393224 | tf_op jit(solution)/shard_map/ppermute | solution.py:358
  48.8 0.0 collective-permute-done.12.refs_4_.refs_7_.refs_1_.refs_2_
  48.8 2.4 %shard_map.32 = (f32[8,512]{1,0:T(8,128)S(1)}, f32[8,512]{1,0:T(8,128)S(1)}, f32[8,512]{1,0:T(8,128)S(1)}) custom-call(bf16[352,1024]{1,0:T(8,128)(2,1)S(1)} %shard_map.31.refs_0_.refs_3_.refs_6_.refs_1_, bf16[352,1024]{1,0:T(8,128)(2,1)S(1)} %collective-permute-done.10.refs_1_, bf16[352,1024]{1,0:T(8,128)(2,1)S(1)} %collective-permute-done.11.refs_2_, ...), custom_call_target="tpu_custom_call" | custom-call | flops 1522532352 | bytes 3604480 | tf_op jit(solution)/shard_map/pallas_call | solution.py:342
  51.3 2.4 %shard_map.35 = (f32[8,512]{1,0:T(8,128)S(1)}, f32[8,512]{1,0:T(8,128)S(1)}, f32[8,512]{1,0:T(8,128)S(1)}) custom-call(bf16[352,1024]{1,0:T(8,128)(2,1)S(1)} %shard_map.31.refs_0_.refs_3_.refs_6_.refs_1_, bf16[352,1024]{1,0:T(8,128)(2,1)S(1)} %collective-permute-done.10.refs_1_, bf16[352,1024]{1,0:T(8,128)(2,1)S(1)} %collective-permute-done.11.refs_2_, ...), custom_call_target="tpu_custom_call" | custom-call | flops 1522532352 | bytes 3604480 | tf_op jit(solution)/shard_map/pallas_call | solution.py:342
  53.7 0.0 collective-permute-done.20.refs_12_.refs_7_
  53.7 0.1 collective-permute-start.21
  53.8 2.7 %collective-permute-done.18 = bf16[240,1024]{1,0:T(8,128)(2,1)S(1)} collective-permute-done((bf16[240,1024]{1,0:T(8,128)(2,1)S(1)}, bf16[240,1024]{1,0:T(8,128)(2,1)S(1)}, u32[]{:S(2)}, u32[]{:S(2)}) %collective-permute-start.18) | collective-permute-done | bytes 491552 | tf_op jit(solution)/shard_map/ppermute | solution.py:358
  56.5 0.4 collective-permute-start.24
  56.9 0.0 collective-permute-done.19
  57.0 1.7 %shard_map.37 = f32[8,512]{1,0:T(8,128)S(1)} custom-call(bf16[176,1024]{1,0:T(8,128)(2,1)S(1)} %slice.51.upper_ref, bf16[176,1024]{1,0:T(8,128)(2,1)S(1)} %slice.52.lower_ref, bf16[352,1024]{1,0:T(8,128)(2,1)S(1)} %shard_map.31.refs_0_.refs_3_.refs_6_.refs_1_, bf16[352,1024]{1,0:T(8,128)(2,1)S(1)} %collective-permute-done.12.refs_4_.refs_7_.refs_1_.refs_2_, ...), custom_call_target="tpu_custom_call" | custom-call | flops 1015021568 | bytes 3604480 | tf_op jit(solution)/shard_map/pallas_call | solution.py:342
  58.7 2.0 %shard_map.36 = (f32[8,512]{1,0:T(8,128)S(1)}, f32[8,512]{1,0:T(8,128)S(1)}, f32[8,512]{1,0:T(8,128)S(1)}) custom-call(bf16[352,1024]{1,0:T(8,128)(2,1)S(1)} %shard_map.31.refs_0_.refs_3_.refs_6_.refs_1_, bf16[352,1024]{1,0:T(8,128)(2,1)S(1)} %collective-permute-done.10.refs_1_, bf16[352,1024]{1,0:T(8,128)(2,1)S(1)} %collective-permute-done.11.refs_2_, ...), custom_call_target="tpu_custom_call" | custom-call | flops 1268776960 | bytes 5963776 | tf_op jit(solution)/shard_map/pallas_call | solution.py:342
  60.7 1.6 %collective-permute-start.23 = (f32[8,512]{1,0:T(8,128)S(1)}, f32[8,512]{1,0:T(8,128)S(1)}, u32[]{:S(2)}, u32[]{:S(2)}) collective-permute-start(f32[8,512]{1,0:T(8,128)S(1)} %maximum_maximum_fusion.1), channel_id=1, source_target_pairs={{0,32},{1,33},{2,34},{3,35},{4,36},{5,37},{6,38},{7,39},{8,40},{9,... | collective-permute-start | bytes 49160 | tf_op jit(solution)/shard_map/ppermute | solution.py:358
  62.3 1.7 %collective-permute-start.22 = (f32[8,512]{1,0:T(8,128)S(1)}, f32[8,512]{1,0:T(8,128)S(1)}, u32[]{:S(2)}, u32[]{:S(2)}) collective-permute-start(f32[8,512]{1,0:T(8,128)S(1)} %maximum_maximum_fusion.2), channel_id=1, source_target_pairs={{0,96},{1,97},{2,98},{3,99},{4,100},{5,101},{6,102},{7,103},{8,104... | collective-permute-start | bytes 49160 | tf_op jit(solution)/shard_map/ppermute | solution.py:358
  64.0 0.0 collective-permute-done.24.refs_0_
  64.0 1.3 %shard_map.38 = f32[8,512]{1,0:T(8,128)S(1)} custom-call(bf16[176,1024]{1,0:T(8,128)(2,1)S(1)} %slice.51.upper_ref, bf16[176,1024]{1,0:T(8,128)(2,1)S(1)} %slice.52.lower_ref, bf16[64,1024]{1,0:T(8,128)(2,1)S(1)} %collective-permute-done.24.refs_0_, bf16[352,1024]{1,0:T(8,128)(2,1)S(1)} %shard_map.31.refs_0_.refs_3_.refs_6_.refs_1_, ...), custom_call_target="tpu_custom_call" | custom-call | flops 507510784 | bytes 4259840 | tf_op jit(solution)/shard_map/pallas_call | solution.py:342
  65.4 1.8 %collective-permute-start.25 = (f32[8,512]{1,0:T(8,128)S(1)}, f32[8,512]{1,0:T(8,128)S(1)}, u32[]{:S(2)}, u32[]{:S(2)}) collective-permute-start(f32[8,512]{1,0:T(8,128)S(1)} %max.48), channel_id=1, source_target_pairs={{0,64},{1,65},{2,66},{3,67},{4,68},{5,69},{6,70},{7,71},{8,72},{9,... | collective-permute-start | bytes 49160 | tf_op jit(solution)/shard_map/ppermute | solution.py:358
  67.1 3.5 %collective-permute-done.25 = f32[8,512]{1,0:T(8,128)S(1)} collective-permute-done((f32[8,512]{1,0:T(8,128)S(1)}, f32[8,512]{1,0:T(8,128)S(1)}, u32[]{:S(2)}, u32[]{:S(2)}) %collective-permute-start.25) | collective-permute-done | bytes 16416 | tf_op jit(solution)/shard_map/ppermute | solution.py:358
  70.7 1.9 %collective-permute-start.26 = (f32[8,512]{1,0:T(8,128)S(1)}, f32[8,512]{1,0:T(8,128)S(1)}, u32[]{:S(2)}, u32[]{:S(2)}) collective-permute-start(f32[8,512]{1,0:T(8,128)S(1)} %maximum_maximum_fusion.own_ref), channel_id=1, source_target_pairs={{0,4},{1,5},{2,6},{3,7},{4,0},{5,1},{6,2},{7,3},{8,12},{9,13},{10,... | collective-permute-start | bytes 49160 | tf_op jit(solution)/shard_map/ppermute | solution.py:358
  72.6 1.9 %collective-permute-done.26.side_ref = f32[8,512]{1,0:T(8,128)S(1)} collective-permute-done((f32[8,512]{1,0:T(8,128)S(1)}, f32[8,512]{1,0:T(8,128)S(1)}, u32[]{:S(2)}, u32[]{:S(2)}) %collective-permute-start.26) | collective-permute-done | bytes 16416 | tf_op jit(solution)/shard_map/ppermute | solution.py:358
  74.5 1.5 %collective-permute-start.27 = (f32[16,512]{1,0:T(8,128)S(1)}, f32[16,512]{1,0:T(8,128)S(1)}, u32[]{:S(2)}, u32[]{:S(2)}) collective-permute-start(f32[16,512]{1,0:T(8,128)S(1)} %pad_maximum_fusion.3), channel_id=1, source_target_pairs={{0,3},{1,0},{2,1},{3,2},{4,7},{5,4},{6,5},{7,6},{8,11},{9,8},{10,9... | collective-permute-start | bytes 98312 | tf_op jit(solution)/shard_map/ppermute | solution.py:358
  76.0 1.2 %collective-permute-start.28 = (f32[16,512]{1,0:T(8,128)S(1)}, f32[16,512]{1,0:T(8,128)S(1)}, u32[]{:S(2)}, u32[]{:S(2)}) collective-permute-start(f32[16,512]{1,0:T(8,128)S(1)} %pad_maximum_fusion.3), channel_id=1, source_target_pairs={{0,2},{1,3},{2,0},{3,1},{4,6},{5,7},{6,4},{7,5},{8,10},{9,11},{10,... | collective-permute-start | bytes 98312 | tf_op jit(solution)/shard_map/ppermute | solution.py:358
  77.3 0.7 collective-permute-start.29
  77.9 0.5 collective-permute-done.27.z1_ref
  78.4 3.0 %collective-permute-done.28.z2_ref = f32[16,512]{1,0:T(8,128)S(1)} collective-permute-done((f32[16,512]{1,0:T(8,128)S(1)}, f32[16,512]{1,0:T(8,128)S(1)}, u32[]{:S(2)}, u32[]{:S(2)}) %collective-permute-start.28) | collective-permute-done | bytes 32800 | tf_op jit(solution)/shard_map/ppermute | solution.py:358
  81.5 0.9 %collective-permute-done.29.z3_ref = f32[16,512]{1,0:T(8,128)S(1)} collective-permute-done((f32[16,512]{1,0:T(8,128)S(1)}, f32[16,512]{1,0:T(8,128)S(1)}, u32[]{:S(2)}, u32[]{:S(2)}) %collective-permute-start.29) | collective-permute-done | bytes 32800 | tf_op jit(solution)/shard_map/ppermute | solution.py:358
  82.4 0.7 shard_map.39
  83.2 0.0 copy-start.1
  83.2 0.6 copy-done.1
  (23 shorter events, 0.2 us)
Async XLA Ops:
  2.2 13.9 %collective-permute-start.2 = (bf16[64,1024]{1,0:T(8,128)(2,1)S(1)}, bf16[64,1024]{1,0:T(8,128)(2,1)S(1)}, u32[]{:S(2)}, u32[]{:S(2)}) collective-permute-start(bf16[64,1024]{1,0:T(8,128)(2,1)S(1)} %get-tuple-element.246.own_ref), channel_id=1, source_target_pairs={{0,4},{1,5},{2,6},{3,7},{4,0},{5,1},{6,2},{7,3},{8,12},{9,13},{10,... | collective-permute-start | bytes 393224 | tf_op jit(solution)/shard_map/ppermute | solution.py:358
  3.8 9.0 %collective-permute-start.3 = (bf16[48,1024]{1,0:T(8,128)(2,1)S(1)}, bf16[48,1024]{1,0:T(8,128)(2,1)S(1)}, u32[]{:S(2)}, u32[]{:S(2)}) collective-permute-start(bf16[48,1024]{1,0:T(8,128)(2,1)S(1)} %get-tuple-element.248), channel_id=1, source_target_pairs={{0,5},{1,6},{2,7},{3,4},{4,1},{5,2},{6,3},{7,0},{8,13},{9,14},{10,... | collective-permute-start | bytes 294920 | tf_op jit(solution)/shard_map/ppermute | solution.py:358
  5.7 7.1 %collective-permute-start.4 = (bf16[48,1024]{1,0:T(8,128)(2,1)S(1)}, bf16[48,1024]{1,0:T(8,128)(2,1)S(1)}, u32[]{:S(2)}, u32[]{:S(2)}) collective-permute-start(bf16[48,1024]{1,0:T(8,128)(2,1)S(1)} %get-tuple-element.249), channel_id=1, source_target_pairs={{0,7},{1,4},{2,5},{3,6},{4,3},{5,0},{6,1},{7,2},{8,15},{9,12},{10,... | collective-permute-start | bytes 294920 | tf_op jit(solution)/shard_map/ppermute | solution.py:358
  8.0 8.6 %collective-permute-start.5 = (bf16[48,1024]{1,0:T(8,128)(2,1)S(1)}, bf16[48,1024]{1,0:T(8,128)(2,1)S(1)}, u32[]{:S(2)}, u32[]{:S(2)}) collective-permute-start(bf16[48,1024]{1,0:T(8,128)(2,1)S(1)} %get-tuple-element.250), channel_id=1, source_target_pairs={{0,6},{1,7},{2,4},{3,5},{4,2},{5,3},{6,0},{7,1},{8,14},{9,15},{10,... | collective-permute-start | bytes 294920 | tf_op jit(solution)/shard_map/ppermute | solution.py:358
  10.6 8.3 %collective-permute-start.6 = (bf16[48,1024]{1,0:T(8,128)(2,1)S(1)}, bf16[48,1024]{1,0:T(8,128)(2,1)S(1)}, u32[]{:S(2)}, u32[]{:S(2)}) collective-permute-start(bf16[48,1024]{1,0:T(8,128)(2,1)S(1)} %get-tuple-element.251), channel_id=1, source_target_pairs={{0,2},{1,3},{2,0},{3,1},{4,6},{5,7},{6,4},{7,5},{8,10},{9,11},{10,... | collective-permute-start | bytes 294920 | tf_op jit(solution)/shard_map/ppermute | solution.py:358
  12.8 8.1 %collective-permute-start.7 = (bf16[48,1024]{1,0:T(8,128)(2,1)S(1)}, bf16[48,1024]{1,0:T(8,128)(2,1)S(1)}, u32[]{:S(2)}, u32[]{:S(2)}) collective-permute-start(bf16[48,1024]{1,0:T(8,128)(2,1)S(1)} %get-tuple-element.252), channel_id=1, source_target_pairs={{0,1},{1,2},{2,3},{3,0},{4,5},{5,6},{6,7},{7,4},{8,9},{9,10},{10,1... | collective-permute-start | bytes 294920 | tf_op jit(solution)/shard_map/ppermute | solution.py:358
  12.8 8.1 %collective-permute-start.8 = (bf16[48,1024]{1,0:T(8,128)(2,1)S(1)}, bf16[48,1024]{1,0:T(8,128)(2,1)S(1)}, u32[]{:S(2)}, u32[]{:S(2)}) collective-permute-start(bf16[48,1024]{1,0:T(8,128)(2,1)S(1)} %get-tuple-element.253), channel_id=1, source_target_pairs={{0,3},{1,0},{2,1},{3,2},{4,7},{5,4},{6,5},{7,6},{8,11},{9,8},{10,9... | collective-permute-start | bytes 294920 | tf_op jit(solution)/shard_map/ppermute | solution.py:358
  16.1 4.8 %collective-permute-start.9 = (bf16[48,1024]{1,0:T(8,128)(2,1)S(1)}, bf16[48,1024]{1,0:T(8,128)(2,1)S(1)}, u32[]{:S(2)}, u32[]{:S(2)}) collective-permute-start(bf16[48,1024]{1,0:T(8,128)(2,1)S(1)} %get-tuple-element.254), channel_id=1, source_target_pairs={{0,4},{1,5},{2,6},{3,7},{4,0},{5,1},{6,2},{7,3},{8,12},{9,13},{10,... | collective-permute-start | bytes 294920 | tf_op jit(solution)/shard_map/ppermute | solution.py:358
  21.5 19.7 %collective-permute-start.13 = (bf16[352,1024]{1,0:T(8,128)(2,1)S(1)}, bf16[352,1024]{1,0:T(8,128)(2,1)S(1)}, u32[]{:S(2)}, u32[]{:S(2)}) collective-permute-start(bf16[352,1024]{1,0:T(8,128)(2,1)S(1)} %shard_map.31.refs_0_.refs_3_.refs_6_.refs_1_), channel_id=1, source_target_pairs={{0,8},{1,9},{2,10},{3,11},{4,12},{5,13},{6,14},{7,15},{8,0},{9,1},... | collective-permute-start | bytes 2162696 | tf_op jit(solution)/shard_map/ppermute | solution.py:358
  24.1 6.5 %collective-permute-start.14 = (bf16[64,1024]{1,0:T(8,128)(2,1)S(1)}, bf16[64,1024]{1,0:T(8,128)(2,1)S(1)}, u32[]{:S(2)}, u32[]{:S(2)}) collective-permute-start(bf16[64,1024]{1,0:T(8,128)(2,1)S(1)} %shard_map.33.refs_0_), channel_id=1, source_target_pairs={{0,1},{1,2},{2,3},{3,0},{4,5},{5,6},{6,7},{7,4},{8,9},{9,10},{10,1... | collective-permute-start | bytes 393224 | tf_op jit(solution)/shard_map/ppermute | solution.py:358
  24.3 18.3 %collective-permute-start.10 = (bf16[352,1024]{1,0:T(8,128)(2,1)S(1)}, bf16[352,1024]{1,0:T(8,128)(2,1)S(1)}, u32[]{:S(2)}, u32[]{:S(2)}) collective-permute-start(bf16[352,1024]{1,0:T(8,128)(2,1)S(1)} %shard_map.31.refs_0_.refs_3_.refs_6_.refs_1_), channel_id=1, source_target_pairs={{0,32},{1,33},{2,34},{3,35},{4,36},{5,37},{6,38},{7,39},{8,40},{9,... | collective-permute-start | bytes 2162696 | tf_op jit(solution)/shard_map/ppermute | solution.py:358
  25.9 16.8 %collective-permute-start.11 = (bf16[352,1024]{1,0:T(8,128)(2,1)S(1)}, bf16[352,1024]{1,0:T(8,128)(2,1)S(1)}, u32[]{:S(2)}, u32[]{:S(2)}) collective-permute-start(bf16[352,1024]{1,0:T(8,128)(2,1)S(1)} %shard_map.31.refs_0_.refs_3_.refs_6_.refs_1_), channel_id=1, source_target_pairs={{0,96},{1,97},{2,98},{3,99},{4,100},{5,101},{6,102},{7,103},{8,104... | collective-permute-start | bytes 2162696 | tf_op jit(solution)/shard_map/ppermute | solution.py:358
  27.6 7.0 %collective-permute-start.15 = (bf16[64,1024]{1,0:T(8,128)(2,1)S(1)}, bf16[64,1024]{1,0:T(8,128)(2,1)S(1)}, u32[]{:S(2)}, u32[]{:S(2)}) collective-permute-start(bf16[64,1024]{1,0:T(8,128)(2,1)S(1)} %shard_map.33.refs_0_), channel_id=1, source_target_pairs={{0,3},{1,0},{2,1},{3,2},{4,7},{5,4},{6,5},{7,6},{8,11},{9,8},{10,9... | collective-permute-start | bytes 393224 | tf_op jit(solution)/shard_map/ppermute | solution.py:358
  30.7 6.5 %collective-permute-start.16 = (bf16[64,1024]{1,0:T(8,128)(2,1)S(1)}, bf16[64,1024]{1,0:T(8,128)(2,1)S(1)}, u32[]{:S(2)}, u32[]{:S(2)}) collective-permute-start(bf16[64,1024]{1,0:T(8,128)(2,1)S(1)} %shard_map.33.refs_0_), channel_id=1, source_target_pairs={{0,2},{1,3},{2,0},{3,1},{4,6},{5,7},{6,4},{7,5},{8,10},{9,11},{10,... | collective-permute-start | bytes 393224 | tf_op jit(solution)/shard_map/ppermute | solution.py:358
  34.6 14.2 %collective-permute-start.12 = (bf16[352,1024]{1,0:T(8,128)(2,1)S(1)}, bf16[352,1024]{1,0:T(8,128)(2,1)S(1)}, u32[]{:S(2)}, u32[]{:S(2)}) collective-permute-start(bf16[352,1024]{1,0:T(8,128)(2,1)S(1)} %shard_map.31.refs_0_.refs_3_.refs_6_.refs_1_), channel_id=1, source_target_pairs={{0,16},{1,17},{2,18},{3,19},{4,20},{5,21},{6,22},{7,23},{8,24},{9,... | collective-permute-start | bytes 2162696 | tf_op jit(solution)/shard_map/ppermute | solution.py:358
  41.3 9.9 %collective-permute-start.17 = (bf16[416,1024]{1,0:T(8,128)(2,1)S(1)}, bf16[416,1024]{1,0:T(8,128)(2,1)S(1)}, u32[]{:S(2)}, u32[]{:S(2)}) collective-permute-start(bf16[416,1024]{1,0:T(8,128)(2,1)S(1)} %pad_maximum_fusion), channel_id=1, source_target_pairs={{0,16},{1,17},{2,18},{3,19},{4,20},{5,21},{6,22},{7,23},{8,24},{9,... | collective-permute-start | bytes 2555912 | tf_op jit(solution)/shard_map/ppermute | solution.py:358
  42.8 13.7 %collective-permute-start.18 = (bf16[240,1024]{1,0:T(8,128)(2,1)S(1)}, bf16[240,1024]{1,0:T(8,128)(2,1)S(1)}, u32[]{:S(2)}, u32[]{:S(2)}) collective-permute-start(bf16[240,1024]{1,0:T(8,128)(2,1)S(1)} %get-tuple-element.322), channel_id=1, source_target_pairs={{0,32},{1,33},{2,34},{3,35},{4,36},{5,37},{6,38},{7,39},{8,40},{9,... | collective-permute-start | bytes 1474568 | tf_op jit(solution)/shard_map/ppermute | solution.py:358
  44.4 12.5 %collective-permute-start.19 = (bf16[240,1024]{1,0:T(8,128)(2,1)S(1)}, bf16[240,1024]{1,0:T(8,128)(2,1)S(1)}, u32[]{:S(2)}, u32[]{:S(2)}) collective-permute-start(bf16[240,1024]{1,0:T(8,128)(2,1)S(1)} %get-tuple-element.321), channel_id=1, source_target_pairs={{0,96},{1,97},{2,98},{3,99},{4,100},{5,101},{6,102},{7,103},{8,104... | collective-permute-start | bytes 1474568 | tf_op jit(solution)/shard_map/ppermute | solution.py:358
  46.1 7.6 %collective-permute-start.20 = (bf16[64,1024]{1,0:T(8,128)(2,1)S(1)}, bf16[64,1024]{1,0:T(8,128)(2,1)S(1)}, u32[]{:S(2)}, u32[]{:S(2)}) collective-permute-start(bf16[64,1024]{1,0:T(8,128)(2,1)S(1)} %shard_map.34.refs_3_.refs_10_.refs_5_), channel_id=1, source_target_pairs={{0,8},{1,9},{2,10},{3,11},{4,12},{5,13},{6,14},{7,15},{8,0},{9,1},... | collective-permute-start | bytes 393224 | tf_op jit(solution)/shard_map/ppermute | solution.py:358
  53.7 5.0 %collective-permute-start.21 = (bf16[64,1024]{1,0:T(8,128)(2,1)S(1)}, bf16[64,1024]{1,0:T(8,128)(2,1)S(1)}, u32[]{:S(2)}, u32[]{:S(2)}) collective-permute-start(bf16[64,1024]{1,0:T(8,128)(2,1)S(1)} %collective-permute-done.20.refs_12_.refs_7_), channel_id=1, source_target_pairs={{0,16},{1,17},{2,18},{3,19},{4,20},{5,21},{6,22},{7,23},{8,24},{9,... | collective-permute-start | bytes 393224 | tf_op jit(solution)/shard_map/ppermute | solution.py:358
  56.5 7.5 %collective-permute-start.24 = (bf16[64,1024]{1,0:T(8,128)(2,1)S(1)}, bf16[64,1024]{1,0:T(8,128)(2,1)S(1)}, u32[]{:S(2)}, u32[]{:S(2)}) collective-permute-start(bf16[64,1024]{1,0:T(8,128)(2,1)S(1)} %slice.47.refs_4_), channel_id=1, source_target_pairs={{0,32},{1,33},{2,34},{3,35},{4,36},{5,37},{6,38},{7,39},{8,40},{9,... | collective-permute-start | bytes 393224 | tf_op jit(solution)/shard_map/ppermute | solution.py:358
  60.7 6.5 %collective-permute-start.23 = (f32[8,512]{1,0:T(8,128)S(1)}, f32[8,512]{1,0:T(8,128)S(1)}, u32[]{:S(2)}, u32[]{:S(2)}) collective-permute-start(f32[8,512]{1,0:T(8,128)S(1)} %maximum_maximum_fusion.1), channel_id=1, source_target_pairs={{0,32},{1,33},{2,34},{3,35},{4,36},{5,37},{6,38},{7,39},{8,40},{9,... | collective-permute-start | bytes 49160 | tf_op jit(solution)/shard_map/ppermute | solution.py:358
  62.3 20.9 %copy-start = (s32[384]{0:T(512)S(1)}, s32[384]{0:T(512)}, u32[]{:S(2)}) copy-start(s32[384]{0:T(512)} %ids_ref.1) | copy-start | bytes 4612
  62.3 4.9 %collective-permute-start.22 = (f32[8,512]{1,0:T(8,128)S(1)}, f32[8,512]{1,0:T(8,128)S(1)}, u32[]{:S(2)}, u32[]{:S(2)}) collective-permute-start(f32[8,512]{1,0:T(8,128)S(1)} %maximum_maximum_fusion.2), channel_id=1, source_target_pairs={{0,96},{1,97},{2,98},{3,99},{4,100},{5,101},{6,102},{7,103},{8,104... | collective-permute-start | bytes 49160 | tf_op jit(solution)/shard_map/ppermute | solution.py:358
  65.4 5.3 %collective-permute-start.25 = (f32[8,512]{1,0:T(8,128)S(1)}, f32[8,512]{1,0:T(8,128)S(1)}, u32[]{:S(2)}, u32[]{:S(2)}) collective-permute-start(f32[8,512]{1,0:T(8,128)S(1)} %max.48), channel_id=1, source_target_pairs={{0,64},{1,65},{2,66},{3,67},{4,68},{5,69},{6,70},{7,71},{8,72},{9,... | collective-permute-start | bytes 49160 | tf_op jit(solution)/shard_map/ppermute | solution.py:358
  70.7 3.8 %collective-permute-start.26 = (f32[8,512]{1,0:T(8,128)S(1)}, f32[8,512]{1,0:T(8,128)S(1)}, u32[]{:S(2)}, u32[]{:S(2)}) collective-permute-start(f32[8,512]{1,0:T(8,128)S(1)} %maximum_maximum_fusion.own_ref), channel_id=1, source_target_pairs={{0,4},{1,5},{2,6},{3,7},{4,0},{5,1},{6,2},{7,3},{8,12},{9,13},{10,... | collective-permute-start | bytes 49160 | tf_op jit(solution)/shard_map/ppermute | solution.py:358
  74.5 3.9 %collective-permute-start.27 = (f32[16,512]{1,0:T(8,128)S(1)}, f32[16,512]{1,0:T(8,128)S(1)}, u32[]{:S(2)}, u32[]{:S(2)}) collective-permute-start(f32[16,512]{1,0:T(8,128)S(1)} %pad_maximum_fusion.3), channel_id=1, source_target_pairs={{0,3},{1,0},{2,1},{3,2},{4,7},{5,4},{6,5},{7,6},{8,11},{9,8},{10,9... | collective-permute-start | bytes 98312 | tf_op jit(solution)/shard_map/ppermute | solution.py:358
  76.0 5.4 %collective-permute-start.28 = (f32[16,512]{1,0:T(8,128)S(1)}, f32[16,512]{1,0:T(8,128)S(1)}, u32[]{:S(2)}, u32[]{:S(2)}) collective-permute-start(f32[16,512]{1,0:T(8,128)S(1)} %pad_maximum_fusion.3), channel_id=1, source_target_pairs={{0,2},{1,3},{2,0},{3,1},{4,6},{5,7},{6,4},{7,5},{8,10},{9,11},{10,... | collective-permute-start | bytes 98312 | tf_op jit(solution)/shard_map/ppermute | solution.py:358
  77.3 5.1 %collective-permute-start.29 = (f32[16,512]{1,0:T(8,128)S(1)}, f32[16,512]{1,0:T(8,128)S(1)}, u32[]{:S(2)}, u32[]{:S(2)}) collective-permute-start(f32[16,512]{1,0:T(8,128)S(1)} %pad_maximum_fusion.3), channel_id=1, source_target_pairs={{0,1},{1,2},{2,3},{3,0},{4,5},{5,6},{6,7},{7,4},{8,9},{9,10},{10,1... | collective-permute-start | bytes 98312 | tf_op jit(solution)/shard_map/ppermute | solution.py:358
  83.2 0.6 copy-start.1

commit v4 on v3

--- a/solution.py
+++ b/solution.py
@@ -424,7 +424,7 @@
     from_sibling = along(join(across, extra), to_sibling)
     below_extra, above_extra, sibling_extra = from_lower[UPPER:], from_upper[UPPER:], from_sibling[BLOCK:]
     across_sibling = from_sibling[:BLOCK]
-    far, far_extra = (from_lower[:UPPER], from_upper[:UPPER]), along(below_extra, to_y(1))
+    far, far_extra = (from_lower[:UPPER], from_upper[:UPPER]), along(extra, to_y(2))
     vector = shape((8, LANES), f32)
     flops = 2 * BLOCK * BLOCK * width
     blocks, rights = (block, below, above), (block, sibling, across, across_sibling)

time: 84.2 us -> 84.1 us (level)
  waiting for transfers between devices: 28.7 us -> 26.8 us
  starting transfers between devices: 39.4 us -> 41 us
    ppermute x28, waiting for transfers between devices: 28.7 us -> 26.8 us  [along(): lax.ppermute(value, ('grp', 'sub'), [(index(*place), index(*move(*place))...]
    ppermute x28, starting transfers between devices: 39.4 us -> 41 us  [along(): lax.ppermute(value, ('grp', 'sub'), [(index(*place), index(*move(*place))...]
where the time goes in v4:
time: 84.1 us; the launch traced here: 83.5 us
  starting transfers between devices  41 us (49%)
  waiting for transfers between devices  26.8 us (32%)
  Pallas kernels  14.5 us (17%)
    ppermute x28, starting transfers between devices, along(): lax.ppermute(value, ('grp', 'sub'), [(index(*place), index(*move(*place))...  41 us
    ppermute x28, waiting for transfers between devices, along(): lax.ppermute(value, ('grp', 'sub'), [(index(*place), index(*move(*place))...  26.8 us
    pallas_call x10, Pallas kernels, call(): pl.pallas_call(kernel, out_shape=outs, in_specs=[SMEM] * scalars + [VMEM]...  14.5 us
  transfers between devices with their start and end apart: 28, of which 13 were waited for; matrix products, arithmetic and copies ran while one was open for 0% of the time, Pallas kernels for 13%

profile of v4, /device:TPU:0, one launch (start us, length us, event | category | flops | bytes accessed | tf_op | source)
XLA Modules:
  0.0 83.5 jit_solution(5936364831822586201)
XLA Ops:
  0.0 0.1 pad_add_fusion.at_ref
  0.1 2.1 %shard_map.30 = (bf16[48,1024]{1,0:T(8,128)(2,1)S(1)}, bf16[48,1024]{1,0:T(8,128)(2,1)S(1)}, bf16[48,1024]{1,0:T(8,128)(2,1)S(1)}, bf16[48,1024]{1,0:T(8,128)(2,...) custom-call(s32[2]{0:T(128)S(1)} %pad_add_fusion.at_ref, ...), custom_call_target="tpu_custom_call" | custom-call | flops 500000000 | bytes 787976 | tf_op jit(solution)/shard_map/pallas_call | solution.py:342
  2.2 1.7 %collective-permute-start.2 = (bf16[64,1024]{1,0:T(8,128)(2,1)S(1)}, bf16[64,1024]{1,0:T(8,128)(2,1)S(1)}, u32[]{:S(2)}, u32[]{:S(2)}) collective-permute-start(bf16[64,1024]{1,0:T(8,128)(2,1)S(1)} %get-tuple-element.246.own_ref), channel_id=1, source_target_pairs={{0,4},{1,5},{2,6},{3,7},{4,0},{5,1},{6,2},{7,3},{8,12},{9,13},{10,... | collective-permute-start | bytes 393224 | tf_op jit(solution)/shard_map/ppermute | solution.py:358
  3.8 1.9 %collective-permute-start.3 = (bf16[48,1024]{1,0:T(8,128)(2,1)S(1)}, bf16[48,1024]{1,0:T(8,128)(2,1)S(1)}, u32[]{:S(2)}, u32[]{:S(2)}) collective-permute-start(bf16[48,1024]{1,0:T(8,128)(2,1)S(1)} %get-tuple-element.248), channel_id=1, source_target_pairs={{0,5},{1,6},{2,7},{3,4},{4,1},{5,2},{6,3},{7,0},{8,13},{9,14},{10,... | collective-permute-start | bytes 294920 | tf_op jit(solution)/shard_map/ppermute | solution.py:358
  5.7 2.3 %collective-permute-start.4 = (bf16[48,1024]{1,0:T(8,128)(2,1)S(1)}, bf16[48,1024]{1,0:T(8,128)(2,1)S(1)}, u32[]{:S(2)}, u32[]{:S(2)}) collective-permute-start(bf16[48,1024]{1,0:T(8,128)(2,1)S(1)} %get-tuple-element.249), channel_id=1, source_target_pairs={{0,7},{1,4},{2,5},{3,6},{4,3},{5,0},{6,1},{7,2},{8,15},{9,12},{10,... | collective-permute-start | bytes 294920 | tf_op jit(solution)/shard_map/ppermute | solution.py:358
  8.0 2.6 %collective-permute-start.5 = (bf16[48,1024]{1,0:T(8,128)(2,1)S(1)}, bf16[48,1024]{1,0:T(8,128)(2,1)S(1)}, u32[]{:S(2)}, u32[]{:S(2)}) collective-permute-start(bf16[48,1024]{1,0:T(8,128)(2,1)S(1)} %get-tuple-element.250), channel_id=1, source_target_pairs={{0,6},{1,7},{2,4},{3,5},{4,2},{5,3},{6,0},{7,1},{8,14},{9,15},{10,... | collective-permute-start | bytes 294920 | tf_op jit(solution)/shard_map/ppermute | solution.py:358
  10.6 1.7 %collective-permute-start.6 = (bf16[48,1024]{1,0:T(8,128)(2,1)S(1)}, bf16[48,1024]{1,0:T(8,128)(2,1)S(1)}, u32[]{:S(2)}, u32[]{:S(2)}) collective-permute-start(bf16[48,1024]{1,0:T(8,128)(2,1)S(1)} %get-tuple-element.251), channel_id=1, source_target_pairs={{0,2},{1,3},{2,0},{3,1},{4,6},{5,7},{6,4},{7,5},{8,10},{9,11},{10,... | collective-permute-start | bytes 294920 | tf_op jit(solution)/shard_map/ppermute | solution.py:358
  12.3 0.5 collective-permute-done.3.refs_1_
  12.8 0.0 collective-permute-start.7
  12.8 0.0 collective-permute-done.4.refs_2_
  12.8 3.3 %collective-permute-start.8 = (bf16[48,1024]{1,0:T(8,128)(2,1)S(1)}, bf16[48,1024]{1,0:T(8,128)(2,1)S(1)}, u32[]{:S(2)}, u32[]{:S(2)}) collective-permute-start(bf16[48,1024]{1,0:T(8,128)(2,1)S(1)} %get-tuple-element.253), channel_id=1, source_target_pairs={{0,3},{1,0},{2,1},{3,2},{4,7},{5,4},{6,5},{7,6},{8,11},{9,8},{10,9... | collective-permute-start | bytes 294920 | tf_op jit(solution)/shard_map/ppermute | solution.py:358
  16.1 0.0 collective-permute-done.2.other_ref
  16.1 0.5 collective-permute-start.9
  16.6 0.0 collective-permute-done.5.refs_3_
  16.6 2.3 %collective-permute-done.6.refs_4_ = bf16[48,1024]{1,0:T(8,128)(2,1)S(1)} collective-permute-done((bf16[48,1024]{1,0:T(8,128)(2,1)S(1)}, bf16[48,1024]{1,0:T(8,128)(2,1)S(1)}, u32[]{:S(2)}, u32[]{:S(2)}) %collective-permute-start.6) | collective-permute-done | bytes 98336 | tf_op jit(solution)/shard_map/ppermute | solution.py:358
  18.9 2.0 %collective-permute-done.7.refs_5_ = bf16[48,1024]{1,0:T(8,128)(2,1)S(1)} collective-permute-done((bf16[48,1024]{1,0:T(8,128)(2,1)S(1)}, bf16[48,1024]{1,0:T(8,128)(2,1)S(1)}, u32[]{:S(2)}, u32[]{:S(2)}) %collective-permute-start.7) | collective-permute-done | bytes 98336 | tf_op jit(solution)/shard_map/ppermute | solution.py:358
  20.9 0.0 collective-permute-done.8.refs_6_
  20.9 0.0 collective-permute-done.9.refs_7_
  20.9 0.6 shard_map.31.refs_0_.refs_3_.refs_6_.refs_1_
  21.5 2.1 %collective-permute-start.13 = (bf16[352,1024]{1,0:T(8,128)(2,1)S(1)}, bf16[352,1024]{1,0:T(8,128)(2,1)S(1)}, u32[]{:S(2)}, u32[]{:S(2)}) collective-permute-start(bf16[352,1024]{1,0:T(8,128)(2,1)S(1)} %shard_map.31.refs_0_.refs_3_.refs_6_.refs_1_), channel_id=1, source_target_pairs={{0,8},{1,9},{2,10},{3,11},{4,12},{5,13},{6,14},{7,15},{8,0},{9,1},... | collective-permute-start | bytes 2162696 | tf_op jit(solution)/shard_map/ppermute | solution.py:358
  23.5 0.6 shard_map.33.refs_0_
  24.1 0.2 collective-permute-start.14
  24.3 1.6 %collective-permute-start.10 = (bf16[352,1024]{1,0:T(8,128)(2,1)S(1)}, bf16[352,1024]{1,0:T(8,128)(2,1)S(1)}, u32[]{:S(2)}, u32[]{:S(2)}) collective-permute-start(bf16[352,1024]{1,0:T(8,128)(2,1)S(1)} %shard_map.31.refs_0_.refs_3_.refs_6_.refs_1_), channel_id=1, source_target_pairs={{0,32},{1,33},{2,34},{3,35},{4,36},{5,37},{6,38},{7,39},{8,40},{9,... | collective-permute-start | bytes 2162696 | tf_op jit(solution)/shard_map/ppermute | solution.py:358
  25.9 1.7 %collective-permute-start.11 = (bf16[352,1024]{1,0:T(8,128)(2,1)S(1)}, bf16[352,1024]{1,0:T(8,128)(2,1)S(1)}, u32[]{:S(2)}, u32[]{:S(2)}) collective-permute-start(bf16[352,1024]{1,0:T(8,128)(2,1)S(1)} %shard_map.31.refs_0_.refs_3_.refs_6_.refs_1_), channel_id=1, source_target_pairs={{0,96},{1,97},{2,98},{3,99},{4,100},{5,101},{6,102},{7,103},{8,104... | collective-permute-start | bytes 2162696 | tf_op jit(solution)/shard_map/ppermute | solution.py:358
  27.6 3.1 %collective-permute-start.15 = (bf16[64,1024]{1,0:T(8,128)(2,1)S(1)}, bf16[64,1024]{1,0:T(8,128)(2,1)S(1)}, u32[]{:S(2)}, u32[]{:S(2)}) collective-permute-start(bf16[64,1024]{1,0:T(8,128)(2,1)S(1)} %shard_map.33.refs_0_), channel_id=1, source_target_pairs={{0,3},{1,0},{2,1},{3,2},{4,7},{5,4},{6,5},{7,6},{8,11},{9,8},{10,9... | collective-permute-start | bytes 393224 | tf_op jit(solution)/shard_map/ppermute | solution.py:358
  30.7 0.0 collective-permute-done.14.refs_1_
  30.7 0.0 collective-permute-start.16
  30.7 3.9 %collective-permute-done.15.refs_2_ = bf16[64,1024]{1,0:T(8,128)(2,1)S(1)} collective-permute-done((bf16[64,1024]{1,0:T(8,128)(2,1)S(1)}, bf16[64,1024]{1,0:T(8,128)(2,1)S(1)}, u32[]{:S(2)}, u32[]{:S(2)}) %collective-permute-start.15) | collective-permute-done | bytes 131104 | tf_op jit(solution)/shard_map/ppermute | solution.py:358
  34.6 2.5 %collective-permute-done.16.refs_3_ = bf16[64,1024]{1,0:T(8,128)(2,1)S(1)} collective-permute-done((bf16[64,1024]{1,0:T(8,128)(2,1)S(1)}, bf16[64,1024]{1,0:T(8,128)(2,1)S(1)}, u32[]{:S(2)}, u32[]{:S(2)}) %collective-permute-start.16) | collective-permute-done | bytes 131104 | tf_op jit(solution)/shard_map/ppermute | solution.py:358
  37.2 0.6 shard_map.34.refs_3_.refs_10_.refs_5_
  37.8 3.4 %collective-permute-done.13.refs_3_.refs_8_.refs_2_ = bf16[352,1024]{1,0:T(8,128)(2,1)S(1)} collective-permute-done((bf16[352,1024]{1,0:T(8,128)(2,1)S(1)}, bf16[352,1024]{1,0:T(8,128)(2,1)S(1)}, u32[]{:S(2)}, u32[]{:S(2)}) %collective-permute-start.13) | collective-permute-done | bytes 720928 | tf_op jit(solution)/shard_map/ppermute | solution.py:358
  41.2 0.1 pad_maximum_fusion
  41.3 0.1 collective-permute-start.17
  41.4 1.3 %collective-permute-done.10.refs_1_ = bf16[352,1024]{1,0:T(8,128)(2,1)S(1)} collective-permute-done((bf16[352,1024]{1,0:T(8,128)(2,1)S(1)}, bf16[352,1024]{1,0:T(8,128)(2,1)S(1)}, u32[]{:S(2)}, u32[]{:S(2)}) %collective-permute-start.10) | collective-permute-done | bytes 720928 | tf_op jit(solution)/shard_map/ppermute | solution.py:358
  42.7 0.1 pad_maximum_fusion.1
  42.8 1.6 %collective-permute-start.18 = (bf16[240,1024]{1,0:T(8,128)(2,1)S(1)}, bf16[240,1024]{1,0:T(8,128)(2,1)S(1)}, u32[]{:S(2)}, u32[]{:S(2)}) collective-permute-start(bf16[240,1024]{1,0:T(8,128)(2,1)S(1)} %get-tuple-element.322), channel_id=1, source_target_pairs={{0,32},{1,33},{2,34},{3,35},{4,36},{5,37},{6,38},{7,39},{8,40},{9,... | collective-permute-start | bytes 1474568 | tf_op jit(solution)/shard_map/ppermute | solution.py:358
  44.4 1.7 %collective-permute-start.19 = (bf16[240,1024]{1,0:T(8,128)(2,1)S(1)}, bf16[240,1024]{1,0:T(8,128)(2,1)S(1)}, u32[]{:S(2)}, u32[]{:S(2)}) collective-permute-start(bf16[240,1024]{1,0:T(8,128)(2,1)S(1)} %get-tuple-element.321), channel_id=1, source_target_pairs={{0,96},{1,97},{2,98},{3,99},{4,100},{5,101},{6,102},{7,103},{8,104... | collective-permute-start | bytes 1474568 | tf_op jit(solution)/shard_map/ppermute | solution.py:358
  46.1 2.7 %collective-permute-start.20 = (bf16[64,1024]{1,0:T(8,128)(2,1)S(1)}, bf16[64,1024]{1,0:T(8,128)(2,1)S(1)}, u32[]{:S(2)}, u32[]{:S(2)}) collective-permute-start(bf16[64,1024]{1,0:T(8,128)(2,1)S(1)} %shard_map.34.refs_3_.refs_10_.refs_5_), channel_id=1, source_target_pairs={{0,8},{1,9},{2,10},{3,11},{4,12},{5,13},{6,14},{7,15},{8,0},{9,1},... | collective-permute-start | bytes 393224 | tf_op jit(solution)/shard_map/ppermute | solution.py:358
  48.8 2.4 %shard_map.32 = (f32[8,512]{1,0:T(8,128)S(1)}, f32[8,512]{1,0:T(8,128)S(1)}, f32[8,512]{1,0:T(8,128)S(1)}) custom-call(bf16[352,1024]{1,0:T(8,128)(2,1)S(1)} %shard_map.31.refs_0_.refs_3_.refs_6_.refs_1_, bf16[352,1024]{1,0:T(8,128)(2,1)S(1)} %collective-permute-done.10.refs_1_, bf16[352,1024]{1,0:T(8,128)(2,1)S(1)} %collective-permute-done.11.refs_2_, ...), custom_call_target="tpu_custom_call" | custom-call | flops 1522532352 | bytes 3604480 | tf_op jit(solution)/shard_map/pallas_call | solution.py:342
  51.3 2.4 %shard_map.35 = (f32[8,512]{1,0:T(8,128)S(1)}, f32[8,512]{1,0:T(8,128)S(1)}, f32[8,512]{1,0:T(8,128)S(1)}) custom-call(bf16[352,1024]{1,0:T(8,128)(2,1)S(1)} %shard_map.31.refs_0_.refs_3_.refs_6_.refs_1_, bf16[352,1024]{1,0:T(8,128)(2,1)S(1)} %collective-permute-done.10.refs_1_, bf16[352,1024]{1,0:T(8,128)(2,1)S(1)} %collective-permute-done.11.refs_2_, ...), custom_call_target="tpu_custom_call" | custom-call | flops 1522532352 | bytes 3604480 | tf_op jit(solution)/shard_map/pallas_call | solution.py:342
  53.7 0.0 collective-permute-done.20.refs_12_.refs_7_
  53.7 0.1 collective-permute-start.21
  53.8 1.8 %collective-permute-start.24 = (bf16[64,1024]{1,0:T(8,128)(2,1)S(1)}, bf16[64,1024]{1,0:T(8,128)(2,1)S(1)}, u32[]{:S(2)}, u32[]{:S(2)}) collective-permute-start(bf16[64,1024]{1,0:T(8,128)(2,1)S(1)} %shard_map.34.refs_3_.refs_10_.refs_5_), channel_id=1, source_target_pairs={{0,64},{1,65},{2,66},{3,67},{4,68},{5,69},{6,70},{7,71},{8,72},{9,... | collective-permute-start | bytes 393224 | tf_op jit(solution)/shard_map/ppermute | solution.py:358
  55.6 0.9 %collective-permute-done.18 = bf16[240,1024]{1,0:T(8,128)(2,1)S(1)} collective-permute-done((bf16[240,1024]{1,0:T(8,128)(2,1)S(1)}, bf16[240,1024]{1,0:T(8,128)(2,1)S(1)}, u32[]{:S(2)}, u32[]{:S(2)}) %collective-permute-start.18) | collective-permute-done | bytes 491552 | tf_op jit(solution)/shard_map/ppermute | solution.py:358
  56.5 0.0 collective-permute-done.19
  56.6 1.7 %shard_map.37 = f32[8,512]{1,0:T(8,128)S(1)} custom-call(bf16[176,1024]{1,0:T(8,128)(2,1)S(1)} %slice.51.upper_ref, bf16[176,1024]{1,0:T(8,128)(2,1)S(1)} %slice.52.lower_ref, bf16[352,1024]{1,0:T(8,128)(2,1)S(1)} %shard_map.31.refs_0_.refs_3_.refs_6_.refs_1_, bf16[352,1024]{1,0:T(8,128)(2,1)S(1)} %collective-permute-done.12.refs_4_.refs_7_.refs_1_.refs_2_, ...), custom_call_target="tpu_custom_call" | custom-call | flops 1015021568 | bytes 3604480 | tf_op jit(solution)/shard_map/pallas_call | solution.py:342
  58.3 2.0 %shard_map.36 = (f32[8,512]{1,0:T(8,128)S(1)}, f32[8,512]{1,0:T(8,128)S(1)}, f32[8,512]{1,0:T(8,128)S(1)}) custom-call(bf16[352,1024]{1,0:T(8,128)(2,1)S(1)} %shard_map.31.refs_0_.refs_3_.refs_6_.refs_1_, bf16[352,1024]{1,0:T(8,128)(2,1)S(1)} %collective-permute-done.10.refs_1_, bf16[352,1024]{1,0:T(8,128)(2,1)S(1)} %collective-permute-done.11.refs_2_, ...), custom_call_target="tpu_custom_call" | custom-call | flops 1268776960 | bytes 5963776 | tf_op jit(solution)/shard_map/pallas_call | solution.py:342
  60.3 1.6 %collective-permute-start.23 = (f32[8,512]{1,0:T(8,128)S(1)}, f32[8,512]{1,0:T(8,128)S(1)}, u32[]{:S(2)}, u32[]{:S(2)}) collective-permute-start(f32[8,512]{1,0:T(8,128)S(1)} %maximum_maximum_fusion.1), channel_id=1, source_target_pairs={{0,32},{1,33},{2,34},{3,35},{4,36},{5,37},{6,38},{7,39},{8,40},{9,... | collective-permute-start | bytes 49160 | tf_op jit(solution)/shard_map/ppermute | solution.py:358
  61.9 1.8 %collective-permute-start.22 = (f32[8,512]{1,0:T(8,128)S(1)}, f32[8,512]{1,0:T(8,128)S(1)}, u32[]{:S(2)}, u32[]{:S(2)}) collective-permute-start(f32[8,512]{1,0:T(8,128)S(1)} %maximum_maximum_fusion.2), channel_id=1, source_target_pairs={{0,96},{1,97},{2,98},{3,99},{4,100},{5,101},{6,102},{7,103},{8,104... | collective-permute-start | bytes 49160 | tf_op jit(solution)/shard_map/ppermute | solution.py:358
  63.6 0.0 collective-permute-done.24.refs_0_
  63.6 1.3 %shard_map.38 = f32[8,512]{1,0:T(8,128)S(1)} custom-call(bf16[176,1024]{1,0:T(8,128)(2,1)S(1)} %slice.51.upper_ref, bf16[176,1024]{1,0:T(8,128)(2,1)S(1)} %slice.52.lower_ref, bf16[64,1024]{1,0:T(8,128)(2,1)S(1)} %collective-permute-done.24.refs_0_, bf16[352,1024]{1,0:T(8,128)(2,1)S(1)} %shard_map.31.refs_0_.refs_3_.refs_6_.refs_1_, ...), custom_call_target="tpu_custom_call" | custom-call | flops 507510784 | bytes 4259840 | tf_op jit(solution)/shard_map/pallas_call | solution.py:342
  65.0 1.7 %collective-permute-start.25 = (f32[8,512]{1,0:T(8,128)S(1)}, f32[8,512]{1,0:T(8,128)S(1)}, u32[]{:S(2)}, u32[]{:S(2)}) collective-permute-start(f32[8,512]{1,0:T(8,128)S(1)} %max.48), channel_id=1, source_target_pairs={{0,64},{1,65},{2,66},{3,67},{4,68},{5,69},{6,70},{7,71},{8,72},{9,... | collective-permute-start | bytes 49160 | tf_op jit(solution)/shard_map/ppermute | solution.py:358
  66.7 3.6 %collective-permute-done.25 = f32[8,512]{1,0:T(8,128)S(1)} collective-permute-done((f32[8,512]{1,0:T(8,128)S(1)}, f32[8,512]{1,0:T(8,128)S(1)}, u32[]{:S(2)}, u32[]{:S(2)}) %collective-permute-start.25) | collective-permute-done | bytes 16416 | tf_op jit(solution)/shard_map/ppermute | solution.py:358
  70.3 2.2 %collective-permute-start.26 = (f32[8,512]{1,0:T(8,128)S(1)}, f32[8,512]{1,0:T(8,128)S(1)}, u32[]{:S(2)}, u32[]{:S(2)}) collective-permute-start(f32[8,512]{1,0:T(8,128)S(1)} %maximum_maximum_fusion.own_ref), channel_id=1, source_target_pairs={{0,4},{1,5},{2,6},{3,7},{4,0},{5,1},{6,2},{7,3},{8,12},{9,13},{10,... | collective-permute-start | bytes 49160 | tf_op jit(solution)/shard_map/ppermute | solution.py:358
  72.5 1.7 %collective-permute-done.26.side_ref = f32[8,512]{1,0:T(8,128)S(1)} collective-permute-done((f32[8,512]{1,0:T(8,128)S(1)}, f32[8,512]{1,0:T(8,128)S(1)}, u32[]{:S(2)}, u32[]{:S(2)}) %collective-permute-start.26) | collective-permute-done | bytes 16416 | tf_op jit(solution)/shard_map/ppermute | solution.py:358
  74.2 1.6 %collective-permute-start.27 = (f32[16,512]{1,0:T(8,128)S(1)}, f32[16,512]{1,0:T(8,128)S(1)}, u32[]{:S(2)}, u32[]{:S(2)}) collective-permute-start(f32[16,512]{1,0:T(8,128)S(1)} %pad_maximum_fusion.3), channel_id=1, source_target_pairs={{0,3},{1,0},{2,1},{3,2},{4,7},{5,4},{6,5},{7,6},{8,11},{9,8},{10,9... | collective-permute-start | bytes 98312 | tf_op jit(solution)/shard_map/ppermute | solution.py:358
  75.8 1.2 %collective-permute-start.28 = (f32[16,512]{1,0:T(8,128)S(1)}, f32[16,512]{1,0:T(8,128)S(1)}, u32[]{:S(2)}, u32[]{:S(2)}) collective-permute-start(f32[16,512]{1,0:T(8,128)S(1)} %pad_maximum_fusion.3), channel_id=1, source_target_pairs={{0,2},{1,3},{2,0},{3,1},{4,6},{5,7},{6,4},{7,5},{8,10},{9,11},{10,... | collective-permute-start | bytes 98312 | tf_op jit(solution)/shard_map/ppermute | solution.py:358
  77.0 0.6 collective-permute-start.29
  77.6 0.5 collective-permute-done.27.z1_ref
  78.1 3.1 %collective-permute-done.28.z2_ref = f32[16,512]{1,0:T(8,128)S(1)} collective-permute-done((f32[16,512]{1,0:T(8,128)S(1)}, f32[16,512]{1,0:T(8,128)S(1)}, u32[]{:S(2)}, u32[]{:S(2)}) %collective-permute-start.28) | collective-permute-done | bytes 32800 | tf_op jit(solution)/shard_map/ppermute | solution.py:358
  81.2 0.9 %collective-permute-done.29.z3_ref = f32[16,512]{1,0:T(8,128)S(1)} collective-permute-done((f32[16,512]{1,0:T(8,128)S(1)}, f32[16,512]{1,0:T(8,128)S(1)}, u32[]{:S(2)}, u32[]{:S(2)}) %collective-permute-start.29) | collective-permute-done | bytes 32800 | tf_op jit(solution)/shard_map/ppermute | solution.py:358
  82.1 0.7 shard_map.39
  82.9 0.0 copy-start.1
  82.9 0.6 copy-done.1
  (23 shorter events, 0.2 us)
Async XLA Ops:
  2.2 13.9 %collective-permute-start.2 = (bf16[64,1024]{1,0:T(8,128)(2,1)S(1)}, bf16[64,1024]{1,0:T(8,128)(2,1)S(1)}, u32[]{:S(2)}, u32[]{:S(2)}) collective-permute-start(bf16[64,1024]{1,0:T(8,128)(2,1)S(1)} %get-tuple-element.246.own_ref), channel_id=1, source_target_pairs={{0,4},{1,5},{2,6},{3,7},{4,0},{5,1},{6,2},{7,3},{8,12},{9,13},{10,... | collective-permute-start | bytes 393224 | tf_op jit(solution)/shard_map/ppermute | solution.py:358
  3.8 9.0 %collective-permute-start.3 = (bf16[48,1024]{1,0:T(8,128)(2,1)S(1)}, bf16[48,1024]{1,0:T(8,128)(2,1)S(1)}, u32[]{:S(2)}, u32[]{:S(2)}) collective-permute-start(bf16[48,1024]{1,0:T(8,128)(2,1)S(1)} %get-tuple-element.248), channel_id=1, source_target_pairs={{0,5},{1,6},{2,7},{3,4},{4,1},{5,2},{6,3},{7,0},{8,13},{9,14},{10,... | collective-permute-start | bytes 294920 | tf_op jit(solution)/shard_map/ppermute | solution.py:358
  5.7 7.1 %collective-permute-start.4 = (bf16[48,1024]{1,0:T(8,128)(2,1)S(1)}, bf16[48,1024]{1,0:T(8,128)(2,1)S(1)}, u32[]{:S(2)}, u32[]{:S(2)}) collective-permute-start(bf16[48,1024]{1,0:T(8,128)(2,1)S(1)} %get-tuple-element.249), channel_id=1, source_target_pairs={{0,7},{1,4},{2,5},{3,6},{4,3},{5,0},{6,1},{7,2},{8,15},{9,12},{10,... | collective-permute-start | bytes 294920 | tf_op jit(solution)/shard_map/ppermute | solution.py:358
  8.0 8.6 %collective-permute-start.5 = (bf16[48,1024]{1,0:T(8,128)(2,1)S(1)}, bf16[48,1024]{1,0:T(8,128)(2,1)S(1)}, u32[]{:S(2)}, u32[]{:S(2)}) collective-permute-start(bf16[48,1024]{1,0:T(8,128)(2,1)S(1)} %get-tuple-element.250), channel_id=1, source_target_pairs={{0,6},{1,7},{2,4},{3,5},{4,2},{5,3},{6,0},{7,1},{8,14},{9,15},{10,... | collective-permute-start | bytes 294920 | tf_op jit(solution)/shard_map/ppermute | solution.py:358
  10.6 8.3 %collective-permute-start.6 = (bf16[48,1024]{1,0:T(8,128)(2,1)S(1)}, bf16[48,1024]{1,0:T(8,128)(2,1)S(1)}, u32[]{:S(2)}, u32[]{:S(2)}) collective-permute-start(bf16[48,1024]{1,0:T(8,128)(2,1)S(1)} %get-tuple-element.251), channel_id=1, source_target_pairs={{0,2},{1,3},{2,0},{3,1},{4,6},{5,7},{6,4},{7,5},{8,10},{9,11},{10,... | collective-permute-start | bytes 294920 | tf_op jit(solution)/shard_map/ppermute | solution.py:358
  12.8 8.1 %collective-permute-start.7 = (bf16[48,1024]{1,0:T(8,128)(2,1)S(1)}, bf16[48,1024]{1,0:T(8,128)(2,1)S(1)}, u32[]{:S(2)}, u32[]{:S(2)}) collective-permute-start(bf16[48,1024]{1,0:T(8,128)(2,1)S(1)} %get-tuple-element.252), channel_id=1, source_target_pairs={{0,1},{1,2},{2,3},{3,0},{4,5},{5,6},{6,7},{7,4},{8,9},{9,10},{10,1... | collective-permute-start | bytes 294920 | tf_op jit(solution)/shard_map/ppermute | solution.py:358
  12.8 8.1 %collective-permute-start.8 = (bf16[48,1024]{1,0:T(8,128)(2,1)S(1)}, bf16[48,1024]{1,0:T(8,128)(2,1)S(1)}, u32[]{:S(2)}, u32[]{:S(2)}) collective-permute-start(bf16[48,1024]{1,0:T(8,128)(2,1)S(1)} %get-tuple-element.253), channel_id=1, source_target_pairs={{0,3},{1,0},{2,1},{3,2},{4,7},{5,4},{6,5},{7,6},{8,11},{9,8},{10,9... | collective-permute-start | bytes 294920 | tf_op jit(solution)/shard_map/ppermute | solution.py:358
  16.1 4.8 %collective-permute-start.9 = (bf16[48,1024]{1,0:T(8,128)(2,1)S(1)}, bf16[48,1024]{1,0:T(8,128)(2,1)S(1)}, u32[]{:S(2)}, u32[]{:S(2)}) collective-permute-start(bf16[48,1024]{1,0:T(8,128)(2,1)S(1)} %get-tuple-element.254), channel_id=1, source_target_pairs={{0,4},{1,5},{2,6},{3,7},{4,0},{5,1},{6,2},{7,3},{8,12},{9,13},{10,... | collective-permute-start | bytes 294920 | tf_op jit(solution)/shard_map/ppermute | solution.py:358
  21.5 19.7 %collective-permute-start.13 = (bf16[352,1024]{1,0:T(8,128)(2,1)S(1)}, bf16[352,1024]{1,0:T(8,128)(2,1)S(1)}, u32[]{:S(2)}, u32[]{:S(2)}) collective-permute-start(bf16[352,1024]{1,0:T(8,128)(2,1)S(1)} %shard_map.31.refs_0_.refs_3_.refs_6_.refs_1_), channel_id=1, source_target_pairs={{0,8},{1,9},{2,10},{3,11},{4,12},{5,13},{6,14},{7,15},{8,0},{9,1},... | collective-permute-start | bytes 2162696 | tf_op jit(solution)/shard_map/ppermute | solution.py:358
  24.1 6.5 %collective-permute-start.14 = (bf16[64,1024]{1,0:T(8,128)(2,1)S(1)}, bf16[64,1024]{1,0:T(8,128)(2,1)S(1)}, u32[]{:S(2)}, u32[]{:S(2)}) collective-permute-start(bf16[64,1024]{1,0:T(8,128)(2,1)S(1)} %shard_map.33.refs_0_), channel_id=1, source_target_pairs={{0,1},{1,2},{2,3},{3,0},{4,5},{5,6},{6,7},{7,4},{8,9},{9,10},{10,1... | collective-permute-start | bytes 393224 | tf_op jit(solution)/shard_map/ppermute | solution.py:358
  24.3 18.3 %collective-permute-start.10 = (bf16[352,1024]{1,0:T(8,128)(2,1)S(1)}, bf16[352,1024]{1,0:T(8,128)(2,1)S(1)}, u32[]{:S(2)}, u32[]{:S(2)}) collective-permute-start(bf16[352,1024]{1,0:T(8,128)(2,1)S(1)} %shard_map.31.refs_0_.refs_3_.refs_6_.refs_1_), channel_id=1, source_target_pairs={{0,32},{1,33},{2,34},{3,35},{4,36},{5,37},{6,38},{7,39},{8,40},{9,... | collective-permute-start | bytes 2162696 | tf_op jit(solution)/shard_map/ppermute | solution.py:358
  25.9 16.8 %collective-permute-start.11 = (bf16[352,1024]{1,0:T(8,128)(2,1)S(1)}, bf16[352,1024]{1,0:T(8,128)(2,1)S(1)}, u32[]{:S(2)}, u32[]{:S(2)}) collective-permute-start(bf16[352,1024]{1,0:T(8,128)(2,1)S(1)} %shard_map.31.refs_0_.refs_3_.refs_6_.refs_1_), channel_id=1, source_target_pairs={{0,96},{1,97},{2,98},{3,99},{4,100},{5,101},{6,102},{7,103},{8,104... | collective-permute-start | bytes 2162696 | tf_op jit(solution)/shard_map/ppermute | solution.py:358
  27.6 7.0 %collective-permute-start.15 = (bf16[64,1024]{1,0:T(8,128)(2,1)S(1)}, bf16[64,1024]{1,0:T(8,128)(2,1)S(1)}, u32[]{:S(2)}, u32[]{:S(2)}) collective-permute-start(bf16[64,1024]{1,0:T(8,128)(2,1)S(1)} %shard_map.33.refs_0_), channel_id=1, source_target_pairs={{0,3},{1,0},{2,1},{3,2},{4,7},{5,4},{6,5},{7,6},{8,11},{9,8},{10,9... | collective-permute-start | bytes 393224 | tf_op jit(solution)/shard_map/ppermute | solution.py:358
  30.7 6.5 %collective-permute-start.16 = (bf16[64,1024]{1,0:T(8,128)(2,1)S(1)}, bf16[64,1024]{1,0:T(8,128)(2,1)S(1)}, u32[]{:S(2)}, u32[]{:S(2)}) collective-permute-start(bf16[64,1024]{1,0:T(8,128)(2,1)S(1)} %shard_map.33.refs_0_), channel_id=1, source_target_pairs={{0,2},{1,3},{2,0},{3,1},{4,6},{5,7},{6,4},{7,5},{8,10},{9,11},{10,... | collective-permute-start | bytes 393224 | tf_op jit(solution)/shard_map/ppermute | solution.py:358
  34.6 14.2 %collective-permute-start.12 = (bf16[352,1024]{1,0:T(8,128)(2,1)S(1)}, bf16[352,1024]{1,0:T(8,128)(2,1)S(1)}, u32[]{:S(2)}, u32[]{:S(2)}) collective-permute-start(bf16[352,1024]{1,0:T(8,128)(2,1)S(1)} %shard_map.31.refs_0_.refs_3_.refs_6_.refs_1_), channel_id=1, source_target_pairs={{0,16},{1,17},{2,18},{3,19},{4,20},{5,21},{6,22},{7,23},{8,24},{9,... | collective-permute-start | bytes 2162696 | tf_op jit(solution)/shard_map/ppermute | solution.py:358
  41.3 9.9 %collective-permute-start.17 = (bf16[416,1024]{1,0:T(8,128)(2,1)S(1)}, bf16[416,1024]{1,0:T(8,128)(2,1)S(1)}, u32[]{:S(2)}, u32[]{:S(2)}) collective-permute-start(bf16[416,1024]{1,0:T(8,128)(2,1)S(1)} %pad_maximum_fusion), channel_id=1, source_target_pairs={{0,16},{1,17},{2,18},{3,19},{4,20},{5,21},{6,22},{7,23},{8,24},{9,... | collective-permute-start | bytes 2555912 | tf_op jit(solution)/shard_map/ppermute | solution.py:358
  42.8 13.7 %collective-permute-start.18 = (bf16[240,1024]{1,0:T(8,128)(2,1)S(1)}, bf16[240,1024]{1,0:T(8,128)(2,1)S(1)}, u32[]{:S(2)}, u32[]{:S(2)}) collective-permute-start(bf16[240,1024]{1,0:T(8,128)(2,1)S(1)} %get-tuple-element.322), channel_id=1, source_target_pairs={{0,32},{1,33},{2,34},{3,35},{4,36},{5,37},{6,38},{7,39},{8,40},{9,... | collective-permute-start | bytes 1474568 | tf_op jit(solution)/shard_map/ppermute | solution.py:358
  44.4 12.1 %collective-permute-start.19 = (bf16[240,1024]{1,0:T(8,128)(2,1)S(1)}, bf16[240,1024]{1,0:T(8,128)(2,1)S(1)}, u32[]{:S(2)}, u32[]{:S(2)}) collective-permute-start(bf16[240,1024]{1,0:T(8,128)(2,1)S(1)} %get-tuple-element.321), channel_id=1, source_target_pairs={{0,96},{1,97},{2,98},{3,99},{4,100},{5,101},{6,102},{7,103},{8,104... | collective-permute-start | bytes 1474568 | tf_op jit(solution)/shard_map/ppermute | solution.py:358
  46.1 7.6 %collective-permute-start.20 = (bf16[64,1024]{1,0:T(8,128)(2,1)S(1)}, bf16[64,1024]{1,0:T(8,128)(2,1)S(1)}, u32[]{:S(2)}, u32[]{:S(2)}) collective-permute-start(bf16[64,1024]{1,0:T(8,128)(2,1)S(1)} %shard_map.34.refs_3_.refs_10_.refs_5_), channel_id=1, source_target_pairs={{0,8},{1,9},{2,10},{3,11},{4,12},{5,13},{6,14},{7,15},{8,0},{9,1},... | collective-permute-start | bytes 393224 | tf_op jit(solution)/shard_map/ppermute | solution.py:358
  53.7 4.6 %collective-permute-start.21 = (bf16[64,1024]{1,0:T(8,128)(2,1)S(1)}, bf16[64,1024]{1,0:T(8,128)(2,1)S(1)}, u32[]{:S(2)}, u32[]{:S(2)}) collective-permute-start(bf16[64,1024]{1,0:T(8,128)(2,1)S(1)} %collective-permute-done.20.refs_12_.refs_7_), channel_id=1, source_target_pairs={{0,16},{1,17},{2,18},{3,19},{4,20},{5,21},{6,22},{7,23},{8,24},{9,... | collective-permute-start | bytes 393224 | tf_op jit(solution)/shard_map/ppermute | solution.py:358
  53.8 9.8 %collective-permute-start.24 = (bf16[64,1024]{1,0:T(8,128)(2,1)S(1)}, bf16[64,1024]{1,0:T(8,128)(2,1)S(1)}, u32[]{:S(2)}, u32[]{:S(2)}) collective-permute-start(bf16[64,1024]{1,0:T(8,128)(2,1)S(1)} %shard_map.34.refs_3_.refs_10_.refs_5_), channel_id=1, source_target_pairs={{0,64},{1,65},{2,66},{3,67},{4,68},{5,69},{6,70},{7,71},{8,72},{9,... | collective-permute-start | bytes 393224 | tf_op jit(solution)/shard_map/ppermute | solution.py:358
  60.3 6.4 %collective-permute-start.23 = (f32[8,512]{1,0:T(8,128)S(1)}, f32[8,512]{1,0:T(8,128)S(1)}, u32[]{:S(2)}, u32[]{:S(2)}) collective-permute-start(f32[8,512]{1,0:T(8,128)S(1)} %maximum_maximum_fusion.1), channel_id=1, source_target_pairs={{0,32},{1,33},{2,34},{3,35},{4,36},{5,37},{6,38},{7,39},{8,40},{9,... | collective-permute-start | bytes 49160 | tf_op jit(solution)/shard_map/ppermute | solution.py:358
  61.9 21.0 %copy-start = (s32[384]{0:T(512)S(1)}, s32[384]{0:T(512)}, u32[]{:S(2)}) copy-start(s32[384]{0:T(512)} %ids_ref.1) | copy-start | bytes 4612
  61.9 4.9 %collective-permute-start.22 = (f32[8,512]{1,0:T(8,128)S(1)}, f32[8,512]{1,0:T(8,128)S(1)}, u32[]{:S(2)}, u32[]{:S(2)}) collective-permute-start(f32[8,512]{1,0:T(8,128)S(1)} %maximum_maximum_fusion.2), channel_id=1, source_target_pairs={{0,96},{1,97},{2,98},{3,99},{4,100},{5,101},{6,102},{7,103},{8,104... | collective-permute-start | bytes 49160 | tf_op jit(solution)/shard_map/ppermute | solution.py:358
  65.0 5.3 %collective-permute-start.25 = (f32[8,512]{1,0:T(8,128)S(1)}, f32[8,512]{1,0:T(8,128)S(1)}, u32[]{:S(2)}, u32[]{:S(2)}) collective-permute-start(f32[8,512]{1,0:T(8,128)S(1)} %max.48), channel_id=1, source_target_pairs={{0,64},{1,65},{2,66},{3,67},{4,68},{5,69},{6,70},{7,71},{8,72},{9,... | collective-permute-start | bytes 49160 | tf_op jit(solution)/shard_map/ppermute | solution.py:358
  70.3 3.9 %collective-permute-start.26 = (f32[8,512]{1,0:T(8,128)S(1)}, f32[8,512]{1,0:T(8,128)S(1)}, u32[]{:S(2)}, u32[]{:S(2)}) collective-permute-start(f32[8,512]{1,0:T(8,128)S(1)} %maximum_maximum_fusion.own_ref), channel_id=1, source_target_pairs={{0,4},{1,5},{2,6},{3,7},{4,0},{5,1},{6,2},{7,3},{8,12},{9,13},{10,... | collective-permute-start | bytes 49160 | tf_op jit(solution)/shard_map/ppermute | solution.py:358
  74.2 3.9 %collective-permute-start.27 = (f32[16,512]{1,0:T(8,128)S(1)}, f32[16,512]{1,0:T(8,128)S(1)}, u32[]{:S(2)}, u32[]{:S(2)}) collective-permute-start(f32[16,512]{1,0:T(8,128)S(1)} %pad_maximum_fusion.3), channel_id=1, source_target_pairs={{0,3},{1,0},{2,1},{3,2},{4,7},{5,4},{6,5},{7,6},{8,11},{9,8},{10,9... | collective-permute-start | bytes 98312 | tf_op jit(solution)/shard_map/ppermute | solution.py:358
  75.8 5.4 %collective-permute-start.28 = (f32[16,512]{1,0:T(8,128)S(1)}, f32[16,512]{1,0:T(8,128)S(1)}, u32[]{:S(2)}, u32[]{:S(2)}) collective-permute-start(f32[16,512]{1,0:T(8,128)S(1)} %pad_maximum_fusion.3), channel_id=1, source_target_pairs={{0,2},{1,3},{2,0},{3,1},{4,6},{5,7},{6,4},{7,5},{8,10},{9,11},{10,... | collective-permute-start | bytes 98312 | tf_op jit(solution)/shard_map/ppermute | solution.py:358
  77.0 5.1 %collective-permute-start.29 = (f32[16,512]{1,0:T(8,128)S(1)}, f32[16,512]{1,0:T(8,128)S(1)}, u32[]{:S(2)}, u32[]{:S(2)}) collective-permute-start(f32[16,512]{1,0:T(8,128)S(1)} %pad_maximum_fusion.3), channel_id=1, source_target_pairs={{0,1},{1,2},{2,3},{3,0},{4,5},{5,6},{6,7},{7,4},{8,9},{9,10},{10,1... | collective-permute-start | bytes 98312 | tf_op jit(solution)/shard_map/ppermute | solution.py:358
  82.9 0.6 copy-start.1
